TPU v7x, 32 devices: a whole 2x2x4 slice. The times are simulated.
32 devices in a mesh: seq: 16 (over z, y, core), head: 2 (over x).
Axes of the slice: x: 2, y: 2, z: 4, core: 2. Of those that a mesh axis runs over, the one named last changes fastest.
Arguments:
- queries: bfloat16 [6144, 3072], P('seq', 'head')
- keys: bfloat16 [6144, 3072], P('seq', 'head')
- values: bfloat16 [6144, 3072], P('seq', 'head'), may hold values from -6 to 6
- kv_tiles: int32 [16, 13], replicated, may hold values from -1 to 15, as said below
- tile_order: int32 [16], replicated, may hold values from 0 to 15, as said below
- out_weight: bfloat16 [3072, 3072], P('head'), may hold values from -0.109375 to 0.109375
Outputs:
- projected: bfloat16 [6144, 3072], P('seq', 'head')
Inputs may be any that keep to these rules, and one draw needn't show every extreme that they name: tile_order is a rotation: slot p holds tile (p + c) mod 16 for one c. `kv_tiles`: row t lists distinct tiles in increasing order, then -1 entries; it always holds t; every listed u has |u - t| <= 6; t - 6 and t + 6 are listed wherever they are tiles.
All inputs are finite; a program needn't handle non-finite values.
Results may differ from a plain program's by a relative error of at most 0.014.
Values may be sent and summed in bfloat16 or wider, within the bound.
A program may use at most 256 MiB of HBM per device.

v0:
```python
import math

import jax
import jax.numpy as jnp
from jax import lax
from jax.sharding import PartitionSpec as P

HEAD_DIM = 128
REACH = 6


def from_behind(value, axis, by):
    length = lax.axis_size(axis)
    return lax.ppermute(value, axis, [(i, (i + by) % length) for i in range(length)])


def per_device(queries, keys, values, kv_tiles, tile_order, out_weight):
    tile_rows, local_width = queries.shape
    heads_here = local_width // HEAD_DIM
    score_scale = 1.0 / math.sqrt(HEAD_DIM)
    loop_size = lax.axis_size("seq")
    my_slot = lax.axis_index("seq")
    window = 2 * REACH + 1
    own_tile = lax.dynamic_index_in_dim(tile_order, my_slot, 0, keepdims=False)
    listed = lax.dynamic_index_in_dim(kv_tiles, own_tile, 0, keepdims=False)
    present = listed >= 0
    clipped = jnp.maximum(listed, 0)
    slot_ids = jnp.arange(loop_size, dtype=jnp.int32)
    key_slot = jnp.sum(
        jnp.where(tile_order[None, :] == clipped[:, None], slot_ids[None, :], 0), axis=1
    )
    position = (key_slot - my_slot + REACH) % loop_size
    received = {0: (keys, values)}
    moving = {1: (keys, values), -1: (keys, values)}
    for stride in range(1, REACH + 1):
        for heading in (1, -1):
            moved_keys, moved_values = from_behind(
                (moving[heading][0], moving[heading][1]), "seq", heading
            )
            moving[heading] = (moved_keys, moved_values)
            received[-heading * stride] = (moved_keys, moved_values)
    key_heads = jnp.stack([received[offset_value][0] for offset_value in range(-REACH, REACH + 1)])
    value_heads = jnp.stack(
        [received[offset_value][1] for offset_value in range(-REACH, REACH + 1)]
    )
    key_heads = key_heads.reshape(window, tile_rows, heads_here, HEAD_DIM)
    value_heads = value_heads.reshape(window, tile_rows, heads_here, HEAD_DIM)
    query_heads = queries.reshape(tile_rows, heads_here, HEAD_DIM)

    def block_scores(block_index):
        key_block = lax.dynamic_index_in_dim(key_heads, block_index, 0, keepdims=False)
        return (
            jnp.einsum("qhd,khd->hqk", query_heads, key_block, preferred_element_type=jnp.float32)
            * score_scale
        )

    def add_block(block_index, stored_scores, top_score, running_state):
        denominator, summed = running_state
        exponent = jnp.exp(stored_scores - top_score[:, :, None])
        value_block = lax.dynamic_index_in_dim(value_heads, block_index, 0, keepdims=False)
        summed = summed + jnp.einsum(
            "hqk,khd->qhd",
            exponent.astype(jnp.bfloat16),
            value_block,
            preferred_element_type=jnp.float32,
        )
        return (denominator + jnp.sum(exponent, axis=2), summed)

    lowest = jnp.full((heads_here, tile_rows), -jnp.inf, jnp.float32)
    score_store = jnp.zeros((window, heads_here, tile_rows, tile_rows), jnp.float32)
    starting = (
        jnp.zeros((heads_here, tile_rows), jnp.float32),
        jnp.zeros((tile_rows, heads_here, HEAD_DIM), jnp.float32),
    )
    block_used = jnp.any(
        (position[:, None] == jnp.arange(window, dtype=jnp.int32)[None, :]) & present[:, None],
        axis=0,
    )

    def find_top(block_index, carried):
        running_top, stored = carried
        fresh_scores = block_scores(block_index)
        block_max = jnp.max(fresh_scores, axis=2)
        stored = lax.dynamic_update_index_in_dim(stored, fresh_scores, block_index, 0)
        running_top = jnp.where(
            block_used[block_index], jnp.maximum(running_top, block_max), running_top
        )
        return (running_top, stored)

    top_score, score_store = lax.fori_loop(0, window, find_top, (lowest, score_store))

    def accumulate(block_index, running_state):
        stored_scores = lax.dynamic_index_in_dim(score_store, block_index, 0, keepdims=False)
        updated = add_block(block_index, stored_scores, top_score, running_state)
        return jax.tree.map(
            lambda fresh, stale: jnp.where(block_used[block_index], fresh, stale),
            updated,
            running_state,
        )

    denominator, summed = lax.fori_loop(0, window, accumulate, starting)
    attended = (
        (summed / jnp.transpose(denominator)[:, :, None])
        .reshape(tile_rows, local_width)
        .astype(jnp.bfloat16)
    )
    partial_terms = jnp.dot(attended, out_weight, preferred_element_type=jnp.float32)
    projected = lax.psum_scatter(
        partial_terms.astype(jnp.bfloat16), "head", scatter_dimension=1, tiled=True
    )
    return projected


def solution(mesh):
    return jax.shard_map(
        per_device,
        mesh=mesh,
        in_specs=(P("seq", "head"), P("seq", "head"), P("seq", "head"), P(), P(), P("head", None)),
        out_specs=P("seq", "head"),
        check_vma=False,
    )
```

profile of v0, /device:TPU:0, one launch (start us, length us, event | category | flops | bytes accessed | tf_op | source)
XLA Modules:
  0.0 903.4 jit_solution(3525479056401588545)
XLA Ops:
  14.6 13.2 %collective-permute-done = bf16[384,1536]{0,1:T(8,128)(2,1)S(1)} collective-permute-done((bf16[384,1536]{0,1:T(8,128)(2,1)S(1)}, bf16[384,1536]{0,1:T(8,128)(2,1)S(1)}, u32[]{:S(2)}, u32[]{:S(2)}) %collective-permute-start) | collective-permute-done | bytes 1179680 | tf_op jit(solution)/shard_map/ppermute | solution.py:14
  27.7 22.1 %collective-permute-start.1 = (bf16[384,1536]{0,1:T(8,128)(2,1)S(1)}, bf16[384,1536]{0,1:T(8,128)(2,1)S(1)}, u32[]{:S(2)}, u32[]{:S(2)}) collective-permute-start(bf16[384,1536]{0,1:T(8,128)(2,1)S(1)} %collective-permute-done), channel_id=1, source_target_pairs={{0,2},{2,4},{4,6},{6,8},{8,10},{10,12},{12,14},{14,16},{16,18},{18... | collective-permute-start | bytes 3538952 | tf_op jit(solution)/shard_map/ppermute | solution.py:14
  49.8 12.7 %collective-permute-start.13 = (bf16[384,1536]{1,0:T(8,128)(2,1)S(1)}, bf16[384,1536]{1,0:T(8,128)(2,1)S(1)}, u32[]{:S(2)}, u32[]{:S(2)}) collective-permute-start(bf16[384,1536]{1,0:T(8,128)(2,1)S(1)} %collective-permute-done.12), channel_id=1, source_target_pairs={{0,2},{2,4},{4,6},{6,8},{8,10},{10,12},{12,14},{14,16},{16,18},{18... | collective-permute-start | bytes 3538952 | tf_op jit(solution)/shard_map/ppermute | solution.py:14
  62.6 17.1 %collective-permute-start.7 = (bf16[384,1536]{0,1:T(8,128)(2,1)S(1)}, bf16[384,1536]{0,1:T(8,128)(2,1)S(1)}, u32[]{:S(2)}, u32[]{:S(2)}) collective-permute-start(bf16[384,1536]{0,1:T(8,128)(2,1)S(1)} %collective-permute-done.6), channel_id=1, source_target_pairs={{0,30},{2,0},{4,2},{6,4},{8,6},{10,8},{12,10},{14,12},{16,14},{18,... | collective-permute-start | bytes 3538952 | tf_op jit(solution)/shard_map/ppermute | solution.py:14
  79.7 20.7 %collective-permute-start.2 = (bf16[384,1536]{0,1:T(8,128)(2,1)S(1)}, bf16[384,1536]{0,1:T(8,128)(2,1)S(1)}, u32[]{:S(2)}, u32[]{:S(2)}) collective-permute-start(bf16[384,1536]{0,1:T(8,128)(2,1)S(1)} %collective-permute-done.1), channel_id=1, source_target_pairs={{0,2},{2,4},{4,6},{6,8},{8,10},{10,12},{12,14},{14,16},{16,18},{18... | collective-permute-start | bytes 3538952 | tf_op jit(solution)/shard_map/ppermute | solution.py:14
  100.4 12.6 %collective-permute-start.14 = (bf16[384,1536]{1,0:T(8,128)(2,1)S(1)}, bf16[384,1536]{1,0:T(8,128)(2,1)S(1)}, u32[]{:S(2)}, u32[]{:S(2)}) collective-permute-start(bf16[384,1536]{1,0:T(8,128)(2,1)S(1)} %collective-permute-done.13), channel_id=1, source_target_pairs={{0,2},{2,4},{4,6},{6,8},{8,10},{10,12},{12,14},{14,16},{16,18},{18... | collective-permute-start | bytes 3538952 | tf_op jit(solution)/shard_map/ppermute | solution.py:14
  113.1 17.1 %collective-permute-start.8 = (bf16[384,1536]{0,1:T(8,128)(2,1)S(1)}, bf16[384,1536]{0,1:T(8,128)(2,1)S(1)}, u32[]{:S(2)}, u32[]{:S(2)}) collective-permute-start(bf16[384,1536]{0,1:T(8,128)(2,1)S(1)} %collective-permute-done.7), channel_id=1, source_target_pairs={{0,30},{2,0},{4,2},{6,4},{8,6},{10,8},{12,10},{14,12},{16,14},{18,... | collective-permute-start | bytes 3538952 | tf_op jit(solution)/shard_map/ppermute | solution.py:14
  130.2 20.8 %collective-permute-start.3 = (bf16[384,1536]{0,1:T(8,128)(2,1)S(1)}, bf16[384,1536]{0,1:T(8,128)(2,1)S(1)}, u32[]{:S(2)}, u32[]{:S(2)}) collective-permute-start(bf16[384,1536]{0,1:T(8,128)(2,1)S(1)} %collective-permute-done.2), channel_id=1, source_target_pairs={{0,2},{2,4},{4,6},{6,8},{8,10},{10,12},{12,14},{14,16},{16,18},{18... | collective-permute-start | bytes 3538952 | tf_op jit(solution)/shard_map/ppermute | solution.py:14
  150.9 12.6 %collective-permute-start.15 = (bf16[384,1536]{1,0:T(8,128)(2,1)S(1)}, bf16[384,1536]{1,0:T(8,128)(2,1)}, u32[]{:S(2)}, u32[]{:S(2)}) collective-permute-start(bf16[384,1536]{1,0:T(8,128)(2,1)S(1)} %collective-permute-done.14), channel_id=1, source_target_pairs={{0,2},{2,4},{4,6},{6,8},{8,10},{10,12},{12,14},{14,16},{16,18},{18... | collective-permute-start | bytes 3538952 | tf_op jit(solution)/shard_map/ppermute | solution.py:14
  163.6 17.1 %collective-permute-start.9 = (bf16[384,1536]{0,1:T(8,128)(2,1)S(1)}, bf16[384,1536]{0,1:T(8,128)(2,1)}, u32[]{:S(2)}, u32[]{:S(2)}) collective-permute-start(bf16[384,1536]{0,1:T(8,128)(2,1)S(1)} %collective-permute-done.8), channel_id=1, source_target_pairs={{0,30},{2,0},{4,2},{6,4},{8,6},{10,8},{12,10},{14,12},{16,14},{18,... | collective-permute-start | bytes 3538952 | tf_op jit(solution)/shard_map/ppermute | solution.py:14
  180.7 20.8 %collective-permute-start.4 = (bf16[384,1536]{0,1:T(8,128)(2,1)S(1)}, bf16[384,1536]{0,1:T(8,128)(2,1)}, u32[]{:S(2)}, u32[]{:S(2)}) collective-permute-start(bf16[384,1536]{0,1:T(8,128)(2,1)S(1)} %collective-permute-done.3), channel_id=1, source_target_pairs={{0,2},{2,4},{4,6},{6,8},{8,10},{10,12},{12,14},{14,16},{16,18},{18... | collective-permute-start | bytes 3538952 | tf_op jit(solution)/shard_map/ppermute | solution.py:14
  201.5 12.6 %collective-permute-start.16 = (bf16[384,1536]{1,0:T(8,128)(2,1)}, bf16[384,1536]{1,0:T(8,128)(2,1)}, u32[]{:S(2)}, u32[]{:S(2)}) collective-permute-start(bf16[384,1536]{1,0:T(8,128)(2,1)} %collective-permute-done.15), channel_id=1, source_target_pairs={{0,2},{2,4},{4,6},{6,8},{8,10},{10,12},{12,14},{14,16},{16,18},{18... | collective-permute-start | bytes 3538952 | tf_op jit(solution)/shard_map/ppermute | solution.py:14
  214.2 17.1 %collective-permute-start.10 = (bf16[384,1536]{0,1:T(8,128)(2,1)}, bf16[384,1536]{0,1:T(8,128)(2,1)}, u32[]{:S(2)}, u32[]{:S(2)}) collective-permute-start(bf16[384,1536]{0,1:T(8,128)(2,1)} %collective-permute-done.9), channel_id=1, source_target_pairs={{0,30},{2,0},{4,2},{6,4},{8,6},{10,8},{12,10},{14,12},{16,14},{18,... | collective-permute-start | bytes 3538952 | tf_op jit(solution)/shard_map/ppermute | solution.py:14
  231.2 20.8 %collective-permute-start.5 = (bf16[384,1536]{0,1:T(8,128)(2,1)}, bf16[384,1536]{0,1:T(8,128)(2,1)}, u32[]{:S(2)}, u32[]{:S(2)}) collective-permute-start(bf16[384,1536]{0,1:T(8,128)(2,1)} %collective-permute-done.4), channel_id=1, source_target_pairs={{0,2},{2,4},{4,6},{6,8},{8,10},{10,12},{12,14},{14,16},{16,18},{18... | collective-permute-start | bytes 3538952 | tf_op jit(solution)/shard_map/ppermute | solution.py:14
  302.3 16.0 %collective-permute-done.11 = bf16[384,1536]{0,1:T(8,128)(2,1)S(1)} collective-permute-done((bf16[384,1536]{0,1:T(8,128)(2,1)}, bf16[384,1536]{0,1:T(8,128)(2,1)S(1)}, u32[]{:S(2)}, u32[]{:S(2)}) %collective-permute-start.11) | collective-permute-done | bytes 1179680 | tf_op jit(solution)/shard_map/ppermute | solution.py:14
  323.8 170.6 %while.32 = (s32[]{:T(128)}, f32[12,384]{1,0:T(8,128)S(1)}, f32[13,12,384,384]{2,3,1,0:T(8,128)}, pred[13]{0:T(512)(128)(4,1)S(1)}, bf16[13,384,12,128]{1,3,2,0:...) while((s32[]{:T(128)}, f32[12,384]{1,0:T(8,128)S(1)}, ...), condition=%wide.region_4.5_spmd.clone, body=%wide.region_2.4_spmd.clone.sunk | while | flops 458302464 | bytes 23667812 | solution.py:90
  330.4 6.5 bitcast_dynamic-update-slice_fusion.2
  343.5 6.6 bitcast_dynamic-update-slice_fusion.2
  356.7 6.5 bitcast_dynamic-update-slice_fusion.2
  369.7 6.5 bitcast_dynamic-update-slice_fusion.2
  382.8 6.5 bitcast_dynamic-update-slice_fusion.2
  396.0 6.6 bitcast_dynamic-update-slice_fusion.2
  409.1 6.5 bitcast_dynamic-update-slice_fusion.2
  422.1 6.5 bitcast_dynamic-update-slice_fusion.2
  435.2 6.6 bitcast_dynamic-update-slice_fusion.2
  448.4 6.5 bitcast_dynamic-update-slice_fusion.2
  461.5 6.5 bitcast_dynamic-update-slice_fusion.2
  474.6 6.6 bitcast_dynamic-update-slice_fusion.2
  487.9 6.5 bitcast_dynamic-update-slice_fusion.2
  512.3 332.8 %while.33 = (s32[]{:T(128)}, f32[12,384]{1,0:T(8,128)S(1)}, f32[384,12,128]{0,2,1:T(8,128)}, pred[13]{0:T(512)(128)(4,1)S(1)}, f32[13,12,384,384]{2,3,1,0:T(8,12...) while((s32[]{:T(128)}, f32[12,384]{1,0:T(8,128)S(1)}, ...), condition=%wide.region_7.8_spmd.clone, body=%wide.region_5.7_spmd.clone.sunk | while | flops 461841408 | bytes 69711008 | solution.py:101
  518.5 8.1 copy.64
  527.2 7.6 add_select_fusion.5
  537.2 6.3 constant_dynamic-slice_fusion.3
  543.5 8.1 copy.64
  552.2 8.3 add_select_fusion.5
  562.9 6.3 constant_dynamic-slice_fusion.3
  569.2 8.1 copy.64
  577.9 8.3 add_select_fusion.5
  588.5 6.3 constant_dynamic-slice_fusion.3
  594.8 8.1 copy.64
  603.5 8.3 add_select_fusion.5
  614.2 6.3 constant_dynamic-slice_fusion.3
  620.5 8.1 copy.64
  629.2 8.3 add_select_fusion.5
  646.1 8.1 copy.64
  654.8 8.3 add_select_fusion.5
  671.8 8.1 copy.64
  680.5 8.3 add_select_fusion.5
  697.4 8.1 copy.64
  706.1 8.3 add_select_fusion.5
  723.1 8.1 copy.64
  731.8 8.3 add_select_fusion.5
  748.7 8.1 copy.64
  757.4 8.3 add_select_fusion.5
  768.1 6.3 constant_dynamic-slice_fusion.3
  774.4 8.1 copy.64
  783.1 8.3 add_select_fusion.5
  793.7 6.3 constant_dynamic-slice_fusion.3
  800.1 8.1 copy.64
  808.7 8.3 add_select_fusion.5
  825.7 8.1 copy.64
  834.4 8.3 add_select_fusion.5
  847.0 8.9 convolution_convert_fusion
  855.9 40.7 %reduce-scatter.2.cloned.1.call-done = bf16[384,1536]{1,0:T(8,128)(2,1)} async-done(((bf16[384,3072]{1,0:T(8,128)(2,1)}), bf16[384,1536]{1,0:T(8,128)(2,1)}) %reduce-scatter.2.cloned.1.call-update) | async-done | bytes 1179664 | tf_op jit(solution)/shard_map/reduce_scatter | solution.py:108
  (300 shorter events, 249.3 us)
Async XLA Ops:
  6.5 256.4 %copy-start.30 = (s32[16]{0:T(128)S(1)}, s32[16]{0:T(128)}, u32[]{:S(2)}) copy-start(s32[16]{0:T(128)} %param.14) | copy-start | bytes 196
  6.5 890.0 %reduce-scatter.2.cloned.1.call-start = ((), (), s32[]{:S(2)}) async-start(), calls=%async_computation.1 | async-start | bytes 3538944 | tf_op jit(solution)/shard_map/reduce_scatter | solution.py:108
  8.3 19.5 %collective-permute-start = (bf16[384,1536]{0,1:T(8,128)(2,1)S(1)}, bf16[384,1536]{0,1:T(8,128)(2,1)S(1)}, u32[]{:S(2)}, u32[]{:S(2)}) collective-permute-start(bf16[384,1536]{0,1:T(8,128)(2,1)S(1)} %copy.41), channel_id=1, source_target_pairs={{0,2},{2,4},{4,6},{6,8},{8,10},{10,12},{12,14},{14,16},{16,18},{18... | collective-permute-start | bytes 3538952 | tf_op jit(solution)/shard_map/ppermute | solution.py:14
  8.8 41.1 %collective-permute-start.12 = (bf16[384,1536]{1,0:T(8,128)(2,1)}, bf16[384,1536]{1,0:T(8,128)(2,1)S(1)}, u32[]{:S(2)}, u32[]{:S(2)}) collective-permute-start(bf16[384,1536]{1,0:T(8,128)(2,1)} %param.12), channel_id=1, source_target_pairs={{0,2},{2,4},{4,6},{6,8},{8,10},{10,12},{12,14},{14,16},{16,18},{18... | collective-permute-start | bytes 3538952 | tf_op jit(solution)/shard_map/ppermute | solution.py:14
  11.4 51.2 %collective-permute-start.18 = (bf16[384,1536]{1,0:T(8,128)(2,1)}, bf16[384,1536]{1,0:T(8,128)(2,1)S(1)}, u32[]{:S(2)}, u32[]{:S(2)}) collective-permute-start(bf16[384,1536]{1,0:T(8,128)(2,1)} %param.12), channel_id=1, source_target_pairs={{0,30},{2,0},{4,2},{6,4},{8,6},{10,8},{12,10},{14,12},{16,14},{18,... | collective-permute-start | bytes 3538952 | tf_op jit(solution)/shard_map/ppermute | solution.py:14
  13.9 48.7 %collective-permute-start.6 = (bf16[384,1536]{0,1:T(8,128)(2,1)S(1)}, bf16[384,1536]{0,1:T(8,128)(2,1)S(1)}, u32[]{:S(2)}, u32[]{:S(2)}) collective-permute-start(bf16[384,1536]{0,1:T(8,128)(2,1)S(1)} %copy.41), channel_id=1, source_target_pairs={{0,30},{2,0},{4,2},{6,4},{8,6},{10,8},{12,10},{14,12},{16,14},{18,... | collective-permute-start | bytes 3538952 | tf_op jit(solution)/shard_map/ppermute | solution.py:14
  27.7 34.8 %copy-start.11 = (bf16[384,1536]{0,1:T(8,128)(2,1)}, bf16[384,1536]{0,1:T(8,128)(2,1)S(1)}, u32[]{:S(2)}) copy-start(bf16[384,1536]{0,1:T(8,128)(2,1)S(1)} %collective-permute-done) | copy-start | bytes 3538948
  27.7 52.0 %collective-permute-start.1 = (bf16[384,1536]{0,1:T(8,128)(2,1)S(1)}, bf16[384,1536]{0,1:T(8,128)(2,1)S(1)}, u32[]{:S(2)}, u32[]{:S(2)}) collective-permute-start(bf16[384,1536]{0,1:T(8,128)(2,1)S(1)} %collective-permute-done), channel_id=1, source_target_pairs={{0,2},{2,4},{4,6},{6,8},{8,10},{10,12},{12,14},{14,16},{16,18},{18... | collective-permute-start | bytes 3538952 | tf_op jit(solution)/shard_map/ppermute | solution.py:14
  49.8 164.3 %copy-start.23 = (bf16[384,1536]{1,0:T(8,128)(2,1)}, bf16[384,1536]{1,0:T(8,128)(2,1)S(1)}, u32[]{:S(2)}) copy-start(bf16[384,1536]{1,0:T(8,128)(2,1)S(1)} %collective-permute-done.12) | copy-start | bytes 3538948
  49.8 50.6 %collective-permute-start.13 = (bf16[384,1536]{1,0:T(8,128)(2,1)S(1)}, bf16[384,1536]{1,0:T(8,128)(2,1)S(1)}, u32[]{:S(2)}, u32[]{:S(2)}) collective-permute-start(bf16[384,1536]{1,0:T(8,128)(2,1)S(1)} %collective-permute-done.12), channel_id=1, source_target_pairs={{0,2},{2,4},{4,6},{6,8},{8,10},{10,12},{12,14},{14,16},{16,18},{18... | collective-permute-start | bytes 3538952 | tf_op jit(solution)/shard_map/ppermute | solution.py:14
  62.6 168.7 %copy-start.24 = (bf16[384,1536]{1,0:T(8,128)(2,1)}, bf16[384,1536]{1,0:T(8,128)(2,1)S(1)}, u32[]{:S(2)}) copy-start(bf16[384,1536]{1,0:T(8,128)(2,1)S(1)} %collective-permute-done.18) | copy-start | bytes 3538948
  62.6 50.5 %collective-permute-start.19 = (bf16[384,1536]{1,0:T(8,128)(2,1)S(1)}, bf16[384,1536]{1,0:T(8,128)(2,1)S(1)}, u32[]{:S(2)}, u32[]{:S(2)}) collective-permute-start(bf16[384,1536]{1,0:T(8,128)(2,1)S(1)} %collective-permute-done.18), channel_id=1, source_target_pairs={{0,30},{2,0},{4,2},{6,4},{8,6},{10,8},{12,10},{14,12},{16,14},{18,... | collective-permute-start | bytes 3538952 | tf_op jit(solution)/shard_map/ppermute | solution.py:14
  62.6 17.1 %copy-start.13 = (bf16[384,1536]{0,1:T(8,128)(2,1)}, bf16[384,1536]{0,1:T(8,128)(2,1)S(1)}, u32[]{:S(2)}) copy-start(bf16[384,1536]{0,1:T(8,128)(2,1)S(1)} %collective-permute-done.6) | copy-start | bytes 3538948
  62.6 50.4 %collective-permute-start.7 = (bf16[384,1536]{0,1:T(8,128)(2,1)S(1)}, bf16[384,1536]{0,1:T(8,128)(2,1)S(1)}, u32[]{:S(2)}, u32[]{:S(2)}) collective-permute-start(bf16[384,1536]{0,1:T(8,128)(2,1)S(1)} %collective-permute-done.6), channel_id=1, source_target_pairs={{0,30},{2,0},{4,2},{6,4},{8,6},{10,8},{12,10},{14,12},{16,14},{18,... | collective-permute-start | bytes 3538952 | tf_op jit(solution)/shard_map/ppermute | solution.py:14
  79.7 33.3 %copy-start.15 = (bf16[384,1536]{0,1:T(8,128)(2,1)}, bf16[384,1536]{0,1:T(8,128)(2,1)S(1)}, u32[]{:S(2)}) copy-start(bf16[384,1536]{0,1:T(8,128)(2,1)S(1)} %collective-permute-done.1) | copy-start | bytes 3538948
  79.7 50.4 %collective-permute-start.2 = (bf16[384,1536]{0,1:T(8,128)(2,1)S(1)}, bf16[384,1536]{0,1:T(8,128)(2,1)S(1)}, u32[]{:S(2)}, u32[]{:S(2)}) collective-permute-start(bf16[384,1536]{0,1:T(8,128)(2,1)S(1)} %collective-permute-done.1), channel_id=1, source_target_pairs={{0,2},{2,4},{4,6},{6,8},{8,10},{10,12},{12,14},{14,16},{16,18},{18... | collective-permute-start | bytes 3538952 | tf_op jit(solution)/shard_map/ppermute | solution.py:14
  100.4 130.8 %copy-start.25 = (bf16[384,1536]{1,0:T(8,128)(2,1)}, bf16[384,1536]{1,0:T(8,128)(2,1)S(1)}, u32[]{:S(2)}) copy-start(bf16[384,1536]{1,0:T(8,128)(2,1)S(1)} %collective-permute-done.13) | copy-start | bytes 3538948
  100.4 50.6 %collective-permute-start.14 = (bf16[384,1536]{1,0:T(8,128)(2,1)S(1)}, bf16[384,1536]{1,0:T(8,128)(2,1)S(1)}, u32[]{:S(2)}, u32[]{:S(2)}) collective-permute-start(bf16[384,1536]{1,0:T(8,128)(2,1)S(1)} %collective-permute-done.13), channel_id=1, source_target_pairs={{0,2},{2,4},{4,6},{6,8},{8,10},{10,12},{12,14},{14,16},{16,18},{18... | collective-permute-start | bytes 3538952 | tf_op jit(solution)/shard_map/ppermute | solution.py:14
  113.0 139.0 %copy-start.26 = (bf16[384,1536]{1,0:T(8,128)(2,1)}, bf16[384,1536]{1,0:T(8,128)(2,1)S(1)}, u32[]{:S(2)}) copy-start(bf16[384,1536]{1,0:T(8,128)(2,1)S(1)} %collective-permute-done.19) | copy-start | bytes 3538948
  113.0 50.6 %collective-permute-start.20 = (bf16[384,1536]{1,0:T(8,128)(2,1)S(1)}, bf16[384,1536]{1,0:T(8,128)(2,1)S(1)}, u32[]{:S(2)}, u32[]{:S(2)}) collective-permute-start(bf16[384,1536]{1,0:T(8,128)(2,1)S(1)} %collective-permute-done.19), channel_id=1, source_target_pairs={{0,30},{2,0},{4,2},{6,4},{8,6},{10,8},{12,10},{14,12},{16,14},{18,... | collective-permute-start | bytes 3538952 | tf_op jit(solution)/shard_map/ppermute | solution.py:14
  113.1 17.1 %copy-start.17 = (bf16[384,1536]{0,1:T(8,128)(2,1)}, bf16[384,1536]{0,1:T(8,128)(2,1)S(1)}, u32[]{:S(2)}) copy-start(bf16[384,1536]{0,1:T(8,128)(2,1)S(1)} %collective-permute-done.7) | copy-start | bytes 3538948
  113.1 50.5 %collective-permute-start.8 = (bf16[384,1536]{0,1:T(8,128)(2,1)S(1)}, bf16[384,1536]{0,1:T(8,128)(2,1)S(1)}, u32[]{:S(2)}, u32[]{:S(2)}) collective-permute-start(bf16[384,1536]{0,1:T(8,128)(2,1)S(1)} %collective-permute-done.7), channel_id=1, source_target_pairs={{0,30},{2,0},{4,2},{6,4},{8,6},{10,8},{12,10},{14,12},{16,14},{18,... | collective-permute-start | bytes 3538952 | tf_op jit(solution)/shard_map/ppermute | solution.py:14
  130.2 33.4 %copy-start.19 = (bf16[384,1536]{0,1:T(8,128)(2,1)}, bf16[384,1536]{0,1:T(8,128)(2,1)S(1)}, u32[]{:S(2)}) copy-start(bf16[384,1536]{0,1:T(8,128)(2,1)S(1)} %collective-permute-done.2) | copy-start | bytes 3538948
  130.2 50.6 %collective-permute-start.3 = (bf16[384,1536]{0,1:T(8,128)(2,1)S(1)}, bf16[384,1536]{0,1:T(8,128)(2,1)S(1)}, u32[]{:S(2)}, u32[]{:S(2)}) collective-permute-start(bf16[384,1536]{0,1:T(8,128)(2,1)S(1)} %collective-permute-done.2), channel_id=1, source_target_pairs={{0,2},{2,4},{4,6},{6,8},{8,10},{10,12},{12,14},{14,16},{16,18},{18... | collective-permute-start | bytes 3538952 | tf_op jit(solution)/shard_map/ppermute | solution.py:14
  150.9 101.1 %copy-start.28 = (bf16[384,1536]{1,0:T(8,128)(2,1)}, bf16[384,1536]{1,0:T(8,128)(2,1)S(1)}, u32[]{:S(2)}) copy-start(bf16[384,1536]{1,0:T(8,128)(2,1)S(1)} %collective-permute-done.14) | copy-start | bytes 3538948
  150.9 50.6 %collective-permute-start.15 = (bf16[384,1536]{1,0:T(8,128)(2,1)S(1)}, bf16[384,1536]{1,0:T(8,128)(2,1)}, u32[]{:S(2)}, u32[]{:S(2)}) collective-permute-start(bf16[384,1536]{1,0:T(8,128)(2,1)S(1)} %collective-permute-done.14), channel_id=1, source_target_pairs={{0,2},{2,4},{4,6},{6,8},{8,10},{10,12},{12,14},{14,16},{16,18},{18... | collective-permute-start | bytes 3538952 | tf_op jit(solution)/shard_map/ppermute | solution.py:14
  163.6 88.5 %copy-start.29 = (bf16[384,1536]{1,0:T(8,128)(2,1)}, bf16[384,1536]{1,0:T(8,128)(2,1)S(1)}, u32[]{:S(2)}) copy-start(bf16[384,1536]{1,0:T(8,128)(2,1)S(1)} %collective-permute-done.20) | copy-start | bytes 3538948
  163.6 50.6 %collective-permute-start.21 = (bf16[384,1536]{1,0:T(8,128)(2,1)S(1)}, bf16[384,1536]{1,0:T(8,128)(2,1)}, u32[]{:S(2)}, u32[]{:S(2)}) collective-permute-start(bf16[384,1536]{1,0:T(8,128)(2,1)S(1)} %collective-permute-done.20), channel_id=1, source_target_pairs={{0,30},{2,0},{4,2},{6,4},{8,6},{10,8},{12,10},{14,12},{16,14},{18,... | collective-permute-start | bytes 3538952 | tf_op jit(solution)/shard_map/ppermute | solution.py:14
  163.6 17.1 %copy-start.21 = (bf16[384,1536]{0,1:T(8,128)(2,1)}, bf16[384,1536]{0,1:T(8,128)(2,1)S(1)}, u32[]{:S(2)}) copy-start(bf16[384,1536]{0,1:T(8,128)(2,1)S(1)} %collective-permute-done.8) | copy-start | bytes 3538948
  163.6 50.5 %collective-permute-start.9 = (bf16[384,1536]{0,1:T(8,128)(2,1)S(1)}, bf16[384,1536]{0,1:T(8,128)(2,1)}, u32[]{:S(2)}, u32[]{:S(2)}) collective-permute-start(bf16[384,1536]{0,1:T(8,128)(2,1)S(1)} %collective-permute-done.8), channel_id=1, source_target_pairs={{0,30},{2,0},{4,2},{6,4},{8,6},{10,8},{12,10},{14,12},{16,14},{18,... | collective-permute-start | bytes 3538952 | tf_op jit(solution)/shard_map/ppermute | solution.py:14
  180.7 71.3 %copy-start.27 = (bf16[384,1536]{0,1:T(8,128)(2,1)}, bf16[384,1536]{0,1:T(8,128)(2,1)S(1)}, u32[]{:S(2)}) copy-start(bf16[384,1536]{0,1:T(8,128)(2,1)S(1)} %collective-permute-done.3) | copy-start | bytes 3538948
  180.7 50.5 %collective-permute-start.4 = (bf16[384,1536]{0,1:T(8,128)(2,1)S(1)}, bf16[384,1536]{0,1:T(8,128)(2,1)}, u32[]{:S(2)}, u32[]{:S(2)}) collective-permute-start(bf16[384,1536]{0,1:T(8,128)(2,1)S(1)} %collective-permute-done.3), channel_id=1, source_target_pairs={{0,2},{2,4},{4,6},{6,8},{8,10},{10,12},{12,14},{14,16},{16,18},{18... | collective-permute-start | bytes 3538952 | tf_op jit(solution)/shard_map/ppermute | solution.py:14
  201.5 80.8 %collective-permute-start.16 = (bf16[384,1536]{1,0:T(8,128)(2,1)}, bf16[384,1536]{1,0:T(8,128)(2,1)}, u32[]{:S(2)}, u32[]{:S(2)}) collective-permute-start(bf16[384,1536]{1,0:T(8,128)(2,1)} %collective-permute-done.15), channel_id=1, source_target_pairs={{0,2},{2,4},{4,6},{6,8},{8,10},{10,12},{12,14},{14,16},{16,18},{18... | collective-permute-start | bytes 3538952 | tf_op jit(solution)/shard_map/ppermute | solution.py:14
  214.1 73.1 %collective-permute-start.22 = (bf16[384,1536]{1,0:T(8,128)(2,1)}, bf16[384,1536]{1,0:T(8,128)(2,1)}, u32[]{:S(2)}, u32[]{:S(2)}) collective-permute-start(bf16[384,1536]{1,0:T(8,128)(2,1)} %collective-permute-done.21), channel_id=1, source_target_pairs={{0,30},{2,0},{4,2},{6,4},{8,6},{10,8},{12,10},{14,12},{16,14},{18,... | collective-permute-start | bytes 3538952 | tf_op jit(solution)/shard_map/ppermute | solution.py:14
  214.2 77.4 %collective-permute-start.10 = (bf16[384,1536]{0,1:T(8,128)(2,1)}, bf16[384,1536]{0,1:T(8,128)(2,1)}, u32[]{:S(2)}, u32[]{:S(2)}) collective-permute-start(bf16[384,1536]{0,1:T(8,128)(2,1)} %collective-permute-done.9), channel_id=1, source_target_pairs={{0,30},{2,0},{4,2},{6,4},{8,6},{10,8},{12,10},{14,12},{16,14},{18,... | collective-permute-start | bytes 3538952 | tf_op jit(solution)/shard_map/ppermute | solution.py:14
  231.2 61.5 %collective-permute-start.5 = (bf16[384,1536]{0,1:T(8,128)(2,1)}, bf16[384,1536]{0,1:T(8,128)(2,1)}, u32[]{:S(2)}, u32[]{:S(2)}) collective-permute-start(bf16[384,1536]{0,1:T(8,128)(2,1)} %collective-permute-done.4), channel_id=1, source_target_pairs={{0,2},{2,4},{4,6},{6,8},{8,10},{10,12},{12,14},{14,16},{16,18},{18... | collective-permute-start | bytes 3538952 | tf_op jit(solution)/shard_map/ppermute | solution.py:14
  282.3 212.1 %collective-permute-start.17 = (bf16[384,1536]{1,0:T(8,128)(2,1)}, bf16[384,1536]{1,0:T(8,128)(2,1)}, u32[]{:S(2)}, u32[]{:S(2)}) collective-permute-start(bf16[384,1536]{1,0:T(8,128)(2,1)} %collective-permute-done.16), channel_id=1, source_target_pairs={{0,2},{2,4},{4,6},{6,8},{8,10},{10,12},{12,14},{14,16},{16,18},{18... | collective-permute-start | bytes 3538952 | tf_op jit(solution)/shard_map/ppermute | solution.py:14
  289.6 8.3 copy-start.12
  289.6 219.8 %collective-permute-start.23 = (bf16[384,1536]{1,0:T(8,128)(2,1)}, bf16[384,1536]{1,0:T(8,128)(2,1)}, u32[]{:S(2)}, u32[]{:S(2)}) collective-permute-start(bf16[384,1536]{1,0:T(8,128)(2,1)} %collective-permute-done.22), channel_id=1, source_target_pairs={{0,30},{2,0},{4,2},{6,4},{8,6},{10,8},{12,10},{14,12},{16,14},{18,... | collective-permute-start | bytes 3538952 | tf_op jit(solution)/shard_map/ppermute | solution.py:14
  291.6 26.7 %collective-permute-start.11 = (bf16[384,1536]{0,1:T(8,128)(2,1)}, bf16[384,1536]{0,1:T(8,128)(2,1)S(1)}, u32[]{:S(2)}, u32[]{:S(2)}) collective-permute-start(bf16[384,1536]{0,1:T(8,128)(2,1)} %collective-permute-done.10), channel_id=1, source_target_pairs={{0,30},{2,0},{4,2},{6,4},{8,6},{10,8},{12,10},{14,12},{16,14},{18,... | collective-permute-start | bytes 3538952 | tf_op jit(solution)/shard_map/ppermute | solution.py:14
  551.6 8.9 slice-start
  552.2 8.3 slice-start.1
  577.3 8.9 slice-start
  577.9 8.3 slice-start.1
  602.9 8.9 slice-start
  603.5 8.3 slice-start.1
  628.6 8.9 slice-start
  629.2 8.3 slice-start.1
  654.2 8.9 slice-start
  654.8 8.3 slice-start.1
  679.9 8.9 slice-start
  680.5 8.3 slice-start.1
  705.5 8.9 slice-start
  706.1 8.3 slice-start.1
  731.2 8.9 slice-start
  731.8 8.3 slice-start.1
  756.8 8.9 slice-start
  757.4 8.3 slice-start.1
  782.5 8.9 slice-start
  783.1 8.3 slice-start.1
  808.2 8.9 slice-start
  808.7 8.3 slice-start.1
  833.8 8.9 slice-start
  834.4 8.3 slice-start.1
  (18 other events, 89.0 us)
Sparse Core Ops, SparseCore 0:
  856.0 40.5 reduce-scatter.1
where the time goes:
time: 908 us; the launch traced here: 903 us
  local copies, waits for them, and re-layouts  268 us (30%)
  starting transfers between devices  236 us (26%)
  matrix products  186 us (20%)
  other arithmetic  128 us (14%)
  waiting for transfers between devices  69.9 us (8%)
  between operations  15.7 us (2%)
    ppermute x24, starting transfers between devices, from_behind(): lax.ppermute(value, axis, [(i, (i + by) % length) for i in range(length)])  236 us
    dynamic_slice x26, local copies, waits for them, and re-layouts, accumulate(): lax.dynamic_index_in_dim(score_store, block_index, 0, keepdims=False)  187 us
    dot_general x13, matrix products, add_block(): jnp.einsum('hqk,khd->qhd', exponent.astype(jnp.bfloat16), value_block, pr...  107 us
    dynamic_update_slice x13, other arithmetic, find_top(): lax.dynamic_update_index_in_dim(stored, fresh_scores, block_index, 0)  85 us
    dot_general x13, matrix products, block_scores(): jnp.einsum('qhd,khd->hqk', query_heads, key_block, preferred_element_type...  69.4 us
    reduce_scatter x1, waiting for transfers between devices, per_device(): lax.psum_scatter(partial_terms.astype(jnp.bfloat16), 'head', scatter_dime...  40.7 us
    unnamed x90, local copies, waits for them, and re-layouts  35.1 us
    ppermute x24, waiting for transfers between devices, from_behind(): lax.ppermute(value, axis, [(i, (i + by) % length) for i in range(length)])  29.2 us
  transfers between devices with their start and end apart: 25, of which 3 were waited for; matrix products, arithmetic and copies ran while one was open for 25% of the time, Pallas kernels for 0%

commit v1 on v0

v1 whole, which is shorter than its diff:
```python
import functools
import math

import jax
import jax.numpy as jnp
from jax import lax
from jax.experimental import pallas as pl
from jax.experimental.pallas import tpu as pltpu
from jax.sharding import PartitionSpec as P

HEAD_DIM = 128
REACH = 6


def attention_body(width, place_ref, count_ref, q_ref, k_ref, v_ref, out_ref, scores, tops):
    row = pl.program_id(1)
    count = count_ref[row]
    query = q_ref[0, 0]
    tile_rows = query.shape[0]
    scale = math.log2(math.e) / math.sqrt(HEAD_DIM)
    tops[...] = jnp.full(tops.shape, -jnp.inf, jnp.float32)

    def find(entry, carry):
        place = place_ref[row * width + entry]
        fresh = lax.dot_general(
            query, k_ref[0, place], (((1,), (1,)), ((), ())), preferred_element_type=jnp.float32
        )
        scores[entry] = fresh
        best = tops[...]
        for lane in range(0, fresh.shape[1], HEAD_DIM):
            best = jnp.maximum(best, fresh[:, lane : lane + HEAD_DIM])
        tops[...] = best
        return carry

    lax.fori_loop(0, count, find, 0)
    top = jnp.max(tops[...], axis=1, keepdims=True) * scale
    ones = jnp.ones((k_ref.shape[2], HEAD_DIM), jnp.bfloat16)

    def add(entry, summed):
        place = place_ref[row * width + entry]
        weights = jnp.exp2(scores[entry] * scale - top).astype(jnp.bfloat16)
        paired = jnp.concatenate([v_ref[0, place], ones], axis=1)
        return summed + jnp.dot(weights, paired, preferred_element_type=jnp.float32)

    summed = lax.fori_loop(0, count, add, jnp.zeros((tile_rows, 2 * HEAD_DIM), jnp.float32))
    out_ref[0, 0] = (summed[:, :HEAD_DIM] / summed[:, HEAD_DIM:]).astype(jnp.bfloat16)


def attention(q, k, v, place, count):
    heads, query_tiles, rows, _ = q.shape
    key_tiles = k.shape[1]
    width = place.shape[1]
    units = heads * query_tiles * min(width, key_tiles)
    key_spec = pl.BlockSpec((1, key_tiles, rows, HEAD_DIM), lambda h, t, *_: (h, 0, 0, 0))
    tile_spec = pl.BlockSpec((1, 1, rows, HEAD_DIM), lambda h, t, *_: (h, t, 0, 0))
    return pl.pallas_call(
        functools.partial(attention_body, width),
        out_shape=jax.ShapeDtypeStruct(q.shape, jnp.bfloat16),
        grid_spec=pltpu.PrefetchScalarGridSpec(
            num_scalar_prefetch=2,
            grid=(heads, query_tiles),
            in_specs=[tile_spec, key_spec, key_spec],
            out_specs=tile_spec,
            scratch_shapes=[
                pltpu.VMEM((width, rows, rows), jnp.float32),
                pltpu.VMEM((rows, HEAD_DIM), jnp.float32),
            ],
        ),
        compiler_params=pltpu.CompilerParams(vmem_limit_bytes=40 * 1024 * 1024),
        cost_estimate=pl.CostEstimate(
            flops=units * rows * rows * HEAD_DIM * 4,
            bytes_accessed=2 * (2 * q.size + k.size + v.size),
            transcendentals=units * rows * rows,
        ),
    )(place.reshape(-1), count, q, k, v)


def listed_slots(kv_tiles, tile_order, slot):
    listed = kv_tiles[tile_order[slot]]
    slot_ids = jnp.arange(tile_order.shape[0], dtype=jnp.int32)
    found = jnp.sum(
        jnp.where(tile_order[None, :] == jnp.maximum(listed, 0)[:, None], slot_ids[None, :], 0), axis=1
    )
    return found, jnp.sum((listed >= 0).astype(jnp.int32))


def by_ring(queries, keys, values, kv_tiles, tile_order, out_weight):
    rows, local_width = queries.shape
    heads = local_width // HEAD_DIM
    n = lax.axis_size("seq")
    me = lax.axis_index("seq")
    window = 2 * REACH + 1
    pair = jnp.stack([keys, values])
    received = {0: pair}
    for heading in (1, -1):
        moving = pair
        for stride in range(1, REACH + 1):
            moving = lax.ppermute(moving, "seq", [(i, (i + heading) % n) for i in range(n)])
            received[-heading * stride] = moving
    both = jnp.stack([received[o] for o in range(-REACH, REACH + 1)])
    both = both.reshape(window, 2, rows, heads, HEAD_DIM).transpose(1, 3, 0, 2, 4)
    q = queries.reshape(rows, heads, HEAD_DIM).transpose(1, 0, 2)[:, None]
    slots, count = listed_slots(kv_tiles, tile_order, me)
    place = (slots - me + REACH) % n
    place = jnp.clip(place, 0, window - 1)
    attended = attention(q, both[0], both[1], place[None], count[None])
    attended = attended[:, 0].transpose(1, 0, 2).reshape(rows, local_width)
    partial = jnp.dot(attended, out_weight, preferred_element_type=jnp.float32).astype(jnp.bfloat16)
    return lax.psum_scatter(partial, "head", scatter_dimension=1, tiled=True)


def by_heads(groups, queries, keys, values, kv_tiles, tile_order, out_weight):
    rows, local_width = queries.shape
    heads = local_width // HEAD_DIM
    n = lax.axis_size("seq")
    n_head = lax.axis_size("head")
    sub = n // groups
    share = heads // groups
    me = lax.axis_index("seq")
    plane, inner = me // sub, me % sub

    def plane_shift(x, by):
        return lax.ppermute(
            x, "seq", [(i, (i // sub + by) % groups * sub + i % sub) for i in range(n)]
        )

    def inner_swap(x, bit):
        return lax.ppermute(x, "seq", [(i, i ^ bit) for i in range(n)])

    bits = []
    bit = sub // 2
    while bit:
        bits.append(bit)
        bit //= 2
    mask_place = [0] * sub
    for mask in range(sub):
        mask_place[mask] = sum(1 << i for i, b in enumerate(bits) if mask & b)
    mask_place = jnp.array(mask_place, jnp.int32)

    def place_of(slot):
        return mask_place[(slot % sub) ^ inner] * groups + (plane - slot // sub) % groups

    places, counts = [], []
    for o in range(groups):
        slots, count = listed_slots(kv_tiles, tile_order, (plane - o) % groups * sub + inner)
        places.append(place_of(slots))
        counts.append(count)
    place, count = jnp.stack(places), jnp.stack(counts)

    my_head = lax.axis_index("head")
    columns = out_weight.shape[1] // n_head
    half = out_weight.shape[0] // 2
    own_half = me % 2
    weight_rows = {0: lax.dynamic_slice_in_dim(out_weight, my_head * columns, columns, 1)}
    for o in range(1, n_head):
        piece = lax.dynamic_slice(
            out_weight, (own_half * half, (my_head + o) % n_head * columns), (half, columns)
        )
        piece = lax.ppermute(piece, "head", [(i, (i + o) % n_head) for i in range(n_head)])
        other = inner_swap(piece, 1)
        weight_rows[o] = jnp.where(
            own_half == 0,
            jnp.concatenate([piece, other], axis=0),
            jnp.concatenate([other, piece], axis=0),
        )

    def cut(array, to_plane, j):
        return lax.dynamic_slice_in_dim(array, (to_plane * share + j) * HEAD_DIM, HEAD_DIM, 1)

    total = jnp.zeros((rows, columns), jnp.float32)
    sent_before = None
    home = [[None] * groups for _ in range(share)]
    for j in range(share):
        pieces = []
        for o in range(groups):
            to_plane = (plane + o) % groups
            pieces.append(jnp.stack([cut(a, to_plane, j) for a in (queries, keys, values)]))
        if sent_before is not None:
            pieces, sent_before = lax.optimization_barrier((pieces, sent_before))
        arrived = [pieces[0]] + [plane_shift(pieces[o], o) for o in range(1, groups)]
        sent_before = arrived
        stacked = jnp.stack(arrived)
        q = stacked[:, 0][None]
        both = stacked[:, 1:].transpose(1, 0, 2, 3)
        for b in bits:
            both = jnp.concatenate([both, inner_swap(both, b)], axis=1)
        attended = attention(q, both[0][None], both[1][None], place, count)[0]
        for o in range(groups):
            home[j][o] = attended[o] if o == 0 else plane_shift(attended[o], -o)
    for j in range(share):
        terms, weights = [], []
        for h in range(n_head):
            for o in range(groups):
                piece = home[j][o]
                if h:
                    piece = lax.ppermute(
                        piece, "head", [(i, (i + h) % n_head) for i in range(n_head)]
                    )
                terms.append(piece)
                start = ((plane + o) % groups * share + j) * HEAD_DIM
                weights.append(lax.dynamic_slice_in_dim(weight_rows[h], start, HEAD_DIM, 0))
        total = total + jnp.dot(
            jnp.concatenate(terms, axis=1),
            jnp.concatenate(weights, axis=0),
            preferred_element_type=jnp.float32,
        )
    return total.astype(jnp.bfloat16)


def per_device(queries, keys, values, kv_tiles, tile_order, out_weight):
    n = lax.axis_size("seq")
    groups = math.gcd(queries.shape[1] // HEAD_DIM, n)
    sub = n // groups
    power_of_two = sub & (sub - 1) == 0
    if groups > 1 and sub > 1 and power_of_two and n <= 2 * (2 * REACH + 1):
        return by_heads(groups, queries, keys, values, kv_tiles, tile_order, out_weight)
    return by_ring(queries, keys, values, kv_tiles, tile_order, out_weight)


def solution(mesh):
    return jax.shard_map(
        per_device,
        mesh=mesh,
        in_specs=(P("seq", "head"), P("seq", "head"), P("seq", "head"), P(), P(), P("head", None)),
        out_specs=P("seq", "head"),
        check_vma=False,
    )
```

time: 908 us -> 271 us (0.30)
  local copies, waits for them, and re-layouts: 268 us -> 31.1 us
  starting transfers between devices: 236 us -> 53.9 us
  matrix products: 186 us -> 9 us
  other arithmetic: 128 us -> 27.6 us
  Pallas kernels: 0 us -> 57.8 us
  waiting for transfers between devices: 69.9 us -> 83.8 us
    dynamic_slice x53 -> x2, local copies, waits for them, and re-layouts: 203 us -> 3.92 us  [the longest x1 3.3 us: by_heads(): lax.dynamic_slice(out_weight, (own_half * half, (my_head + o) % n_head *...]
    ppermute x24 -> x38, starting transfers between devices: 236 us -> 53.9 us  [the longest x18 39.6 us: plane_shift(): lax.ppermute(x, 'seq', [(i, (i // sub + by) % groups * sub + i % sub) for...]
    dot_general x27 -> x3, matrix products: 186 us -> 9 us  [by_heads(): jnp.dot(jnp.concatenate(terms, axis=1), jnp.concatenate(weights, axis=0),...]
    dynamic_update_slice x13 -> x0, other arithmetic: 85 us -> none  [find_top(): lax.dynamic_update_index_in_dim(stored, fresh_scores, block_index, 0)]
    pallas_call x0 -> x3, Pallas kernels: none -> 57.8 us  [attention(): pl.pallas_call(functools.partial(attention_body, width), out_shape=jax.Sh...]
    ppermute x24 -> x38, waiting for transfers between devices: 29.2 us -> 83.8 us  [the longest x18 51.5 us: plane_shift(): lax.ppermute(x, 'seq', [(i, (i // sub + by) % groups * sub + i % sub) for...]
    reduce_scatter x1 -> x0, waiting for transfers between devices: 40.7 us -> none  [per_device(): lax.psum_scatter(partial_terms.astype(jnp.bfloat16), 'head', scatter_dime...]
    ppermute x12 -> x0, local copies, waits for them, and re-layouts: 28 us -> none  [from_behind(): lax.ppermute(value, axis, [(i, (i + by) % length) for i in range(length)])]
  transfers between devices with their start and end apart: 25 -> 38, of which waited for: 3 -> 19; matrix products, arithmetic and copies ran while one was open for 25% -> 17% of each run, Pallas kernels for 0% -> 21%
where the time goes in v1:
time: 271 us
  waiting for transfers between devices  83.8 us (31%)
  Pallas kernels  57.8 us (21%)
  starting transfers between devices  53.9 us (20%)
  local copies, waits for them, and re-layouts  31.1 us (11%)
  other arithmetic  27.6 us (10%)
  matrix products  9 us (3%)
  between operations  8.23 us (3%)
    pallas_call x3, Pallas kernels, attention(): pl.pallas_call(functools.partial(attention_body, width), out_shape=jax.Sh...  57.8 us
    ppermute x18, waiting for transfers between devices, plane_shift(): lax.ppermute(x, 'seq', [(i, (i // sub + by) % groups * sub + i % sub) for...  51.5 us
    ppermute x18, starting transfers between devices, plane_shift(): lax.ppermute(x, 'seq', [(i, (i // sub + by) % groups * sub + i % sub) for...  39.6 us
    unnamed x108, local copies, waits for them, and re-layouts  19.7 us
    ppermute x12, waiting for transfers between devices, by_heads(): lax.ppermute(piece, 'head', [(i, (i + h) % n_head) for i in range(n_head)])  18.3 us
    ppermute x7, waiting for transfers between devices, inner_swap(): return lax.ppermute(x, 'seq', [(i, i ^ bit) for i in range(n)])  14.1 us
    ppermute x12, starting transfers between devices, by_heads(): lax.ppermute(piece, 'head', [(i, (i + h) % n_head) for i in range(n_head)])  9.48 us
    dot_general x3, matrix products, by_heads(): jnp.dot(jnp.concatenate(terms, axis=1), jnp.concatenate(weights, axis=0),...  9 us
  transfers between devices with their start and end apart: 38, of which 19 were waited for; matrix products, arithmetic and copies ran while one was open for 17% of the time, Pallas kernels for 21%

profile of v1, /device:TPU:0, one launch (start us, length us, event | category | flops | bytes accessed | tf_op | source)
XLA Modules:
  0.0 271.3 jit_solution(10916461039141590339)
XLA Ops:
  0.0 1.6 dynamic-slice_bitcast_fusion.35
  2.1 1.3 dynamic-slice_bitcast_fusion.33
  4.2 3.0 %collective-permute-start = (bf16[3,384,128]{2,1,0:T(8,128)(2,1)}, bf16[3,384,128]{2,1,0:T(8,128)(2,1)S(1)}, u32[]{:S(2)}, u32[]{:S(2)}) collective-permute-start(bf16[3,384,128]{2,1,0:T(8,128)(2,1)} %pad_maximum_fusion.16), channel_id=1, source_target_pairs={{0,8},{2,10},{4,12},{6,14},{8,16},{10,18},{12,20},{14,22},{16,24},... | collective-permute-start | bytes 884744 | tf_op jit(solution)/shard_map/ppermute | solution.py:123
  8.0 2.6 collective-permute-start.1
  11.3 1.3 collective-permute-start.2
  12.7 3.3 %dynamic_slice.232 = bf16[768,1536]{1,0:T(8,128)(2,1)} dynamic-slice(bf16[1536,3072]{1,0:T(8,128)(2,1)} %param.12, s32[]{:T(128)S(6)} %select_n.498, s32[]{:T(128)S(6)} %select_n.500), dynamic_slice_sizes={768,1536} | dynamic-slice | bytes 4718596 | tf_op jit(solution)/shard_map/dynamic_slice | solution.py:156
  16.0 1.5 collective-permute-start.12
  25.6 1.5 fusion.13
  33.7 2.4 dynamic-slice_dynamic-update-slice_fusion.23
  36.1 2.5 dynamic-slice_dynamic-update-slice_fusion.22
  38.6 2.9 %dynamic-slice_dynamic-update-slice_fusion.21 = (bf16[1024,1536]{1,0:T(8,128)(2,1)}, bf16[1024,1536]{1,0:T(8,128)(2,1)}, bf16[1024,1536]{1,0:T(8,128)(2,1)}) fusion(bf16[1024,1536]{1,0:T(8,128)(2,1)} %get-tuple-element.35, bf16[1536,3072]{1,0:T(8,128)(2,1)} %param.12, s32[]{:T(128)S(6)} %select_n.494, s32[]{:T(128)S(6)} %select_n.492, s32[]{:T(128)S(6)} %select_n.514, ...), kind=kLoop, calls=%fused_computation.50 | loop fusion | bytes 2359312
  41.5 2.9 %dynamic-slice_dynamic-update-slice_fusion.20 = (bf16[1024,1536]{1,0:T(8,128)(2,1)}, bf16[1024,1536]{1,0:T(8,128)(2,1)}, bf16[1024,1536]{1,0:T(8,128)(2,1)}) fusion(bf16[1024,1536]{1,0:T(8,128)(2,1)} %get-tuple-element.32, bf16[1536,3072]{1,0:T(8,128)(2,1)} %param.12, s32[]{:T(128)S(6)} %select_n.495, s32[]{:T(128)S(6)} %select_n.492, ...), kind=kLoop, calls=%fused_computation.49 | loop fusion | bytes 2359312
  45.2 1.0 fusion.4
  46.3 1.6 collective-permute-start.3
  51.0 2.8 %collective-permute-start.16 = (bf16[3,384,128]{2,1,0:T(8,128)(2,1)}, bf16[3,384,128]{2,1,0:T(8,128)(2,1)S(1)}, u32[]{:S(2)}, u32[]{:S(2)}) collective-permute-start(bf16[3,384,128]{2,1,0:T(8,128)(2,1)} %pad_maximum_fusion.22), channel_id=1, source_target_pairs={{0,24},{2,26},{4,28},{6,30},{8,0},{10,2},{12,4},{14,6},{16,8},{18,... | collective-permute-start | bytes 884744 | tf_op jit(solution)/shard_map/ppermute | solution.py:123
  54.5 2.0 dynamic-slice_dynamic-update-slice_fusion.5
  56.5 5.5 %collective-permute-done.14 = bf16[3,384,128]{2,1,0:T(8,128)(2,1)S(1)} collective-permute-done((bf16[3,384,128]{2,1,0:T(8,128)(2,1)}, bf16[3,384,128]{2,1,0:T(8,128)(2,1)S(1)}, u32[]{:S(2)}, u32[]{:S(2)}) %collective-permute-start.14) | collective-permute-done | bytes 294944 | tf_op jit(solution)/shard_map/ppermute | solution.py:123
  62.0 10.1 %collective-permute-done.15 = bf16[3,384,128]{2,1,0:T(8,128)(2,1)S(1)} collective-permute-done((bf16[3,384,128]{2,1,0:T(8,128)(2,1)}, bf16[3,384,128]{2,1,0:T(8,128)(2,1)S(1)}, u32[]{:S(2)}, u32[]{:S(2)}) %collective-permute-start.15) | collective-permute-done | bytes 294944 | tf_op jit(solution)/shard_map/ppermute | solution.py:123
  72.2 12.5 %collective-permute-start.26 = (bf16[3,384,128]{2,1,0:T(8,128)(2,1)}, bf16[3,384,128]{2,1,0:T(8,128)(2,1)S(1)}, u32[]{:S(2)}, u32[]{:S(2)}) collective-permute-start(bf16[3,384,128]{2,1,0:T(8,128)(2,1)} %pad_maximum_fusion.24), channel_id=1, source_target_pairs={{0,8},{2,10},{4,12},{6,14},{8,16},{10,18},{12,20},{14,22},{16,24},... | collective-permute-start | bytes 884744 | tf_op jit(solution)/shard_map/ppermute | solution.py:123
  84.7 2.4 collective-permute-start.28
  87.1 1.4 pad_maximum_fusion.3
  88.6 1.2 fusion.3
  89.8 2.7 collective-permute-done.26
  93.0 7.0 %collective-permute-done.27 = bf16[3,384,128]{2,1,0:T(8,128)(2,1)S(1)} collective-permute-done((bf16[3,384,128]{2,1,0:T(8,128)(2,1)}, bf16[3,384,128]{2,1,0:T(8,128)(2,1)S(1)}, u32[]{:S(2)}, u32[]{:S(2)}) %collective-permute-start.27) | collective-permute-done | bytes 294944 | tf_op jit(solution)/shard_map/ppermute | solution.py:123
  100.1 3.6 %collective-permute-done.28 = bf16[3,384,128]{2,1,0:T(8,128)(2,1)S(1)} collective-permute-done((bf16[3,384,128]{2,1,0:T(8,128)(2,1)}, bf16[3,384,128]{2,1,0:T(8,128)(2,1)S(1)}, u32[]{:S(2)}, u32[]{:S(2)}) %collective-permute-start.28) | collective-permute-done | bytes 294944 | tf_op jit(solution)/shard_map/ppermute | solution.py:123
  104.3 2.6 pad_add_fusion.1.count_ref
  107.0 2.1 dynamic-slice_dynamic-update-slice_fusion.4
  109.1 1.0 maximum_bitcast_fusion.2.q_ref
  110.1 1.1 maximum_bitcast_fusion.1.q_ref
  111.3 1.8 collective-permute-done.17
  113.1 1.3 pad_maximum_fusion.4
  114.4 12.3 %collective-permute-done.29 = bf16[2,4,384,128]{3,2,1,0:T(8,128)(2,1)S(1)} collective-permute-done((bf16[2,4,384,128]{3,2,1,0:T(8,128)(2,1)S(1)}, bf16[2,4,384,128]{3,2,1,0:T(8,128)(2,1)S(1)}, u32[]{:S(2)}, u32[]{:S(2)}) %collective-permute-start.29) | collective-permute-done | bytes 786464 | tf_op jit(solution)/shard_map/ppermute | solution.py:128
  127.4 1.7 pad_maximum_fusion
  129.4 19.3 %shard_map.73 = bf16[1,4,384,128]{3,2,1,0:T(8,128)(2,1)S(1)} custom-call(s32[52]{0:T(128)S(1)} %reshape.654.place_ref, s32[4]{0:T(128)S(1)} %pad_add_fusion.1.count_ref, bf16[1,4,384,128]{3,2,1,0:T(8,128)(2,1)S(1)} %maximum_bitcast_fusion.2.q_ref, bf16[1,16,384,128]{3,2,1,0:T(8,128)(2,1)S(1)} %get-tuple-element.52.k_ref, ...), custom_call_target="tpu_custom_call" | custom-call | flops 3925868544 | bytes 3932160 | tf_op jit(solution)/shard_map/pallas_call | solution.py:56
  148.7 4.7 %collective-permute-start.5 = (bf16[384,128]{1,0:T(8,128)(2,1)S(1)}, bf16[384,128]{1,0:T(8,128)(2,1)S(1)}, u32[]{:S(2)}, u32[]{:S(2)}) collective-permute-start(bf16[384,128]{1,0:T(8,128)(2,1)S(1)} %get-tuple-element.96), channel_id=1, source_target_pairs={{0,24},{2,26},{4,28},{6,30},{8,0},{10,2},{12,4},{14,6},{16,8},{18,... | collective-permute-start | bytes 294920 | tf_op jit(solution)/shard_map/ppermute | solution.py:123
  153.5 2.3 collective-permute-done.5
  156.6 3.9 %collective-permute-done.7 = bf16[384,128]{1,0:T(8,128)(2,1)S(1)} collective-permute-done((bf16[384,128]{1,0:T(8,128)(2,1)S(1)}, bf16[384,128]{1,0:T(8,128)(2,1)S(1)}, u32[]{:S(2)}, u32[]{:S(2)}) %collective-permute-start.7) | collective-permute-done | bytes 98336 | tf_op jit(solution)/shard_map/ppermute | solution.py:123
  160.9 4.1 %collective-permute-done.6 = bf16[384,128]{1,0:T(8,128)(2,1)S(1)} collective-permute-done((bf16[384,128]{1,0:T(8,128)(2,1)S(1)}, bf16[384,128]{1,0:T(8,128)(2,1)S(1)}, u32[]{:S(2)}, u32[]{:S(2)}) %collective-permute-start.6) | collective-permute-done | bytes 98336 | tf_op jit(solution)/shard_map/ppermute | solution.py:123
  165.6 1.7 collective-permute-start.9
  167.3 4.7 %collective-permute-done.9 = bf16[384,128]{1,0:T(8,128)(2,1)S(1)} collective-permute-done((bf16[384,128]{1,0:T(8,128)(2,1)S(1)}, bf16[384,128]{1,0:T(8,128)(2,1)S(1)}, u32[]{:S(2)}, u32[]{:S(2)}) %collective-permute-start.9) | collective-permute-done | bytes 98336 | tf_op jit(solution)/shard_map/ppermute | solution.py:196
  172.5 4.2 %collective-permute-done.10 = bf16[384,128]{1,0:T(8,128)(2,1)S(1)} collective-permute-done((bf16[384,128]{1,0:T(8,128)(2,1)S(1)}, bf16[384,128]{1,0:T(8,128)(2,1)S(1)}, u32[]{:S(2)}, u32[]{:S(2)}) %collective-permute-start.10) | collective-permute-done | bytes 98336 | tf_op jit(solution)/shard_map/ppermute | solution.py:196
  176.7 1.4 pad_maximum_fusion.1
  178.4 19.3 %shard_map.74 = bf16[1,4,384,128]{3,2,1,0:T(8,128)(2,1)S(1)} custom-call(s32[52]{0:T(128)S(1)} %reshape.654.place_ref, s32[4]{0:T(128)S(1)} %pad_add_fusion.1.count_ref, bf16[1,4,384,128]{3,2,1,0:T(8,128)(2,1)S(1)} %maximum_bitcast_fusion.1.q_ref, bf16[1,16,384,128]{3,2,1,0:T(8,128)(2,1)S(1)} %get-tuple-element.54.k_ref, ...), custom_call_target="tpu_custom_call" | custom-call | flops 3925868544 | bytes 3932160 | tf_op jit(solution)/shard_map/pallas_call | solution.py:56
  197.8 2.6 collective-permute-start.20
  200.4 1.2 collective-permute-start.19
  201.6 3.6 %collective-permute-done.21 = bf16[384,128]{1,0:T(8,128)(2,1)S(1)} collective-permute-done((bf16[384,128]{1,0:T(8,128)(2,1)S(1)}, bf16[384,128]{1,0:T(8,128)(2,1)S(1)}, u32[]{:S(2)}, u32[]{:S(2)}) %collective-permute-start.21) | collective-permute-done | bytes 98336 | tf_op jit(solution)/shard_map/ppermute | solution.py:123
  205.7 2.7 collective-permute-done.20
  208.9 1.5 collective-permute-start.24
  211.4 4.3 %collective-permute-done.23 = bf16[384,128]{1,0:T(8,128)(2,1)S(1)} collective-permute-done((bf16[384,128]{1,0:T(8,128)(2,1)S(1)}, bf16[384,128]{1,0:T(8,128)(2,1)S(1)}, u32[]{:S(2)}, u32[]{:S(2)}) %collective-permute-start.23) | collective-permute-done | bytes 98336 | tf_op jit(solution)/shard_map/ppermute | solution.py:196
  216.4 19.3 %shard_map.75 = bf16[1,4,384,128]{3,2,1,0:T(8,128)(2,1)S(1)} custom-call(s32[52]{0:T(128)S(1)} %reshape.654.place_ref, s32[4]{0:T(128)S(1)} %pad_add_fusion.1.count_ref, bf16[1,4,384,128]{3,2,1,0:T(8,128)(2,1)S(1)} %maximum_bitcast_fusion.q_ref, bf16[1,16,384,128]{3,2,1,0:T(8,128)(2,1)S(1)} %get-tuple-element.56.k_ref, ...), custom_call_target="tpu_custom_call" | custom-call | flops 3925868544 | bytes 3932160 | tf_op jit(solution)/shard_map/pallas_call | solution.py:56
  235.7 1.1 collective-permute-start.33
  236.8 3.4 %collective-permute-start.32 = (bf16[384,128]{1,0:T(8,128)(2,1)S(1)}, bf16[384,128]{1,0:T(8,128)(2,1)S(1)}, u32[]{:S(2)}, u32[]{:S(2)}) collective-permute-start(bf16[384,128]{1,0:T(8,128)(2,1)S(1)} %get-tuple-element.103), channel_id=1, source_target_pairs={{0,16},{2,18},{4,20},{6,22},{8,24},{10,26},{12,28},{14,30},{16,0},... | collective-permute-start | bytes 294920 | tf_op jit(solution)/shard_map/ppermute | solution.py:123
  240.8 2.4 collective-permute-done.33
  244.1 3.3 %collective-permute-done.32 = bf16[384,128]{1,0:T(8,128)(2,1)S(1)} collective-permute-done((bf16[384,128]{1,0:T(8,128)(2,1)S(1)}, bf16[384,128]{1,0:T(8,128)(2,1)S(1)}, u32[]{:S(2)}, u32[]{:S(2)}) %collective-permute-start.32) | collective-permute-done | bytes 98336 | tf_op jit(solution)/shard_map/ppermute | solution.py:123
  248.2 1.3 collective-permute-start.35
  249.7 4.7 %collective-permute-done.35 = bf16[384,128]{1,0:T(8,128)(2,1)S(1)} collective-permute-done((bf16[384,128]{1,0:T(8,128)(2,1)S(1)}, bf16[384,128]{1,0:T(8,128)(2,1)S(1)}, u32[]{:S(2)}, u32[]{:S(2)}) %collective-permute-start.35) | collective-permute-done | bytes 98336 | tf_op jit(solution)/shard_map/ppermute | solution.py:196
  254.5 3.8 %maximum_select_fusion = bf16[1536,1536]{1,0:T(8,128)(2,1)S(1)} fusion(bf16[768,1536]{1,0:T(8,128)(2,1)S(1)} %collective-permute-done.13, bf16[768,1536]{1,0:T(8,128)(2,1)} %collective-permute-done.12, pred[]{:T(512)S(6)} %eq.111), kind=kLoop, calls=%fused_computation.4 | loop fusion | flops 21233664 | bytes 9437185 | tf_op jit(solution)/shard_map/jit(_where)/select_n | solution.py:161
  258.4 1.0 dynamic-slice_dynamic-update-slice_fusion.19
  259.4 1.0 dynamic-slice_dynamic-update-slice_fusion.18
  260.4 1.0 dynamic-slice_dynamic-update-slice_fusion.17
  261.3 1.0 dynamic-slice_dynamic-update-slice_fusion.16
  262.3 1.4 fusion.35
  263.7 3.3 %fusion.34 = f32[384,1536]{1,0:T(8,128)S(1)} fusion(bf16[384,1024]{1,0:T(8,128)(2,1)S(1)} %constant_dynamic-update-slice_fusion.8, bf16[1024,1536]{1,0:T(8,128)(2,1)} %get-tuple-element.41), kind=kOutput, calls=%fused_computation.236 | convolution fusion | flops 1207959552 | bytes 6291456 | tf_op jit(solution)/shard_map/dot_general | solution.py:202
  267.0 4.3 %fusion.1 = bf16[384,1536]{1,0:T(8,128)(2,1)} fusion(f32[384,1536]{1,0:T(8,128)S(1)} %fusion.35, f32[384,1536]{1,0:T(8,128)S(1)} %fusion.34, bf16[384,1024]{1,0:T(8,128)(2,1)S(1)} %constant_dynamic-update-slice_fusion, bf16[1024,1536]{1,0:T(8,128)(2,1)} %get-tuple-element.39), kind=kOutput, calls=%fused_computation.10 | convolution fusion | flops 1209729024 | bytes 9830400 | tf_op jit(solution)/shard_map/dot_general | solution.py:202
  (184 shorter events, 24.6 us)
Async XLA Ops:
  4.2 13.4 %copy-start.35 = (s32[16]{0:T(128)S(1)}, s32[16]{0:T(128)}, u32[]{:S(2)}) copy-start(s32[16]{0:T(128)} %param.11) | copy-start | bytes 196
  4.2 24.7 %copy-start.32 = (bf16[1,384,128]{2,1,0:T(8,128)(2,1)S(1)}, bf16[1,384,128]{2,1,0:T(8,128)(2,1)}, u32[]{:S(2)}) copy-start(bf16[1,384,128]{2,1,0:T(8,128)(2,1)} %get-tuple-element.81) | copy-start | bytes 294916
  4.2 24.7 %copy-start.33 = (bf16[1,384,128]{2,1,0:T(8,128)(2,1)S(1)}, bf16[1,384,128]{2,1,0:T(8,128)(2,1)}, u32[]{:S(2)}) copy-start(bf16[1,384,128]{2,1,0:T(8,128)(2,1)} %get-tuple-element.128) | copy-start | bytes 294916
  4.2 40.3 %collective-permute-start = (bf16[3,384,128]{2,1,0:T(8,128)(2,1)}, bf16[3,384,128]{2,1,0:T(8,128)(2,1)S(1)}, u32[]{:S(2)}, u32[]{:S(2)}) collective-permute-start(bf16[3,384,128]{2,1,0:T(8,128)(2,1)} %pad_maximum_fusion.16), channel_id=1, source_target_pairs={{0,8},{2,10},{4,12},{6,14},{8,16},{10,18},{12,20},{14,22},{16,24},... | collective-permute-start | bytes 884744 | tf_op jit(solution)/shard_map/ppermute | solution.py:123
  8.0 21.0 %copy-start.30 = (bf16[1,384,128]{2,1,0:T(8,128)(2,1)S(1)}, bf16[1,384,128]{2,1,0:T(8,128)(2,1)}, u32[]{:S(2)}) copy-start(bf16[1,384,128]{2,1,0:T(8,128)(2,1)} %get-tuple-element.82) | copy-start | bytes 294916
  8.0 21.0 %copy-start.31 = (bf16[1,384,128]{2,1,0:T(8,128)(2,1)S(1)}, bf16[1,384,128]{2,1,0:T(8,128)(2,1)}, u32[]{:S(2)}) copy-start(bf16[1,384,128]{2,1,0:T(8,128)(2,1)} %get-tuple-element.127) | copy-start | bytes 294916
  8.0 36.5 %collective-permute-start.1 = (bf16[3,384,128]{2,1,0:T(8,128)(2,1)}, bf16[3,384,128]{2,1,0:T(8,128)(2,1)}, u32[]{:S(2)}, u32[]{:S(2)}) collective-permute-start(bf16[3,384,128]{2,1,0:T(8,128)(2,1)} %pad_maximum_fusion.17), channel_id=1, source_target_pairs={{0,16},{2,18},{4,20},{6,22},{8,24},{10,26},{12,28},{14,30},{16,0},... | collective-permute-start | bytes 884744 | tf_op jit(solution)/shard_map/ppermute | solution.py:123
  11.3 18.4 %copy-start.28 = (bf16[1,384,128]{2,1,0:T(8,128)(2,1)S(1)}, bf16[1,384,128]{2,1,0:T(8,128)(2,1)}, u32[]{:S(2)}) copy-start(bf16[1,384,128]{2,1,0:T(8,128)(2,1)} %get-tuple-element.83) | copy-start | bytes 294916
  11.3 18.4 %copy-start.29 = (bf16[1,384,128]{2,1,0:T(8,128)(2,1)S(1)}, bf16[1,384,128]{2,1,0:T(8,128)(2,1)}, u32[]{:S(2)}) copy-start(bf16[1,384,128]{2,1,0:T(8,128)(2,1)} %get-tuple-element.126) | copy-start | bytes 294916
  11.3 33.1 %collective-permute-start.2 = (bf16[3,384,128]{2,1,0:T(8,128)(2,1)}, bf16[3,384,128]{2,1,0:T(8,128)(2,1)S(1)}, u32[]{:S(2)}, u32[]{:S(2)}) collective-permute-start(bf16[3,384,128]{2,1,0:T(8,128)(2,1)} %pad_maximum_fusion.18), channel_id=1, source_target_pairs={{0,24},{2,26},{4,28},{6,30},{8,0},{10,2},{12,4},{14,6},{16,8},{18,... | collective-permute-start | bytes 884744 | tf_op jit(solution)/shard_map/ppermute | solution.py:123
  12.7 17.1 %copy-start.26 = (bf16[1,384,128]{2,1,0:T(8,128)(2,1)S(1)}, bf16[1,384,128]{2,1,0:T(8,128)(2,1)}, u32[]{:S(2)}) copy-start(bf16[1,384,128]{2,1,0:T(8,128)(2,1)} %get-tuple-element.84) | copy-start | bytes 294916
  12.7 17.1 %copy-start.27 = (bf16[1,384,128]{2,1,0:T(8,128)(2,1)S(1)}, bf16[1,384,128]{2,1,0:T(8,128)(2,1)}, u32[]{:S(2)}) copy-start(bf16[1,384,128]{2,1,0:T(8,128)(2,1)} %get-tuple-element.125) | copy-start | bytes 294916
  12.7 17.9 %copy-start.24 = (bf16[1,384,128]{2,1,0:T(8,128)(2,1)S(1)}, bf16[1,384,128]{2,1,0:T(8,128)(2,1)}, u32[]{:S(2)}) copy-start(bf16[1,384,128]{2,1,0:T(8,128)(2,1)} %get-tuple-element.85) | copy-start | bytes 294916
  12.7 17.9 %copy-start.25 = (bf16[1,384,128]{2,1,0:T(8,128)(2,1)S(1)}, bf16[1,384,128]{2,1,0:T(8,128)(2,1)}, u32[]{:S(2)}) copy-start(bf16[1,384,128]{2,1,0:T(8,128)(2,1)} %get-tuple-element.124) | copy-start | bytes 294916
  12.7 18.7 %copy-start.22 = (bf16[1,384,128]{2,1,0:T(8,128)(2,1)S(1)}, bf16[1,384,128]{2,1,0:T(8,128)(2,1)}, u32[]{:S(2)}) copy-start(bf16[1,384,128]{2,1,0:T(8,128)(2,1)} %get-tuple-element.86) | copy-start | bytes 294916
  12.7 18.6 %copy-start.23 = (bf16[1,384,128]{2,1,0:T(8,128)(2,1)S(1)}, bf16[1,384,128]{2,1,0:T(8,128)(2,1)}, u32[]{:S(2)}) copy-start(bf16[1,384,128]{2,1,0:T(8,128)(2,1)} %get-tuple-element.123) | copy-start | bytes 294916
  12.7 19.4 %copy-start.20 = (bf16[1,384,128]{2,1,0:T(8,128)(2,1)S(1)}, bf16[1,384,128]{2,1,0:T(8,128)(2,1)}, u32[]{:S(2)}) copy-start(bf16[1,384,128]{2,1,0:T(8,128)(2,1)} %get-tuple-element.87) | copy-start | bytes 294916
  12.7 19.4 %copy-start.21 = (bf16[1,384,128]{2,1,0:T(8,128)(2,1)S(1)}, bf16[1,384,128]{2,1,0:T(8,128)(2,1)}, u32[]{:S(2)}) copy-start(bf16[1,384,128]{2,1,0:T(8,128)(2,1)} %get-tuple-element.122) | copy-start | bytes 294916
  16.0 16.1 %copy-start.19 = (bf16[1,384,128]{2,1,0:T(8,128)(2,1)S(1)}, bf16[1,384,128]{2,1,0:T(8,128)(2,1)}, u32[]{:S(2)}) copy-start(bf16[1,384,128]{2,1,0:T(8,128)(2,1)} %get-tuple-element.118) | copy-start | bytes 294916
  16.0 110.9 %collective-permute-start.12 = (bf16[768,1536]{1,0:T(8,128)(2,1)}, bf16[768,1536]{1,0:T(8,128)(2,1)}, u32[]{:S(2)}, u32[]{:S(2)}) collective-permute-start(bf16[768,1536]{1,0:T(8,128)(2,1)} %dynamic_slice.232), channel_id=1, source_target_pairs={{0,1},{1,0},{2,3},{3,2},{4,5},{5,4},{6,7},{7,6},{8,9},{9,8},{10,11... | collective-permute-start | bytes 7077896 | tf_op jit(solution)/shard_map/ppermute | solution.py:159
  29.8 73.8 %copy-start.3 = (bf16[3,384,128]{2,1,0:T(8,128)(2,1)}, bf16[3,384,128]{2,1,0:T(8,128)(2,1)S(1)}, u32[]{:S(2)}) copy-start(bf16[3,384,128]{2,1,0:T(8,128)(2,1)S(1)} %pad_maximum_fusion.23) | copy-start | bytes 884740
  32.2 56.4 %copy-start.5 = (bf16[3,384,128]{2,1,0:T(8,128)(2,1)}, bf16[3,384,128]{2,1,0:T(8,128)(2,1)S(1)}, u32[]{:S(2)}) copy-start(bf16[3,384,128]{2,1,0:T(8,128)(2,1)S(1)} %pad_maximum_fusion.19) | copy-start | bytes 884740
  38.6 9.3 %copy-start = (s32[4]{0:T(128)S(1)}, s32[4]{0:T(128)}, u32[]{:S(2)}) copy-start(s32[4]{0:T(128)} %constant.361.clone) | copy-start | bytes 52
  41.5 12.3 %copy-start.36 = (s32[13]{0:T(128)S(1)}, s32[13]{0:T(128)}, u32[]{:S(2)}) copy-start(s32[13]{0:T(128)} %fusion.25) | copy-start | bytes 160
  46.3 40.8 %collective-permute-start.3 = (bf16[2,4,384,128]{3,2,1,0:T(8,128)(2,1)S(1)}, bf16[2,4,384,128]{3,2,1,0:T(8,128)(2,1)S(1)}, u32[]{:S(2)}, u32[]{:S(2)}) collective-permute-start(bf16[2,4,384,128]{3,2,1,0:T(8,128)(2,1)S(1)} %fusion.4), channel_id=1, source_target_pairs={{0,4},{2,6},{4,0},{6,2},{8,12},{10,14},{12,8},{14,10},{16,20},{18,... | collective-permute-start | bytes 2359304 | tf_op jit(solution)/shard_map/ppermute | solution.py:128
  49.9 12.1 %collective-permute-start.14 = (bf16[3,384,128]{2,1,0:T(8,128)(2,1)}, bf16[3,384,128]{2,1,0:T(8,128)(2,1)S(1)}, u32[]{:S(2)}, u32[]{:S(2)}) collective-permute-start(bf16[3,384,128]{2,1,0:T(8,128)(2,1)} %pad_maximum_fusion.20), channel_id=1, source_target_pairs={{0,8},{2,10},{4,12},{6,14},{8,16},{10,18},{12,20},{14,22},{16,24},... | collective-permute-start | bytes 884744 | tf_op jit(solution)/shard_map/ppermute | solution.py:123
  50.7 21.5 %collective-permute-start.15 = (bf16[3,384,128]{2,1,0:T(8,128)(2,1)}, bf16[3,384,128]{2,1,0:T(8,128)(2,1)S(1)}, u32[]{:S(2)}, u32[]{:S(2)}) collective-permute-start(bf16[3,384,128]{2,1,0:T(8,128)(2,1)} %pad_maximum_fusion.21), channel_id=1, source_target_pairs={{0,16},{2,18},{4,20},{6,22},{8,24},{10,26},{12,28},{14,30},{16,0},... | collective-permute-start | bytes 884744 | tf_op jit(solution)/shard_map/ppermute | solution.py:123
  51.0 21.2 %collective-permute-start.16 = (bf16[3,384,128]{2,1,0:T(8,128)(2,1)}, bf16[3,384,128]{2,1,0:T(8,128)(2,1)S(1)}, u32[]{:S(2)}, u32[]{:S(2)}) collective-permute-start(bf16[3,384,128]{2,1,0:T(8,128)(2,1)} %pad_maximum_fusion.22), channel_id=1, source_target_pairs={{0,24},{2,26},{4,28},{6,30},{8,0},{10,2},{12,4},{14,6},{16,8},{18,... | collective-permute-start | bytes 884744 | tf_op jit(solution)/shard_map/ppermute | solution.py:123
  62.0 26.5 %copy-start.10 = (bf16[3,384,128]{2,1,0:T(8,128)(2,1)}, bf16[3,384,128]{2,1,0:T(8,128)(2,1)S(1)}, u32[]{:S(2)}) copy-start(bf16[3,384,128]{2,1,0:T(8,128)(2,1)S(1)} %collective-permute-done.14) | copy-start | bytes 884740
  72.2 16.4 %copy-start.11 = (bf16[3,384,128]{2,1,0:T(8,128)(2,1)}, bf16[3,384,128]{2,1,0:T(8,128)(2,1)S(1)}, u32[]{:S(2)}) copy-start(bf16[3,384,128]{2,1,0:T(8,128)(2,1)S(1)} %collective-permute-done.15) | copy-start | bytes 884740
  72.2 16.4 %copy-start.12 = (bf16[3,384,128]{2,1,0:T(8,128)(2,1)}, bf16[3,384,128]{2,1,0:T(8,128)(2,1)S(1)}, u32[]{:S(2)}) copy-start(bf16[3,384,128]{2,1,0:T(8,128)(2,1)S(1)} %collective-permute-done.16) | copy-start | bytes 884740
  72.2 20.3 %collective-permute-start.26 = (bf16[3,384,128]{2,1,0:T(8,128)(2,1)}, bf16[3,384,128]{2,1,0:T(8,128)(2,1)S(1)}, u32[]{:S(2)}, u32[]{:S(2)}) collective-permute-start(bf16[3,384,128]{2,1,0:T(8,128)(2,1)} %pad_maximum_fusion.24), channel_id=1, source_target_pairs={{0,8},{2,10},{4,12},{6,14},{8,16},{10,18},{12,20},{14,22},{16,24},... | collective-permute-start | bytes 884744 | tf_op jit(solution)/shard_map/ppermute | solution.py:123
  84.7 15.3 %collective-permute-start.27 = (bf16[3,384,128]{2,1,0:T(8,128)(2,1)}, bf16[3,384,128]{2,1,0:T(8,128)(2,1)S(1)}, u32[]{:S(2)}, u32[]{:S(2)}) collective-permute-start(bf16[3,384,128]{2,1,0:T(8,128)(2,1)} %pad_maximum_fusion.25), channel_id=1, source_target_pairs={{0,16},{2,18},{4,20},{6,22},{8,24},{10,26},{12,28},{14,30},{16,0},... | collective-permute-start | bytes 884744 | tf_op jit(solution)/shard_map/ppermute | solution.py:123
  84.7 18.9 %collective-permute-start.28 = (bf16[3,384,128]{2,1,0:T(8,128)(2,1)}, bf16[3,384,128]{2,1,0:T(8,128)(2,1)S(1)}, u32[]{:S(2)}, u32[]{:S(2)}) collective-permute-start(bf16[3,384,128]{2,1,0:T(8,128)(2,1)} %pad_maximum_fusion.26), channel_id=1, source_target_pairs={{0,24},{2,26},{4,28},{6,30},{8,0},{10,2},{12,4},{14,6},{16,8},{18,... | collective-permute-start | bytes 884744 | tf_op jit(solution)/shard_map/ppermute | solution.py:123
  87.1 16.5 %copy-start.1 = (bf16[2,4,384,128]{3,2,1,0:T(8,128)(2,1)}, bf16[2,4,384,128]{3,2,1,0:T(8,128)(2,1)S(1)}, u32[]{:S(2)}) copy-start(bf16[2,4,384,128]{3,2,1,0:T(8,128)(2,1)S(1)} %collective-permute-done.3) | copy-start | bytes 2359300
  88.5 38.9 %collective-permute-start.4 = (bf16[2,8,384,128]{3,2,1,0:T(8,128)(2,1)}, bf16[2,8,384,128]{3,2,1,0:T(8,128)(2,1)}, u32[]{:S(2)}, u32[]{:S(2)}) collective-permute-start(bf16[2,8,384,128]{3,2,1,0:T(8,128)(2,1)} %pad_maximum_fusion.3), channel_id=1, source_target_pairs={{0,2},{2,0},{4,6},{6,4},{8,10},{10,8},{12,14},{14,12},{16,18},{18,... | collective-permute-start | bytes 4718600 | tf_op jit(solution)/shard_map/ppermute | solution.py:128
  92.5 11.8 %copy-start.13 = (bf16[3,384,128]{2,1,0:T(8,128)(2,1)}, bf16[3,384,128]{2,1,0:T(8,128)(2,1)S(1)}, u32[]{:S(2)}) copy-start(bf16[3,384,128]{2,1,0:T(8,128)(2,1)S(1)} %collective-permute-done.26) | copy-start | bytes 884740
  92.5 20.6 %collective-permute-start.17 = (bf16[2,4,384,128]{3,2,1,0:T(8,128)(2,1)S(1)}, bf16[2,4,384,128]{3,2,1,0:T(8,128)(2,1)}, u32[]{:S(2)}, u32[]{:S(2)}) collective-permute-start(bf16[2,4,384,128]{3,2,1,0:T(8,128)(2,1)S(1)} %fusion.3), channel_id=1, source_target_pairs={{0,4},{2,6},{4,0},{6,2},{8,12},{10,14},{12,8},{14,10},{16,20},{18,... | collective-permute-start | bytes 2359304 | tf_op jit(solution)/shard_map/ppermute | solution.py:128
  103.7 23.0 %collective-permute-start.29 = (bf16[2,4,384,128]{3,2,1,0:T(8,128)(2,1)S(1)}, bf16[2,4,384,128]{3,2,1,0:T(8,128)(2,1)S(1)}, u32[]{:S(2)}, u32[]{:S(2)}) collective-permute-start(bf16[2,4,384,128]{3,2,1,0:T(8,128)(2,1)S(1)} %fusion.2), channel_id=1, source_target_pairs={{0,4},{2,6},{4,0},{6,2},{8,12},{10,14},{12,8},{14,10},{16,20},{18,... | collective-permute-start | bytes 2359304 | tf_op jit(solution)/shard_map/ppermute | solution.py:128
  111.3 16.1 %copy-start.2 = (bf16[2,4,384,128]{3,2,1,0:T(8,128)(2,1)S(1)}, bf16[2,4,384,128]{3,2,1,0:T(8,128)(2,1)}, u32[]{:S(2)}) copy-start(bf16[2,4,384,128]{3,2,1,0:T(8,128)(2,1)} %copy-done.1) | copy-start | bytes 2359300
  114.4 62.3 %collective-permute-start.18 = (bf16[2,8,384,128]{3,2,1,0:T(8,128)(2,1)S(1)}, bf16[2,8,384,128]{3,2,1,0:T(8,128)(2,1)S(1)}, u32[]{:S(2)}, u32[]{:S(2)}) collective-permute-start(bf16[2,8,384,128]{3,2,1,0:T(8,128)(2,1)S(1)} %pad_maximum_fusion.4), channel_id=1, source_target_pairs={{0,2},{2,0},{4,6},{6,4},{8,10},{10,8},{12,14},{14,12},{16,18},{18,... | collective-permute-start | bytes 4718600 | tf_op jit(solution)/shard_map/ppermute | solution.py:128
  126.8 89.0 %collective-permute-start.30 = (bf16[2,8,384,128]{3,2,1,0:T(8,128)(2,1)S(1)}, bf16[2,8,384,128]{3,2,1,0:T(8,128)(2,1)S(1)}, u32[]{:S(2)}, u32[]{:S(2)}) collective-permute-start(bf16[2,8,384,128]{3,2,1,0:T(8,128)(2,1)S(1)} %pad_maximum_fusion.5), channel_id=1, source_target_pairs={{0,2},{2,0},{4,6},{6,4},{8,10},{10,8},{12,14},{14,12},{16,18},{18,... | collective-permute-start | bytes 4718600 | tf_op jit(solution)/shard_map/ppermute | solution.py:128
  126.9 127.6 %collective-permute-start.13 = (bf16[768,1536]{1,0:T(8,128)(2,1)}, bf16[768,1536]{1,0:T(8,128)(2,1)S(1)}, u32[]{:S(2)}, u32[]{:S(2)}) collective-permute-start(bf16[768,1536]{1,0:T(8,128)(2,1)} %collective-permute-done.12), channel_id=1, source_target_pairs={{0,2},{2,0},{4,6},{6,4},{8,10},{10,8},{12,14},{14,12},{16,18},{18,... | collective-permute-start | bytes 7077896 | tf_op jit(solution)/shard_map/ppermute | solution.py:128
  148.7 7.2 %collective-permute-start.5 = (bf16[384,128]{1,0:T(8,128)(2,1)S(1)}, bf16[384,128]{1,0:T(8,128)(2,1)S(1)}, u32[]{:S(2)}, u32[]{:S(2)}) collective-permute-start(bf16[384,128]{1,0:T(8,128)(2,1)S(1)} %get-tuple-element.96), channel_id=1, source_target_pairs={{0,24},{2,26},{4,28},{6,30},{8,0},{10,2},{12,4},{14,6},{16,8},{18,... | collective-permute-start | bytes 294920 | tf_op jit(solution)/shard_map/ppermute | solution.py:123
  153.4 7.1 %collective-permute-start.7 = (bf16[384,128]{1,0:T(8,128)(2,1)S(1)}, bf16[384,128]{1,0:T(8,128)(2,1)S(1)}, u32[]{:S(2)}, u32[]{:S(2)}) collective-permute-start(bf16[384,128]{1,0:T(8,128)(2,1)S(1)} %get-tuple-element.94), channel_id=1, source_target_pairs={{0,8},{2,10},{4,12},{6,14},{8,16},{10,18},{12,20},{14,22},{16,24},... | collective-permute-start | bytes 294920 | tf_op jit(solution)/shard_map/ppermute | solution.py:123
  155.8 9.3 %collective-permute-start.6 = (bf16[384,128]{1,0:T(8,128)(2,1)S(1)}, bf16[384,128]{1,0:T(8,128)(2,1)S(1)}, u32[]{:S(2)}, u32[]{:S(2)}) collective-permute-start(bf16[384,128]{1,0:T(8,128)(2,1)S(1)} %get-tuple-element.95), channel_id=1, source_target_pairs={{0,16},{2,18},{4,20},{6,22},{8,24},{10,26},{12,28},{14,30},{16,0},... | collective-permute-start | bytes 294920 | tf_op jit(solution)/shard_map/ppermute | solution.py:123
  160.5 5.1 %collective-permute-start.8 = (bf16[384,128]{1,0:T(8,128)(2,1)S(1)}, bf16[384,128]{1,0:T(8,128)(2,1)S(1)}, u32[]{:S(2)}, u32[]{:S(2)}) collective-permute-start(bf16[384,128]{1,0:T(8,128)(2,1)S(1)} %get-tuple-element.93), channel_id=1, source_target_pairs={{0,1},{1,0},{2,3},{3,2},{4,5},{5,4},{6,7},{7,6},{8,9},{9,8},{10,11... | collective-permute-start | bytes 294920 | tf_op jit(solution)/shard_map/ppermute | solution.py:196
  165.1 11.6 %collective-permute-start.11 = (bf16[384,128]{1,0:T(8,128)(2,1)S(1)}, bf16[384,128]{1,0:T(8,128)(2,1)S(1)}, u32[]{:S(2)}, u32[]{:S(2)}) collective-permute-start(bf16[384,128]{1,0:T(8,128)(2,1)S(1)} %collective-permute-done.7), channel_id=1, source_target_pairs={{0,1},{1,0},{2,3},{3,2},{4,5},{5,4},{6,7},{7,6},{8,9},{9,8},{10,11... | collective-permute-start | bytes 294920 | tf_op jit(solution)/shard_map/ppermute | solution.py:196
  165.6 6.4 %collective-permute-start.9 = (bf16[384,128]{1,0:T(8,128)(2,1)S(1)}, bf16[384,128]{1,0:T(8,128)(2,1)S(1)}, u32[]{:S(2)}, u32[]{:S(2)}) collective-permute-start(bf16[384,128]{1,0:T(8,128)(2,1)S(1)} %collective-permute-done.5), channel_id=1, source_target_pairs={{0,1},{1,0},{2,3},{3,2},{4,5},{5,4},{6,7},{7,6},{8,9},{9,8},{10,11... | collective-permute-start | bytes 294920 | tf_op jit(solution)/shard_map/ppermute | solution.py:196
  172.0 4.6 %collective-permute-start.10 = (bf16[384,128]{1,0:T(8,128)(2,1)S(1)}, bf16[384,128]{1,0:T(8,128)(2,1)S(1)}, u32[]{:S(2)}, u32[]{:S(2)}) collective-permute-start(bf16[384,128]{1,0:T(8,128)(2,1)S(1)} %collective-permute-done.6), channel_id=1, source_target_pairs={{0,1},{1,0},{2,3},{3,2},{4,5},{5,4},{6,7},{7,6},{8,9},{9,8},{10,11... | collective-permute-start | bytes 294920 | tf_op jit(solution)/shard_map/ppermute | solution.py:196
  197.7 7.5 %collective-permute-start.21 = (bf16[384,128]{1,0:T(8,128)(2,1)S(1)}, bf16[384,128]{1,0:T(8,128)(2,1)S(1)}, u32[]{:S(2)}, u32[]{:S(2)}) collective-permute-start(bf16[384,128]{1,0:T(8,128)(2,1)S(1)} %get-tuple-element.98), channel_id=1, source_target_pairs={{0,8},{2,10},{4,12},{6,14},{8,16},{10,18},{12,20},{14,22},{16,24},... | collective-permute-start | bytes 294920 | tf_op jit(solution)/shard_map/ppermute | solution.py:123
  197.8 10.6 %collective-permute-start.20 = (bf16[384,128]{1,0:T(8,128)(2,1)S(1)}, bf16[384,128]{1,0:T(8,128)(2,1)S(1)}, u32[]{:S(2)}, u32[]{:S(2)}) collective-permute-start(bf16[384,128]{1,0:T(8,128)(2,1)S(1)} %get-tuple-element.99), channel_id=1, source_target_pairs={{0,16},{2,18},{4,20},{6,22},{8,24},{10,26},{12,28},{14,30},{16,0},... | collective-permute-start | bytes 294920 | tf_op jit(solution)/shard_map/ppermute | solution.py:123
  200.4 8.5 %collective-permute-start.19 = (bf16[384,128]{1,0:T(8,128)(2,1)S(1)}, bf16[384,128]{1,0:T(8,128)(2,1)S(1)}, u32[]{:S(2)}, u32[]{:S(2)}) collective-permute-start(bf16[384,128]{1,0:T(8,128)(2,1)S(1)} %get-tuple-element.100), channel_id=1, source_target_pairs={{0,24},{2,26},{4,28},{6,30},{8,0},{10,2},{12,4},{14,6},{16,8},{18,... | collective-permute-start | bytes 294920 | tf_op jit(solution)/shard_map/ppermute | solution.py:123
  205.3 5.6 %collective-permute-start.22 = (bf16[384,128]{1,0:T(8,128)(2,1)S(1)}, bf16[384,128]{1,0:T(8,128)(2,1)S(1)}, u32[]{:S(2)}, u32[]{:S(2)}) collective-permute-start(bf16[384,128]{1,0:T(8,128)(2,1)S(1)} %get-tuple-element.97), channel_id=1, source_target_pairs={{0,1},{1,0},{2,3},{3,2},{4,5},{5,4},{6,7},{7,6},{8,9},{9,8},{10,11... | collective-permute-start | bytes 294920 | tf_op jit(solution)/shard_map/ppermute | solution.py:196
  208.4 7.4 %collective-permute-start.25 = (bf16[384,128]{1,0:T(8,128)(2,1)S(1)}, bf16[384,128]{1,0:T(8,128)(2,1)S(1)}, u32[]{:S(2)}, u32[]{:S(2)}) collective-permute-start(bf16[384,128]{1,0:T(8,128)(2,1)S(1)} %collective-permute-done.21), channel_id=1, source_target_pairs={{0,1},{1,0},{2,3},{3,2},{4,5},{5,4},{6,7},{7,6},{8,9},{9,8},{10,11... | collective-permute-start | bytes 294920 | tf_op jit(solution)/shard_map/ppermute | solution.py:196
  208.9 6.8 %collective-permute-start.24 = (bf16[384,128]{1,0:T(8,128)(2,1)S(1)}, bf16[384,128]{1,0:T(8,128)(2,1)S(1)}, u32[]{:S(2)}, u32[]{:S(2)}) collective-permute-start(bf16[384,128]{1,0:T(8,128)(2,1)S(1)} %collective-permute-done.20), channel_id=1, source_target_pairs={{0,1},{1,0},{2,3},{3,2},{4,5},{5,4},{6,7},{7,6},{8,9},{9,8},{10,11... | collective-permute-start | bytes 294920 | tf_op jit(solution)/shard_map/ppermute | solution.py:196
  210.8 4.9 %collective-permute-start.23 = (bf16[384,128]{1,0:T(8,128)(2,1)S(1)}, bf16[384,128]{1,0:T(8,128)(2,1)S(1)}, u32[]{:S(2)}, u32[]{:S(2)}) collective-permute-start(bf16[384,128]{1,0:T(8,128)(2,1)S(1)} %collective-permute-done.19), channel_id=1, source_target_pairs={{0,1},{1,0},{2,3},{3,2},{4,5},{5,4},{6,7},{7,6},{8,9},{9,8},{10,11... | collective-permute-start | bytes 294920 | tf_op jit(solution)/shard_map/ppermute | solution.py:196
  235.7 7.5 %collective-permute-start.33 = (bf16[384,128]{1,0:T(8,128)(2,1)S(1)}, bf16[384,128]{1,0:T(8,128)(2,1)S(1)}, u32[]{:S(2)}, u32[]{:S(2)}) collective-permute-start(bf16[384,128]{1,0:T(8,128)(2,1)S(1)} %get-tuple-element.102), channel_id=1, source_target_pairs={{0,8},{2,10},{4,12},{6,14},{8,16},{10,18},{12,20},{14,22},{16,24},... | collective-permute-start | bytes 294920 | tf_op jit(solution)/shard_map/ppermute | solution.py:123
  236.8 10.7 %collective-permute-start.32 = (bf16[384,128]{1,0:T(8,128)(2,1)S(1)}, bf16[384,128]{1,0:T(8,128)(2,1)S(1)}, u32[]{:S(2)}, u32[]{:S(2)}) collective-permute-start(bf16[384,128]{1,0:T(8,128)(2,1)S(1)} %get-tuple-element.103), channel_id=1, source_target_pairs={{0,16},{2,18},{4,20},{6,22},{8,24},{10,26},{12,28},{14,30},{16,0},... | collective-permute-start | bytes 294920 | tf_op jit(solution)/shard_map/ppermute | solution.py:123
  240.2 8.0 %collective-permute-start.31 = (bf16[384,128]{1,0:T(8,128)(2,1)S(1)}, bf16[384,128]{1,0:T(8,128)(2,1)S(1)}, u32[]{:S(2)}, u32[]{:S(2)}) collective-permute-start(bf16[384,128]{1,0:T(8,128)(2,1)S(1)} %get-tuple-element.104), channel_id=1, source_target_pairs={{0,24},{2,26},{4,28},{6,30},{8,0},{10,2},{12,4},{14,6},{16,8},{18,... | collective-permute-start | bytes 294920 | tf_op jit(solution)/shard_map/ppermute | solution.py:123
  240.2 9.4 %collective-permute-start.34 = (bf16[384,128]{1,0:T(8,128)(2,1)S(1)}, bf16[384,128]{1,0:T(8,128)(2,1)S(1)}, u32[]{:S(2)}, u32[]{:S(2)}) collective-permute-start(bf16[384,128]{1,0:T(8,128)(2,1)S(1)} %get-tuple-element.101), channel_id=1, source_target_pairs={{0,1},{1,0},{2,3},{3,2},{4,5},{5,4},{6,7},{7,6},{8,9},{9,8},{10,11... | collective-permute-start | bytes 294920 | tf_op jit(solution)/shard_map/ppermute | solution.py:196
  243.2 11.2 %collective-permute-start.37 = (bf16[384,128]{1,0:T(8,128)(2,1)S(1)}, bf16[384,128]{1,0:T(8,128)(2,1)S(1)}, u32[]{:S(2)}, u32[]{:S(2)}) collective-permute-start(bf16[384,128]{1,0:T(8,128)(2,1)S(1)} %collective-permute-done.33), channel_id=1, source_target_pairs={{0,1},{1,0},{2,3},{3,2},{4,5},{5,4},{6,7},{7,6},{8,9},{9,8},{10,11... | collective-permute-start | bytes 294920 | tf_op jit(solution)/shard_map/ppermute | solution.py:196
  247.5 6.9 %collective-permute-start.36 = (bf16[384,128]{1,0:T(8,128)(2,1)S(1)}, bf16[384,128]{1,0:T(8,128)(2,1)S(1)}, u32[]{:S(2)}, u32[]{:S(2)}) collective-permute-start(bf16[384,128]{1,0:T(8,128)(2,1)S(1)} %collective-permute-done.32), channel_id=1, source_target_pairs={{0,1},{1,0},{2,3},{3,2},{4,5},{5,4},{6,7},{7,6},{8,9},{9,8},{10,11... | collective-permute-start | bytes 294920 | tf_op jit(solution)/shard_map/ppermute | solution.py:196
  248.2 6.2 %collective-permute-start.35 = (bf16[384,128]{1,0:T(8,128)(2,1)S(1)}, bf16[384,128]{1,0:T(8,128)(2,1)S(1)}, u32[]{:S(2)}, u32[]{:S(2)}) collective-permute-start(bf16[384,128]{1,0:T(8,128)(2,1)S(1)} %collective-permute-done.31), channel_id=1, source_target_pairs={{0,1},{1,0},{2,3},{3,2},{4,5},{5,4},{6,7},{7,6},{8,9},{9,8},{10,11... | collective-permute-start | bytes 294920 | tf_op jit(solution)/shard_map/ppermute | solution.py:196
  (13 other events, 49.7 us)

commit v2 on v1

v2 whole, which is shorter than its diff:
```python
import functools
import math

import jax
import jax.numpy as jnp
from jax import lax
from jax.experimental import pallas as pl
from jax.experimental.pallas import tpu as pltpu
from jax.sharding import PartitionSpec as P

HEAD_DIM = 128
REACH = 6
MESH = pl.DeviceIdType.MESH


def attention_body(width, place_ref, count_ref, q_ref, k_ref, v_ref, out_ref, scores, tops, summed):
    row = pl.program_id(0)
    count = count_ref[row]
    heads = q_ref.shape[0]
    scale = math.log2(math.e) / math.sqrt(HEAD_DIM)
    tops[...] = jnp.full(tops.shape, -jnp.inf, jnp.float32)
    summed[...] = jnp.zeros(summed.shape, jnp.float32)
    ones = jnp.ones((k_ref.shape[2], HEAD_DIM), jnp.bfloat16)

    def find(entry, carry):
        place = place_ref[row * width + entry]
        for h in range(heads):
            fresh = lax.dot_general(
                q_ref[h, 0],
                k_ref[h, place],
                (((1,), (1,)), ((), ())),
                preferred_element_type=jnp.float32,
            )
            scores[h, entry] = fresh
            best = tops[h]
            for lane in range(0, fresh.shape[1], HEAD_DIM):
                best = jnp.maximum(best, fresh[:, lane : lane + HEAD_DIM])
            tops[h] = best
        return carry

    lax.fori_loop(0, count, find, 0)
    for h in range(heads):
        top = jnp.max(tops[h], axis=1, keepdims=True) * scale
        tops[h] = jnp.broadcast_to(top, tops.shape[1:])

    def add(entry, carry):
        place = place_ref[row * width + entry]
        for h in range(heads):
            weights = jnp.exp2(scores[h, entry] * scale - tops[h][:, :1]).astype(jnp.bfloat16)
            paired = jnp.concatenate([v_ref[h, place], ones], axis=1)
            summed[h] += jnp.dot(weights, paired, preferred_element_type=jnp.float32)
        return carry

    lax.fori_loop(0, count, add, 0)
    for h in range(heads):
        done = summed[h]
        out_ref[0, :, h * HEAD_DIM : (h + 1) * HEAD_DIM] = (
            done[:, :HEAD_DIM] / done[:, HEAD_DIM:]
        ).astype(jnp.bfloat16)


def attention(q, k, v, place, count, first, tiles):
    heads, _, rows, _ = q.shape
    key_tiles = k.shape[1]
    width = place.shape[1]
    units = heads * tiles * min(width, key_tiles)
    key_spec = pl.BlockSpec(
        (heads, key_tiles, rows, HEAD_DIM), lambda t, *_: (0, 0, 0, 0), pipeline_mode=pl.Buffered(1)
    )
    return pl.pallas_call(
        functools.partial(attention_body, width),
        out_shape=jax.ShapeDtypeStruct((tiles, rows, heads * HEAD_DIM), jnp.bfloat16),
        grid_spec=pltpu.PrefetchScalarGridSpec(
            num_scalar_prefetch=2,
            grid=(tiles,),
            in_specs=[
                pl.BlockSpec((heads, 1, rows, HEAD_DIM), lambda t, *_: (0, first + t, 0, 0)),
                key_spec,
                key_spec,
            ],
            out_specs=pl.BlockSpec((1, rows, heads * HEAD_DIM), lambda t, *_: (t, 0, 0)),
            scratch_shapes=[
                pltpu.VMEM((heads, width, rows, rows), jnp.float32),
                pltpu.VMEM((heads, rows, HEAD_DIM), jnp.float32),
                pltpu.VMEM((heads, rows, 2 * HEAD_DIM), jnp.float32),
            ],
        ),
        compiler_params=pltpu.CompilerParams(vmem_limit_bytes=52 * 1024 * 1024),
        cost_estimate=pl.CostEstimate(
            flops=units * rows * rows * HEAD_DIM * 4,
            bytes_accessed=2 * (2 * q.size + k.size + v.size),
            transcendentals=units * rows * rows,
        ),
    )(place[first : first + tiles].reshape(-1), count[first : first + tiles], q, k, v)


def listed_slots(kv_tiles, tile_order, slot):
    listed = kv_tiles[tile_order[slot]]
    slot_ids = jnp.arange(tile_order.shape[0], dtype=jnp.int32)
    found = jnp.sum(
        jnp.where(tile_order[None, :] == jnp.maximum(listed, 0)[:, None], slot_ids[None, :], 0), axis=1
    )
    return found, jnp.sum((listed >= 0).astype(jnp.int32))


def by_ring(queries, keys, values, kv_tiles, tile_order, out_weight):
    rows, local_width = queries.shape
    heads = local_width // HEAD_DIM
    n = lax.axis_size("seq")
    me = lax.axis_index("seq")
    window = 2 * REACH + 1
    pair = jnp.stack([keys, values])
    received = {0: pair}
    for heading in (1, -1):
        moving = pair
        for stride in range(1, REACH + 1):
            moving = lax.ppermute(moving, "seq", [(i, (i + heading) % n) for i in range(n)])
            received[-heading * stride] = moving
    both = jnp.stack([received[o] for o in range(-REACH, REACH + 1)])
    both = both.reshape(window, 2, rows, heads, HEAD_DIM).transpose(1, 3, 0, 2, 4)
    q = queries.reshape(rows, heads, HEAD_DIM).transpose(1, 0, 2)[:, None]
    slots, count = listed_slots(kv_tiles, tile_order, me)
    place = (slots - me + REACH) % n
    place = jnp.clip(place, 0, window - 1)
    attended = attention(q, both[0], both[1], place[None], count[None], 0, 1)[0]
    partial = jnp.dot(attended, out_weight, preferred_element_type=jnp.float32).astype(jnp.bfloat16)
    return lax.psum_scatter(partial, "head", scatter_dimension=1, tiled=True)


def exchange_body(
    groups, share, bits, q_ref, k_ref, v_ref, w_ref, q_out, k_out, v_out, w_out,
    local_sem, plane_send, plane_recv, swap_send, swap_recv, w_send, w_recv,
):
    sub = lax.axis_size("seq") // groups
    me = lax.axis_index("seq")
    plane, inner = me // sub, me % sub
    other = 1 - lax.axis_index("head")

    def across(o):
        return {"seq": (plane + o) % groups * sub + inner}

    def swapped(bit):
        return {"seq": plane * sub + inner + bit * (1 - 2 * (inner // bit % 2))}

    partners = [across(o) for o in range(1, groups)] + [swapped(b) for b in bits] + [{"head": other}]
    barrier = pltpu.get_barrier_semaphore()
    for partner in partners:
        pl.semaphore_signal(barrier, inc=1, device_id=partner, device_id_type=MESH)
    pl.semaphore_wait(barrier, len(partners))

    half = w_ref.shape[0] // 2
    columns = w_out.shape[1]
    own_rows = pl.ds(pl.multiple_of(me % 2 * half, half), half)
    w_cross = pltpu.make_async_remote_copy(
        src_ref=w_ref.at[own_rows, pl.ds(pl.multiple_of(other * columns, columns), columns)],
        dst_ref=w_out.at[own_rows],
        send_sem=w_send.at[0],
        recv_sem=w_recv.at[0],
        device_id={"head": other},
        device_id_type=MESH,
    )
    w_cross.start()
    arrays = ((k_ref, k_out), (v_ref, v_out), (q_ref, q_out))

    def cut(ref, to_plane, j):
        start = (to_plane * share + j) * HEAD_DIM
        return ref.at[:, pl.ds(pl.multiple_of(start, HEAD_DIM), HEAD_DIM)]

    local, crossing = {}, {}
    for j in range(share):
        for a, (src, dst) in enumerate(arrays):
            for o in range(1, groups):
                crossing[j, o, a] = pltpu.make_async_remote_copy(
                    src_ref=cut(src, (plane + o) % groups, j),
                    dst_ref=dst.at[j, o],
                    send_sem=plane_send.at[j, o, a],
                    recv_sem=plane_recv.at[j, o, a],
                    device_id=across(o),
                    device_id_type=MESH,
                )
                crossing[j, o, a].start()
            local[j, a] = pltpu.make_async_copy(cut(src, plane, j), dst.at[j, 0], local_sem.at[j, a])
            local[j, a].start()

    swaps = {}

    def start_swap(j, stage):
        held = groups << stage
        for a in range(2):
            out = arrays[a][1]
            swaps[j, stage, a] = pltpu.make_async_remote_copy(
                src_ref=out.at[j, pl.ds(0, held)],
                dst_ref=out.at[j, pl.ds(held, held)],
                send_sem=swap_send.at[j, stage, a],
                recv_sem=swap_recv.at[j, stage, a],
                device_id=swapped(bits[stage]),
                device_id_type=MESH,
            )
            swaps[j, stage, a].start()

    for step in range(share + len(bits)):
        for stage in range(min(step, len(bits)), -1, -1):
            j = step - stage
            if not 0 <= j < share:
                continue
            for a in range(2):
                if stage == 0:
                    local[j, a].wait()
                    for o in range(1, groups):
                        crossing[j, o, a].wait_recv()
                else:
                    swaps[j, stage - 1, a].wait_recv()
            if stage < len(bits):
                start_swap(j, stage)
        if step == share - 1:
            w_cross.wait_recv()
            w_on = pltpu.make_async_remote_copy(
                src_ref=w_out.at[own_rows],
                dst_ref=w_out.at[own_rows],
                send_sem=w_send.at[1],
                recv_sem=w_recv.at[1],
                device_id=swapped(1),
                device_id_type=MESH,
            )
            w_on.start()
    for j in range(share):
        local[j, 2].wait()
        for o in range(1, groups):
            crossing[j, o, 2].wait_recv()
            for a in range(3):
                crossing[j, o, a].wait_send()
        for stage in range(len(bits)):
            for a in range(2):
                swaps[j, stage, a].wait_send()
    w_cross.wait_send()
    w_on.wait()


def exchange(groups, bits, queries, keys, values, out_weight, columns):
    rows, local_width = queries.shape
    share = local_width // HEAD_DIM // groups
    n = lax.axis_size("seq")
    anywhere = pl.BlockSpec(memory_space=pl.ANY)
    kind = jnp.bfloat16
    stages = len(bits)
    return pl.pallas_call(
        functools.partial(exchange_body, groups, share, bits),
        out_shape=(
            jax.ShapeDtypeStruct((share, groups, rows, HEAD_DIM), kind),
            jax.ShapeDtypeStruct((share, n, rows, HEAD_DIM), kind),
            jax.ShapeDtypeStruct((share, n, rows, HEAD_DIM), kind),
            jax.ShapeDtypeStruct((out_weight.shape[0], columns), kind),
        ),
        in_specs=[anywhere] * 4,
        out_specs=(anywhere,) * 4,
        scratch_shapes=[
            pltpu.SemaphoreType.DMA((share, 3)),
            pltpu.SemaphoreType.DMA((share, groups, 3)),
            pltpu.SemaphoreType.DMA((share, groups, 3)),
            pltpu.SemaphoreType.DMA((share, stages, 2)),
            pltpu.SemaphoreType.DMA((share, stages, 2)),
            pltpu.SemaphoreType.DMA((2,)),
            pltpu.SemaphoreType.DMA((2,)),
        ],
        compiler_params=pltpu.CompilerParams(collective_id=0, has_side_effects=True),
    )(queries, keys, values, out_weight)


def project_body(block_ref, own_ref, far_ref, w_own, w_far, out_ref, total):
    step = pl.program_id(0)

    @pl.when(step == 0)
    def _():
        total[...] = jnp.zeros(total.shape, jnp.float32)

    total[...] += jnp.dot(own_ref[0], w_own[...], preferred_element_type=jnp.float32) + jnp.dot(
        far_ref[0], w_far[...], preferred_element_type=jnp.float32
    )

    @pl.when(step == pl.num_programs(0) - 1)
    def _():
        out_ref[...] = total[...].astype(jnp.bfloat16)


def project(blocks, own, far, out_weight, w_far):
    groups, rows, wide = own.shape
    columns = w_far.shape[1]
    term = pl.BlockSpec((1, rows, wide), lambda s, b: (s, 0, 0))
    return pl.pallas_call(
        project_body,
        out_shape=jax.ShapeDtypeStruct((rows, columns), jnp.bfloat16),
        grid_spec=pltpu.PrefetchScalarGridSpec(
            num_scalar_prefetch=1,
            grid=(groups,),
            in_specs=[
                term,
                term,
                pl.BlockSpec((wide, columns), lambda s, b: (b[s], b[groups])),
                pl.BlockSpec((wide, columns), lambda s, b: (b[s], 0)),
            ],
            out_specs=pl.BlockSpec((rows, columns), lambda s, b: (0, 0)),
            scratch_shapes=[pltpu.VMEM((rows, columns), jnp.float32)],
        ),
        compiler_params=pltpu.CompilerParams(vmem_limit_bytes=40 * 1024 * 1024),
    )(blocks, own, far, out_weight, w_far)


def by_heads(groups, queries, keys, values, kv_tiles, tile_order, out_weight):
    n = lax.axis_size("seq")
    sub = n // groups
    me = lax.axis_index("seq")
    plane, inner = me // sub, me % sub
    bits = []
    bit = sub // 2
    while bit:
        bits.append(bit)
        bit //= 2
    mask_place = [sum(1 << i for i, b in enumerate(bits) if mask & b) for mask in range(sub)]
    mask_place = jnp.array(mask_place, jnp.int32)

    places, counts = [], []
    for o in range(groups):
        slots, count = listed_slots(kv_tiles, tile_order, (plane - o) % groups * sub + inner)
        places.append(mask_place[(slots % sub) ^ inner] * groups + (plane - slots // sub) % groups)
        counts.append(count)
    place, count = jnp.stack(places), jnp.stack(counts)

    columns = out_weight.shape[1] // lax.axis_size("head")
    q, k, v, w_far = exchange(groups, bits, queries, keys, values, out_weight, columns)

    def plane_shift(x, by):
        return lax.ppermute(
            x, "seq", [(i, (i // sub + by) % groups * sub + i % sub) for i in range(n)]
        )

    pieces = [None] * groups
    cuts = [(1, groups - 2), (groups - 1, 1), (0, 1)] if groups > 2 else [(1, 1), (0, 1)]
    for first, tiles in cuts:
        attended = attention(q, k, v, place, count, first, tiles)
        for i in range(tiles):
            o = first + i
            pieces[o] = plane_shift(attended[i], -o) if o else attended[i]
    far = [lax.ppermute(piece, "head", [(0, 1), (1, 0)]) for piece in pieces]
    blocks = jnp.stack([(plane + o) % groups for o in range(groups)] + [lax.axis_index("head")])
    return project(blocks.astype(jnp.int32), jnp.stack(pieces), jnp.stack(far), out_weight, w_far)


def per_device(queries, keys, values, kv_tiles, tile_order, out_weight):
    n = lax.axis_size("seq")
    groups = math.gcd(queries.shape[1] // HEAD_DIM, n)
    sub = n // groups
    power_of_two = sub & (sub - 1) == 0
    two_groups = lax.axis_size("head") == 2
    if two_groups and groups > 1 and sub > 1 and power_of_two and n <= 2 * (2 * REACH + 1):
        return by_heads(groups, queries, keys, values, kv_tiles, tile_order, out_weight)
    return by_ring(queries, keys, values, kv_tiles, tile_order, out_weight)


def solution(mesh):
    return jax.shard_map(
        per_device,
        mesh=mesh,
        in_specs=(P("seq", "head"), P("seq", "head"), P("seq", "head"), P(), P(), P("head", None)),
        out_specs=P("seq", "head"),
        check_vma=False,
    )
```

time: 271 us -> 218 us (0.80)
  the two profiles are of different devices: /device:TPU:0 before, /device:TPU:7 now
where the time goes in v2:
time: 218 us; the launch traced here: 214 us
  Pallas kernels  159 us (73%)
  waiting for transfers between devices  24.7 us (11%)
  local copies, waits for them, and re-layouts  9.26 us (4%)
  starting transfers between devices  8.79 us (4%)
  between operations  7.72 us (4%)
  other arithmetic  4.22 us (2%)
    pallas_call x1, Pallas kernels, exchange(): pl.pallas_call(functools.partial(exchange_body, groups, share, bits), out...  103 us
    pallas_call x3, Pallas kernels, attention(): pl.pallas_call(functools.partial(attention_body, width), out_shape=jax.Sh...  47.1 us
    ppermute x4, waiting for transfers between devices, by_heads(): far = [lax.ppermute(piece, 'head', [(0, 1), (1, 0)]) for piece in pieces]  24.7 us
    pallas_call x1, Pallas kernels, project(): pl.pallas_call(project_body, out_shape=jax.ShapeDtypeStruct((rows, column...  8.77 us
    ppermute x3, starting transfers between devices, plane_shift(): lax.ppermute(x, 'seq', [(i, (i // sub + by) % groups * sub + i % sub) for...  5.79 us
  transfers between devices with their start and end apart: 7, of which 4 were waited for; matrix products, arithmetic and copies ran while one was open for 1% of the time, Pallas kernels for 12%

profile of v2, /device:TPU:7, one launch (start us, length us, event | category | flops | bytes accessed | tf_op | source)
XLA Modules:
  0.0 213.5 jit_solution(14702453517404043605)
XLA Ops:
  0.0 1.5 fusion.24
  9.0 1.5 fusion.5
  10.6 0.9 select_reduce_fusion.3
  11.5 1.3 gather_fusion.2
  12.8 1.3 gather_fusion.1
  14.2 0.1 reshape.434.place_ref
  14.3 1.3 pad_add_fusion.1.count_ref
  15.6 102.9 %shard_map.73 = (bf16[3,4,384,128]{3,2,1,0:T(8,128)(2,1)}, bf16[3,16,384,128]{3,2,1,0:T(8,128)(2,1)}, bf16[3,16,384,128]{3,2,1,0:T(8,128)(2,1)}, bf16[1536,1536]{1,0:T(8,128)(2,1)}) custom-call(bf16[384,1536]{1,0:T(8,128)(2,1)} %q_ref.1, bf16[384,1536]{1,0:T(8,128)(2,1)} %k_ref.1, bf16[384,1536]{1,0:T(8,128)(2,1)} %v_ref.1, bf16[1536,3072]{1,0:T(8,128)(2,1)} %w_own.1), custom_call_target="tpu_custom_call" | custom-call | tf_op jit(solution)/shard_map/pallas_call | solution.py:246
  118.5 0.0 copy-start.1
  118.5 1.3 copy-done.1
  119.8 22.4 %shard_map.75 = bf16[2,384,384]{2,1,0:T(8,128)(2,1)S(1)} custom-call(s32[26]{0:T(128)S(1)} %reshape.434.place_ref, s32[2]{0:T(128)S(1)} %pad_add_fusion.1.count_ref, bf16[3,4,384,128]{3,2,1,0:T(8,128)(2,1)S(1)} %copy-done.1, bf16[3,16,384,128]{3,2,1,0:T(8,128)(2,1)} %get-tuple-element.10.k_ref, bf16[3,16,384,128]{3,2,1,0:T(8,128)(2,1)} %get-tuple-element.11.v_ref), custom_call_target="tpu_custom_call" | custom-call | flops 5888802816 | bytes 11796480 | tf_op jit(solution)/shard_map/pallas_call | solution.py:70
  142.2 0.0 copy-start.3
  142.2 0.0 copy-start.2
  142.2 0.1 slice_bitcast_fusion.1
  142.2 2.4 %collective-permute-start = (bf16[384,384]{1,0:T(8,128)(2,1)S(1)}, bf16[384,384]{1,0:T(8,128)(2,1)S(1)}, u32[]{:S(2)}, u32[]{:S(2)}) collective-permute-start(bf16[384,384]{1,0:T(8,128)(2,1)S(1)} %get-tuple-element.21), channel_id=1, source_target_pairs={{0,24},{2,26},{4,28},{6,30},{8,0},{10,2},{12,4},{14,6},{16,8},{18,... | collective-permute-start | bytes 884744 | tf_op jit(solution)/shard_map/ppermute | solution.py:332
  144.6 0.0 collective-permute-start.1
  144.6 0.0 copy-done.3
  144.6 0.7 gather_fusion.3
  145.3 0.0 copy-done.2
  145.3 12.4 %shard_map.76 = bf16[1,384,384]{2,1,0:T(8,128)(2,1)S(1)} custom-call(s32[13]{0:T(128)S(1)} %fusion.3.place_ref, s32[1]{0:T(128)} %bitcast.32.count_ref, bf16[3,4,384,128]{3,2,1,0:T(8,128)(2,1)S(1)} %copy-done.2, bf16[3,16,384,128]{3,2,1,0:T(8,128)(2,1)} %get-tuple-element.10.k_ref, bf16[3,16,384,128]{3,2,1,0:T(8,128)(2,1)} %get-tuple-element.11.v_ref), custom_call_target="tpu_custom_call" | custom-call | flops 2944401408 | bytes 11796480 | tf_op jit(solution)/shard_map/pallas_call | solution.py:70
  157.7 3.4 %collective-permute-start.2 = (bf16[384,384]{1,0:T(8,128)(2,1)S(1)}, bf16[384,384]{1,0:T(8,128)(2,1)S(1)}, u32[]{:S(2)}, u32[]{:S(2)}) collective-permute-start(bf16[384,384]{1,0:T(8,128)(2,1)S(1)} %bitcast.75), channel_id=1, source_target_pairs={{0,8},{2,10},{4,12},{6,14},{8,16},{10,18},{12,20},{14,22},{16,24},... | collective-permute-start | bytes 884744 | tf_op jit(solution)/shard_map/ppermute | solution.py:332
  161.2 0.7 gather_fusion
  161.9 12.3 %shard_map.74 = bf16[1,384,384]{2,1,0:T(8,128)(2,1)S(1)} custom-call(s32[13]{0:T(128)S(1)} %fusion.place_ref, s32[1]{0:T(128)} %bitcast.9.count_ref, bf16[3,4,384,128]{3,2,1,0:T(8,128)(2,1)S(1)} %copy-done.2, bf16[3,16,384,128]{3,2,1,0:T(8,128)(2,1)} %get-tuple-element.10.k_ref, bf16[3,16,384,128]{3,2,1,0:T(8,128)(2,1)} %get-tuple-element.11.v_ref), custom_call_target="tpu_custom_call" | custom-call | flops 2944401408 | bytes 11796480 | tf_op jit(solution)/shard_map/pallas_call | solution.py:70
  174.2 0.4 collective-permute-start.3
  174.6 0.0 collective-permute-done
  174.6 1.1 collective-permute-start.4
  175.8 0.0 collective-permute-done.1
  175.8 0.3 collective-permute-start.5
  176.1 0.0 collective-permute-done.2
  176.1 1.1 collective-permute-start.6
  177.2 0.1 stack.70.block_ref
  177.3 0.2 pad_maximum_fusion.own_ref
  177.5 5.8 %collective-permute-done.3 = bf16[384,384]{1,0:T(8,128)(2,1)S(1)} collective-permute-done((bf16[384,384]{1,0:T(8,128)(2,1)S(1)}, bf16[384,384]{1,0:T(8,128)(2,1)S(1)}, u32[]{:S(2)}, u32[]{:S(2)}) %collective-permute-start.3) | collective-permute-done | bytes 294944 | tf_op jit(solution)/shard_map/ppermute | solution.py:343
  183.3 6.3 %collective-permute-done.4 = bf16[384,384]{1,0:T(8,128)(2,1)S(1)} collective-permute-done((bf16[384,384]{1,0:T(8,128)(2,1)S(1)}, bf16[384,384]{1,0:T(8,128)(2,1)S(1)}, u32[]{:S(2)}, u32[]{:S(2)}) %collective-permute-start.4) | collective-permute-done | bytes 294944 | tf_op jit(solution)/shard_map/ppermute | solution.py:343
  189.6 6.3 %collective-permute-done.5 = bf16[384,384]{1,0:T(8,128)(2,1)S(1)} collective-permute-done((bf16[384,384]{1,0:T(8,128)(2,1)S(1)}, bf16[384,384]{1,0:T(8,128)(2,1)S(1)}, u32[]{:S(2)}, u32[]{:S(2)}) %collective-permute-start.5) | collective-permute-done | bytes 294944 | tf_op jit(solution)/shard_map/ppermute | solution.py:343
  195.9 6.3 %collective-permute-done.6 = bf16[384,384]{1,0:T(8,128)(2,1)S(1)} collective-permute-done((bf16[384,384]{1,0:T(8,128)(2,1)S(1)}, bf16[384,384]{1,0:T(8,128)(2,1)S(1)}, u32[]{:S(2)}, u32[]{:S(2)}) %collective-permute-start.6) | collective-permute-done | bytes 294944 | tf_op jit(solution)/shard_map/ppermute | solution.py:343
  202.2 0.2 pad_maximum_fusion.1.far_ref
  202.4 0.0 copy-start
  202.4 2.3 %copy-done = bf16[1536,1536]{1,0:T(8,128)(2,1)S(1)} copy-done((bf16[1536,1536]{1,0:T(8,128)(2,1)S(1)}, bf16[1536,1536]{1,0:T(8,128)(2,1)}, u32[]{:S(2)}) %copy-start) | copy-done | bytes 4718616
  204.8 8.8 %shard_map.77 = bf16[384,1536]{1,0:T(8,128)(2,1)} custom-call(s32[5]{0:T(128)S(1)} %stack.70.block_ref, bf16[4,384,384]{2,1,0:T(8,128)(2,1)S(1)} %pad_maximum_fusion.own_ref, bf16[4,384,384]{2,1,0:T(8,128)(2,1)S(1)} %pad_maximum_fusion.1.far_ref, bf16[1536,3072]{1,0:T(8,128)(2,1)} %w_own.1, bf16[1536,1536]{1,0:T(8,128)(2,1)S(1)} %copy-done), custom_call_target="tpu_custom_call" | custom-call | tf_op jit(solution)/shard_map/pallas_call | solution.py:289
  (11 shorter events, 0.1 us)
Async XLA Ops:
  118.5 1.3 copy-start.1
  142.2 2.5 %copy-start.3 = (s32[4]{0:T(128)S(1)}, s32[4]{0:T(128)}, u32[]{:S(2)}) copy-start(s32[4]{0:T(128)} %constant.152.clone) | copy-start | bytes 52
  142.2 3.2 %copy-start.2 = (bf16[3,4,384,128]{3,2,1,0:T(8,128)(2,1)S(1)}, bf16[3,4,384,128]{3,2,1,0:T(8,128)(2,1)}, u32[]{:S(2)}) copy-start(bf16[3,4,384,128]{3,2,1,0:T(8,128)(2,1)} %get-tuple-element.9.q_ref) | copy-start | bytes 3538948
  142.2 32.4 %collective-permute-start = (bf16[384,384]{1,0:T(8,128)(2,1)S(1)}, bf16[384,384]{1,0:T(8,128)(2,1)S(1)}, u32[]{:S(2)}, u32[]{:S(2)}) collective-permute-start(bf16[384,384]{1,0:T(8,128)(2,1)S(1)} %get-tuple-element.21), channel_id=1, source_target_pairs={{0,24},{2,26},{4,28},{6,30},{8,0},{10,2},{12,4},{14,6},{16,8},{18,... | collective-permute-start | bytes 884744 | tf_op jit(solution)/shard_map/ppermute | solution.py:332
  144.6 31.2 %collective-permute-start.1 = (bf16[384,384]{1,0:T(8,128)(2,1)S(1)}, bf16[384,384]{1,0:T(8,128)(2,1)S(1)}, u32[]{:S(2)}, u32[]{:S(2)}) collective-permute-start(bf16[384,384]{1,0:T(8,128)(2,1)S(1)} %get-tuple-element.22), channel_id=1, source_target_pairs={{0,16},{2,18},{4,20},{6,22},{8,24},{10,26},{12,28},{14,30},{16,0},... | collective-permute-start | bytes 884744 | tf_op jit(solution)/shard_map/ppermute | solution.py:332
  157.7 18.4 %collective-permute-start.2 = (bf16[384,384]{1,0:T(8,128)(2,1)S(1)}, bf16[384,384]{1,0:T(8,128)(2,1)S(1)}, u32[]{:S(2)}, u32[]{:S(2)}) collective-permute-start(bf16[384,384]{1,0:T(8,128)(2,1)S(1)} %bitcast.75), channel_id=1, source_target_pairs={{0,8},{2,10},{4,12},{6,14},{8,16},{10,18},{12,20},{14,22},{16,24},... | collective-permute-start | bytes 884744 | tf_op jit(solution)/shard_map/ppermute | solution.py:332
  174.2 9.1 %collective-permute-start.3 = (bf16[384,384]{1,0:T(8,128)(2,1)S(1)}, bf16[384,384]{1,0:T(8,128)(2,1)S(1)}, u32[]{:S(2)}, u32[]{:S(2)}) collective-permute-start(bf16[384,384]{1,0:T(8,128)(2,1)S(1)} %bitcast.74), channel_id=1, source_target_pairs={{0,1},{1,0},{2,3},{3,2},{4,5},{5,4},{6,7},{7,6},{8,9},{9,8},{10,11... | collective-permute-start | bytes 884744 | tf_op jit(solution)/shard_map/ppermute | solution.py:343
  174.6 15.0 %collective-permute-start.4 = (bf16[384,384]{1,0:T(8,128)(2,1)S(1)}, bf16[384,384]{1,0:T(8,128)(2,1)S(1)}, u32[]{:S(2)}, u32[]{:S(2)}) collective-permute-start(bf16[384,384]{1,0:T(8,128)(2,1)S(1)} %collective-permute-done), channel_id=1, source_target_pairs={{0,1},{1,0},{2,3},{3,2},{4,5},{5,4},{6,7},{7,6},{8,9},{9,8},{10,11... | collective-permute-start | bytes 884744 | tf_op jit(solution)/shard_map/ppermute | solution.py:343
  175.8 20.2 %collective-permute-start.5 = (bf16[384,384]{1,0:T(8,128)(2,1)S(1)}, bf16[384,384]{1,0:T(8,128)(2,1)S(1)}, u32[]{:S(2)}, u32[]{:S(2)}) collective-permute-start(bf16[384,384]{1,0:T(8,128)(2,1)S(1)} %collective-permute-done.1), channel_id=1, source_target_pairs={{0,1},{1,0},{2,3},{3,2},{4,5},{5,4},{6,7},{7,6},{8,9},{9,8},{10,11... | collective-permute-start | bytes 884744 | tf_op jit(solution)/shard_map/ppermute | solution.py:343
  176.1 26.1 %collective-permute-start.6 = (bf16[384,384]{1,0:T(8,128)(2,1)S(1)}, bf16[384,384]{1,0:T(8,128)(2,1)S(1)}, u32[]{:S(2)}, u32[]{:S(2)}) collective-permute-start(bf16[384,384]{1,0:T(8,128)(2,1)S(1)} %collective-permute-done.2), channel_id=1, source_target_pairs={{0,1},{1,0},{2,3},{3,2},{4,5},{5,4},{6,7},{7,6},{8,9},{9,8},{10,11... | collective-permute-start | bytes 884744 | tf_op jit(solution)/shard_map/ppermute | solution.py:343
  202.4 2.3 %copy-start = (bf16[1536,1536]{1,0:T(8,128)(2,1)S(1)}, bf16[1536,1536]{1,0:T(8,128)(2,1)}, u32[]{:S(2)}) copy-start(bf16[1536,1536]{1,0:T(8,128)(2,1)} %get-tuple-element.12.w_far) | copy-start | bytes 14155780

commit v3 on v2

--- a/solution.py
+++ b/solution.py
@@ -13,9 +13,21 @@
 MESH = pl.DeviceIdType.MESH
 
 
-def attention_body(width, place_ref, count_ref, q_ref, k_ref, v_ref, out_ref, scores, tops, summed):
-    row = pl.program_id(0)
-    count = count_ref[row]
+def attention_body(
+    slot_of_row, place_of_slot, at_ref, tiles_ref, order_ref, q_ref, k_ref, v_ref, out_ref, scores, tops, summed
+):
+    slots, width = tiles_ref.shape
+    at = [at_ref[i] for i in range(at_ref.shape[0])]
+    first_tile = order_ref[0]
+    own_tile = order_ref[slot_of_row(pl.program_id(0), at)]
+    count = 0
+    for entry in range(width):
+        count += jnp.where(tiles_ref[own_tile, entry] >= 0, 1, 0)
+
+    def place_at(entry):
+        slot = lax.rem(tiles_ref[own_tile, entry] - first_tile + slots, slots)
+        return place_of_slot(slot, at)
+
     heads = q_ref.shape[0]
     scale = math.log2(math.e) / math.sqrt(HEAD_DIM)
     tops[...] = jnp.full(tops.shape, -jnp.inf, jnp.float32)
@@ -23,7 +35,7 @@
     ones = jnp.ones((k_ref.shape[2], HEAD_DIM), jnp.bfloat16)
 
     def find(entry, carry):
-        place = place_ref[row * width + entry]
+        place = place_at(entry)
         for h in range(heads):
             fresh = lax.dot_general(
                 q_ref[h, 0],
@@ -44,9 +56,16 @@
         tops[h] = jnp.broadcast_to(top, tops.shape[1:])
 
     def add(entry, carry):
-        place = place_ref[row * width + entry]
+        place = place_at(entry)
         for h in range(heads):
-            weights = jnp.exp2(scores[h, entry] * scale - tops[h][:, :1]).astype(jnp.bfloat16)
+            top = tops[h]
+            weights = jnp.concatenate(
+                [
+                    jnp.exp2(scores[h, entry, :, lane : lane + HEAD_DIM] * scale - top).astype(jnp.bfloat16)
+                    for lane in range(0, scores.shape[3], HEAD_DIM)
+                ],
+                axis=1,
+            )
             paired = jnp.concatenate([v_ref[h, place], ones], axis=1)
             summed[h] += jnp.dot(weights, paired, preferred_element_type=jnp.float32)
         return carry
@@ -59,19 +78,19 @@
         ).astype(jnp.bfloat16)
 
 
-def attention(q, k, v, place, count, first, tiles):
+def attention(q, k, v, at, kv_tiles, tile_order, slot_of_row, place_of_slot, first, tiles):
     heads, _, rows, _ = q.shape
     key_tiles = k.shape[1]
-    width = place.shape[1]
+    width = kv_tiles.shape[1]
     units = heads * tiles * min(width, key_tiles)
     key_spec = pl.BlockSpec(
         (heads, key_tiles, rows, HEAD_DIM), lambda t, *_: (0, 0, 0, 0), pipeline_mode=pl.Buffered(1)
     )
     return pl.pallas_call(
-        functools.partial(attention_body, width),
+        functools.partial(attention_body, slot_of_row, place_of_slot),
         out_shape=jax.ShapeDtypeStruct((tiles, rows, heads * HEAD_DIM), jnp.bfloat16),
         grid_spec=pltpu.PrefetchScalarGridSpec(
-            num_scalar_prefetch=2,
+            num_scalar_prefetch=3,
             grid=(tiles,),
             in_specs=[
                 pl.BlockSpec((heads, 1, rows, HEAD_DIM), lambda t, *_: (0, first + t, 0, 0)),
@@ -91,16 +110,7 @@
             bytes_accessed=2 * (2 * q.size + k.size + v.size),
             transcendentals=units * rows * rows,
         ),
-    )(place[first : first + tiles].reshape(-1), count[first : first + tiles], q, k, v)
-
-
-def listed_slots(kv_tiles, tile_order, slot):
-    listed = kv_tiles[tile_order[slot]]
-    slot_ids = jnp.arange(tile_order.shape[0], dtype=jnp.int32)
-    found = jnp.sum(
-        jnp.where(tile_order[None, :] == jnp.maximum(listed, 0)[:, None], slot_ids[None, :], 0), axis=1
-    )
-    return found, jnp.sum((listed >= 0).astype(jnp.int32))
+    )(at, kv_tiles, tile_order, q, k, v)
 
 
 def by_ring(queries, keys, values, kv_tiles, tile_order, out_weight):
@@ -119,10 +129,18 @@
     both = jnp.stack([received[o] for o in range(-REACH, REACH + 1)])
     both = both.reshape(window, 2, rows, heads, HEAD_DIM).transpose(1, 3, 0, 2, 4)
     q = queries.reshape(rows, heads, HEAD_DIM).transpose(1, 0, 2)[:, None]
-    slots, count = listed_slots(kv_tiles, tile_order, me)
-    place = (slots - me + REACH) % n
-    place = jnp.clip(place, 0, window - 1)
-    attended = attention(q, both[0], both[1], place[None], count[None], 0, 1)[0]
+    attended = attention(
+        q,
+        both[0],
+        both[1],
+        me.reshape(1).astype(jnp.int32),
+        kv_tiles,
+        tile_order,
+        lambda row, at: at[0],
+        lambda slot, at: lax.rem(slot - at[0] + REACH + n, n),
+        0,
+        1,
+    )[0]
     partial = jnp.dot(attended, out_weight, preferred_element_type=jnp.float32).astype(jnp.bfloat16)
     return lax.psum_scatter(partial, "head", scatter_dimension=1, tiled=True)
 
@@ -167,20 +185,20 @@
         return ref.at[:, pl.ds(pl.multiple_of(start, HEAD_DIM), HEAD_DIM)]
 
     local, crossing = {}, {}
-    for j in range(share):
-        for a, (src, dst) in enumerate(arrays):
-            for o in range(1, groups):
-                crossing[j, o, a] = pltpu.make_async_remote_copy(
-                    src_ref=cut(src, (plane + o) % groups, j),
-                    dst_ref=dst.at[j, o],
-                    send_sem=plane_send.at[j, o, a],
-                    recv_sem=plane_recv.at[j, o, a],
-                    device_id=across(o),
-                    device_id_type=MESH,
-                )
-                crossing[j, o, a].start()
-            local[j, a] = pltpu.make_async_copy(cut(src, plane, j), dst.at[j, 0], local_sem.at[j, a])
-            local[j, a].start()
+    for j, a in [(j, a) for j in range(share) for a in (0, 1)] + [(j, 2) for j in range(share)]:
+        src, dst = arrays[a]
+        for o in range(1, groups):
+            crossing[j, o, a] = pltpu.make_async_remote_copy(
+                src_ref=cut(src, (plane + o) % groups, j),
+                dst_ref=dst.at[j, o],
+                send_sem=plane_send.at[j, o, a],
+                recv_sem=plane_recv.at[j, o, a],
+                device_id=across(o),
+                device_id_type=MESH,
+            )
+            crossing[j, o, a].start()
+        local[j, a] = pltpu.make_async_copy(cut(src, plane, j), dst.at[j, 0], local_sem.at[j, a])
+        local[j, a].start()
 
     swaps = {}
 
@@ -266,43 +284,47 @@
     )(queries, keys, values, out_weight)
 
 
-def project_body(block_ref, own_ref, far_ref, w_own, w_far, out_ref, total):
+def project_body(first, at_ref, term_ref, weight_ref, *refs):
+    base_ref, out_ref, total = (None, *refs) if first else refs
     step = pl.program_id(0)
 
     @pl.when(step == 0)
     def _():
-        total[...] = jnp.zeros(total.shape, jnp.float32)
-
-    total[...] += jnp.dot(own_ref[0], w_own[...], preferred_element_type=jnp.float32) + jnp.dot(
-        far_ref[0], w_far[...], preferred_element_type=jnp.float32
-    )
+        total[...] = jnp.zeros(total.shape, jnp.float32) if first else base_ref[...]
+
+    total[...] += jnp.dot(term_ref[0], weight_ref[...], preferred_element_type=jnp.float32)
 
     @pl.when(step == pl.num_programs(0) - 1)
     def _():
-        out_ref[...] = total[...].astype(jnp.bfloat16)
-
-
-def project(blocks, own, far, out_weight, w_far):
-    groups, rows, wide = own.shape
-    columns = w_far.shape[1]
-    term = pl.BlockSpec((1, rows, wide), lambda s, b: (s, 0, 0))
+        out_ref[...] = total[...].astype(out_ref.dtype)
+
+
+def project(at, terms, weight, column_entry, base):
+    groups, rows, wide = terms.shape
+    first = base is None
+    columns = weight.shape[1] // (lax.axis_size("head") if first else 1)
+    whole = pl.BlockSpec((rows, columns), lambda s, at: (0, 0))
     return pl.pallas_call(
-        project_body,
-        out_shape=jax.ShapeDtypeStruct((rows, columns), jnp.bfloat16),
+        functools.partial(project_body, first),
+        out_shape=jax.ShapeDtypeStruct((rows, columns), jnp.float32 if first else jnp.bfloat16),
         grid_spec=pltpu.PrefetchScalarGridSpec(
             num_scalar_prefetch=1,
             grid=(groups,),
             in_specs=[
-                term,
-                term,
-                pl.BlockSpec((wide, columns), lambda s, b: (b[s], b[groups])),
-                pl.BlockSpec((wide, columns), lambda s, b: (b[s], 0)),
-            ],
-            out_specs=pl.BlockSpec((rows, columns), lambda s, b: (0, 0)),
+                pl.BlockSpec((1, rows, wide), lambda s, at: (s, 0, 0)),
+                pl.BlockSpec((wide, columns), lambda s, at: (at[2 + s], at[column_entry] if first else 0)),
+            ]
+            + ([] if first else [whole]),
+            out_specs=whole,
             scratch_shapes=[pltpu.VMEM((rows, columns), jnp.float32)],
         ),
         compiler_params=pltpu.CompilerParams(vmem_limit_bytes=40 * 1024 * 1024),
-    )(blocks, own, far, out_weight, w_far)
+        cost_estimate=pl.CostEstimate(
+            flops=2 * groups * rows * wide * columns,
+            bytes_accessed=2 * groups * wide * columns + 6 * rows * columns,
+            transcendentals=0,
+        ),
+    )(at, terms, weight, *([] if first else [base]))
 
 
 def by_heads(groups, queries, keys, values, kv_tiles, tile_order, out_weight):
@@ -315,15 +337,20 @@
     while bit:
         bits.append(bit)
         bit //= 2
-    mask_place = [sum(1 << i for i, b in enumerate(bits) if mask & b) for mask in range(sub)]
-    mask_place = jnp.array(mask_place, jnp.int32)
-
-    places, counts = [], []
-    for o in range(groups):
-        slots, count = listed_slots(kv_tiles, tile_order, (plane - o) % groups * sub + inner)
-        places.append(mask_place[(slots % sub) ^ inner] * groups + (plane - slots // sub) % groups)
-        counts.append(count)
-    place, count = jnp.stack(places), jnp.stack(counts)
+    head = lax.axis_index("head")
+    at = jnp.stack([plane, inner] + [(plane + o) % groups for o in range(groups)] + [head])
+    at = at.astype(jnp.int32)
+
+    def slot_of_row(first, row, at):
+        return lax.rem(at[0] - first - row + groups, groups) * sub + at[1]
+
+    def place_of_slot(slot, at):
+        from_plane = lax.div(slot, sub)
+        place = lax.rem(at[0] - from_plane + groups, groups)
+        for stage, bit in enumerate(bits):
+            differs = lax.rem(lax.div(slot, bit) + lax.div(at[1], bit), 2)
+            place += differs * (groups << stage)
+        return place
 
     columns = out_weight.shape[1] // lax.axis_size("head")
     q, k, v, w_far = exchange(groups, bits, queries, keys, values, out_weight, columns)
@@ -333,16 +360,36 @@
             x, "seq", [(i, (i // sub + by) % groups * sub + i % sub) for i in range(n)]
         )
 
-    pieces = [None] * groups
-    cuts = [(1, groups - 2), (groups - 1, 1), (0, 1)] if groups > 2 else [(1, 1), (0, 1)]
-    for first, tiles in cuts:
-        attended = attention(q, k, v, place, count, first, tiles)
+    pieces, far = [None] * groups, [None] * groups
+
+    def attend(first, tiles, q):
+        rows_of = functools.partial(slot_of_row, first)
+        found = attention(q, k, v, at, kv_tiles, tile_order, rows_of, place_of_slot, first, tiles)
         for i in range(tiles):
             o = first + i
-            pieces[o] = plane_shift(attended[i], -o) if o else attended[i]
-    far = [lax.ppermute(piece, "head", [(0, 1), (1, 0)]) for piece in pieces]
-    blocks = jnp.stack([(plane + o) % groups for o in range(groups)] + [lax.axis_index("head")])
-    return project(blocks.astype(jnp.int32), jnp.stack(pieces), jnp.stack(far), out_weight, w_far)
+            pieces[o] = plane_shift(found[i], -o) if o else found[i]
+
+    def to_far(which):
+        for o in which:
+            far[o] = lax.ppermute(pieces[o], "head", [(0, 1), (1, 0)])
+
+    early = list(range(1, groups - 1))
+    if early:
+        attend(1, len(early), q)
+        attend(groups - 1, 1, q)
+        held, q = lax.optimization_barrier(([pieces[o] for o in early], q))
+        for o, piece in zip(early, held):
+            pieces[o] = piece
+        to_far(early)
+    else:
+        attend(groups - 1, 1, q)
+    attend(0, 1, q)
+    held, pieces[0] = lax.optimization_barrier(([far[o] for o in early], pieces[0]))
+    for o, piece in zip(early, held):
+        far[o] = piece
+    to_far([0, groups - 1])
+    half_way = project(at, jnp.stack(pieces), out_weight, 2 + groups, None)
+    return project(at, jnp.stack(far), w_far, None, half_way)
 
 
 def per_device(queries, keys, values, kv_tiles, tile_order, out_weight):

time: 218 us -> 178 us (0.82)
  the two profiles are of different devices: /device:TPU:7 before, /device:TPU:4 now
where the time goes in v3:
time: 178 us; the launch traced here: 179 us
  Pallas kernels  146 us (82%)
  starting transfers between devices  23.7 us (13%)
  waiting for transfers between devices  6.56 us (4%)
    pallas_call x1, Pallas kernels, exchange(): pl.pallas_call(functools.partial(exchange_body, groups, share, bits), out...  87.6 us
    pallas_call x3, Pallas kernels, attention(): pl.pallas_call(functools.partial(attention_body, slot_of_row, place_of_sl...  49.1 us
    ppermute x3, starting transfers between devices, plane_shift(): lax.ppermute(x, 'seq', [(i, (i // sub + by) % groups * sub + i % sub) for...  15.9 us
    pallas_call x2, Pallas kernels, project(): pl.pallas_call(functools.partial(project_body, first), out_shape=jax.Shap...  9.52 us
    ppermute x4, starting transfers between devices, to_far(): far[o] = lax.ppermute(pieces[o], 'head', [(0, 1), (1, 0)])  7.79 us
    ppermute x3, waiting for transfers between devices, plane_shift(): lax.ppermute(x, 'seq', [(i, (i // sub + by) % groups * sub + i % sub) for...  4.56 us
  transfers between devices with their start and end apart: 7, of which 2 were waited for; matrix products, arithmetic and copies ran while one was open for 0% of the time, Pallas kernels for 20%

profile of v3, /device:TPU:4, one launch (start us, length us, event | category | flops | bytes accessed | tf_op | source)
XLA Modules:
  0.0 179.5 jit_solution(9352166120176955159)
XLA Ops:
  0.0 0.0 copy-start.1
  0.0 0.0 copy-start.2
  0.0 87.6 %shard_map.64 = (bf16[3,4,384,128]{3,2,1,0:T(8,128)(2,1)}, bf16[3,16,384,128]{3,2,1,0:T(8,128)(2,1)}, bf16[3,16,384,128]{3,2,1,0:T(8,128)(2,1)}, bf16[1536,1536]{1,0:T(8,128)(2,1)}) custom-call(bf16[384,1536]{1,0:T(8,128)(2,1)} %q_ref.1, bf16[384,1536]{1,0:T(8,128)(2,1)} %k_ref.1, bf16[384,1536]{1,0:T(8,128)(2,1)} %v_ref.1, bf16[1536,3072]{1,0:T(8,128)(2,1)} %weight_ref.1), custom_call_target="tpu_custom_call" | custom-call | tf_op jit(solution)/shard_map/pallas_call | solution.py:264
  87.7 0.1 stack.61.at_ref
  87.7 0.0 copy-done.1
  87.8 0.0 copy-done.2
  87.8 0.0 copy-start
  87.8 1.3 copy-done
  89.0 17.2 %shard_map.65 = bf16[2,384,384]{2,1,0:T(8,128)(2,1)S(1)} custom-call(s32[7]{0:T(128)S(1)} %stack.61.at_ref, s32[16,13]{1,0:T(8,128)S(1)} %copy-done.1, s32[16]{0:T(128)S(1)} %copy-done.2, bf16[3,4,384,128]{3,2,1,0:T(8,128)(2,1)S(1)} %copy-done, bf16[3,16,384,128]{3,2,1,0:T(8,128)(2,1)} %get-tuple-element.16.k_ref, ...), custom_call_target="tpu_custom_call" | custom-call | flops 5888802816 | bytes 11796480 | tf_op jit(solution)/shard_map/pallas_call | solution.py:89
  106.2 0.1 slice_bitcast_fusion
  106.3 11.4 %collective-permute-start.1 = (bf16[384,384]{1,0:T(8,128)(2,1)S(1)}, bf16[384,384]{1,0:T(8,128)(2,1)S(1)}, u32[]{:S(2)}, u32[]{:S(2)}) collective-permute-start(bf16[384,384]{1,0:T(8,128)(2,1)S(1)} %get-tuple-element.25), channel_id=1, source_target_pairs={{0,16},{2,18},{4,20},{6,22},{8,24},{10,26},{12,28},{14,30},{16,0},... | collective-permute-start | bytes 884744 | tf_op jit(solution)/shard_map/ppermute | solution.py:359
  117.7 4.4 %collective-permute-start = (bf16[384,384]{1,0:T(8,128)(2,1)S(1)}, bf16[384,384]{1,0:T(8,128)(2,1)S(1)}, u32[]{:S(2)}, u32[]{:S(2)}) collective-permute-start(bf16[384,384]{1,0:T(8,128)(2,1)S(1)} %get-tuple-element.26), channel_id=1, source_target_pairs={{0,24},{2,26},{4,28},{6,30},{8,0},{10,2},{12,4},{14,6},{16,8},{18,... | collective-permute-start | bytes 884744 | tf_op jit(solution)/shard_map/ppermute | solution.py:359
  122.1 0.0 slice-start
  122.1 0.0 slice-start.1
  122.1 16.1 %shard_map.67 = bf16[1,384,384]{2,1,0:T(8,128)(2,1)S(1)} custom-call(s32[7]{0:T(128)S(1)} %stack.61.at_ref, s32[16,13]{1,0:T(8,128)S(1)} %copy-done.1, s32[16]{0:T(128)S(1)} %copy-done.2, bf16[3,4,384,128]{3,2,1,0:T(8,128)(2,1)S(1)} %copy-done, bf16[3,16,384,128]{3,2,1,0:T(8,128)(2,1)} %get-tuple-element.16.k_ref, ...), custom_call_target="tpu_custom_call" | custom-call | flops 2944401408 | bytes 11796480 | tf_op jit(solution)/shard_map/pallas_call | solution.py:89
  138.2 0.0 slice-start.2
  138.2 0.1 collective-permute-start.5
  138.3 0.0 collective-permute-done.1
  138.3 0.0 collective-permute-done
  138.3 3.9 %collective-permute-start.2 = (bf16[384,384]{1,0:T(8,128)(2,1)S(1)}, bf16[384,384]{1,0:T(8,128)(2,1)S(1)}, u32[]{:S(2)}, u32[]{:S(2)}) collective-permute-start(bf16[384,384]{1,0:T(8,128)(2,1)S(1)} %collective-permute-done), channel_id=1, source_target_pairs={{0,1},{1,0},{2,3},{3,2},{4,5},{5,4},{6,7},{7,6},{8,9},{9,8},{10,11... | collective-permute-start | bytes 884744 | tf_op jit(solution)/shard_map/ppermute | solution.py:374
  142.2 0.1 collective-permute-start.3
  142.3 4.6 %collective-permute-done.5 = bf16[384,384]{1,0:T(8,128)(2,1)S(1)} collective-permute-done((bf16[384,384]{1,0:T(8,128)(2,1)S(1)}, bf16[384,384]{1,0:T(8,128)(2,1)S(1)}, u32[]{:S(2)}, u32[]{:S(2)}) %collective-permute-start.5) | collective-permute-done | bytes 294944 | tf_op jit(solution)/shard_map/ppermute | solution.py:359
  146.8 3.8 %collective-permute-start.6 = (bf16[384,384]{1,0:T(8,128)(2,1)S(1)}, bf16[384,384]{1,0:T(8,128)(2,1)}, u32[]{:S(2)}, u32[]{:S(2)}) collective-permute-start(bf16[384,384]{1,0:T(8,128)(2,1)S(1)} %collective-permute-done.5), channel_id=1, source_target_pairs={{0,1},{1,0},{2,3},{3,2},{4,5},{5,4},{6,7},{7,6},{8,9},{9,8},{10,11... | collective-permute-start | bytes 884744 | tf_op jit(solution)/shard_map/ppermute | solution.py:374
  150.6 15.8 %shard_map.66 = bf16[1,384,384]{2,1,0:T(8,128)(2,1)S(1)} custom-call(s32[7]{0:T(128)S(1)} %stack.61.at_ref, s32[16,13]{1,0:T(8,128)S(1)} %copy-done.1, s32[16]{0:T(128)S(1)} %copy-done.2, bf16[3,4,384,128]{3,2,1,0:T(8,128)(2,1)S(1)} %copy-done, bf16[3,16,384,128]{3,2,1,0:T(8,128)(2,1)} %get-tuple-element.16.k_ref, ...), custom_call_target="tpu_custom_call" | custom-call | flops 2944401408 | bytes 11796480 | tf_op jit(solution)/shard_map/pallas_call | solution.py:89
  166.4 0.0 collective-permute-done.2
  166.4 0.0 collective-permute-done.3
  166.4 0.1 collective-permute-start.4
  166.5 0.0 slice-start.3
  166.5 0.2 pad_maximum_fusion.1.term_ref
  166.7 0.0 slice-done
  166.7 0.0 slice-done.1
  166.7 0.0 slice-done.2
  166.8 0.0 slice-start.4
  166.8 4.4 %shard_map.68.refs_0_ = f32[384,1536]{1,0:T(8,128)S(1)} custom-call(s32[7]{0:T(128)S(1)} %stack.61.at_ref, bf16[4,384,384]{2,1,0:T(8,128)(2,1)S(1)} %pad_maximum_fusion.1.term_ref, bf16[1536,3072]{1,0:T(8,128)(2,1)S(1)} %bitcast.22), custom_call_target="tpu_custom_call" | custom-call | flops 1811939328 | bytes 8257536 | tf_op jit(solution)/shard_map/pallas_call | solution.py:307
  171.2 0.0 collective-permute-done.6
  171.2 2.0 %collective-permute-done.4 = bf16[384,384]{1,0:T(8,128)(2,1)S(1)} collective-permute-done((bf16[384,384]{1,0:T(8,128)(2,1)S(1)}, bf16[384,384]{1,0:T(8,128)(2,1)S(1)}, u32[]{:S(2)}, u32[]{:S(2)}) %collective-permute-start.4) | collective-permute-done | bytes 294944 | tf_op jit(solution)/shard_map/ppermute | solution.py:374
  173.2 1.1 pad_maximum_fusion.term_ref
  174.4 0.0 slice-done.3
  174.4 0.0 slice-done.4
  174.4 5.1 %shard_map.69 = bf16[384,1536]{1,0:T(8,128)(2,1)} custom-call(s32[7]{0:T(128)S(1)} %stack.61.at_ref, bf16[4,384,384]{2,1,0:T(8,128)(2,1)S(1)} %pad_maximum_fusion.term_ref, bf16[1536,1536]{1,0:T(8,128)(2,1)S(1)} %bitcast.24, f32[384,1536]{1,0:T(8,128)S(1)} %shard_map.68.refs_0_), custom_call_target="tpu_custom_call" | custom-call | flops 1811939328 | bytes 8257536 | tf_op jit(solution)/shard_map/pallas_call | solution.py:307
  (2 shorter events, 0.0 us)
Async XLA Ops:
  0.0 87.7 %copy-start.1 = (s32[16,13]{1,0:T(8,128)S(1)}, s32[16,13]{1,0:T(8,128)}, u32[]{:S(2)}) copy-start(s32[16,13]{1,0:T(8,128)} %tiles_ref.5) | copy-start | bytes 2500
  0.0 87.8 %copy-start.2 = (s32[16]{0:T(128)S(1)}, s32[16]{0:T(128)}, u32[]{:S(2)}) copy-start(s32[16]{0:T(128)} %order_ref.5) | copy-start | bytes 196
  87.8 1.3 copy-start
  106.3 32.0 %collective-permute-start.1 = (bf16[384,384]{1,0:T(8,128)(2,1)S(1)}, bf16[384,384]{1,0:T(8,128)(2,1)S(1)}, u32[]{:S(2)}, u32[]{:S(2)}) collective-permute-start(bf16[384,384]{1,0:T(8,128)(2,1)S(1)} %get-tuple-element.25), channel_id=1, source_target_pairs={{0,16},{2,18},{4,20},{6,22},{8,24},{10,26},{12,28},{14,30},{16,0},... | collective-permute-start | bytes 884744 | tf_op jit(solution)/shard_map/ppermute | solution.py:359
  117.7 20.6 %collective-permute-start = (bf16[384,384]{1,0:T(8,128)(2,1)S(1)}, bf16[384,384]{1,0:T(8,128)(2,1)S(1)}, u32[]{:S(2)}, u32[]{:S(2)}) collective-permute-start(bf16[384,384]{1,0:T(8,128)(2,1)S(1)} %get-tuple-element.26), channel_id=1, source_target_pairs={{0,24},{2,26},{4,28},{6,30},{8,0},{10,2},{12,4},{14,6},{16,8},{18,... | collective-permute-start | bytes 884744 | tf_op jit(solution)/shard_map/ppermute | solution.py:359
  122.1 44.6 %slice-start = ((s8[9437184]{0:T(1024)(128)(4,1)}), s8[4194304]{0:T(1024)(128)(4,1)S(1)}, s32[]{:S(2)}) async-start(s8[9437184]{0:T(1024)(128)(4,1)} %bitcast.21), calls=%async_computation | async-start | bytes 8388608
  122.1 44.6 %slice-start.1 = ((s8[9437184]{0:T(1024)(128)(4,1)}), s8[4194304]{0:T(1024)(128)(4,1)S(1)}, s32[]{:S(2)}) async-start(s8[9437184]{0:T(1024)(128)(4,1)} %bitcast.21), calls=%async_computation.1 | async-start | bytes 8388608
  138.2 28.5 %slice-start.2 = ((s8[9437184]{0:T(1024)(128)(4,1)}), s8[1048576]{0:T(1024)(128)(4,1)S(1)}, s32[]{:S(2)}) async-start(s8[9437184]{0:T(1024)(128)(4,1)} %bitcast.21), calls=%async_computation.2 | async-start | bytes 2097152
  138.2 8.6 %collective-permute-start.5 = (bf16[384,384]{1,0:T(8,128)(2,1)S(1)}, bf16[384,384]{1,0:T(8,128)(2,1)S(1)}, u32[]{:S(2)}, u32[]{:S(2)}) collective-permute-start(bf16[384,384]{1,0:T(8,128)(2,1)S(1)} %bitcast.26), channel_id=1, source_target_pairs={{0,8},{2,10},{4,12},{6,14},{8,16},{10,18},{12,20},{14,22},{16,24},... | collective-permute-start | bytes 884744 | tf_op jit(solution)/shard_map/ppermute | solution.py:359
  138.3 28.1 %collective-permute-start.2 = (bf16[384,384]{1,0:T(8,128)(2,1)S(1)}, bf16[384,384]{1,0:T(8,128)(2,1)S(1)}, u32[]{:S(2)}, u32[]{:S(2)}) collective-permute-start(bf16[384,384]{1,0:T(8,128)(2,1)S(1)} %collective-permute-done), channel_id=1, source_target_pairs={{0,1},{1,0},{2,3},{3,2},{4,5},{5,4},{6,7},{7,6},{8,9},{9,8},{10,11... | collective-permute-start | bytes 884744 | tf_op jit(solution)/shard_map/ppermute | solution.py:374
  142.2 24.2 %collective-permute-start.3 = (bf16[384,384]{1,0:T(8,128)(2,1)S(1)}, bf16[384,384]{1,0:T(8,128)(2,1)S(1)}, u32[]{:S(2)}, u32[]{:S(2)}) collective-permute-start(bf16[384,384]{1,0:T(8,128)(2,1)S(1)} %collective-permute-done.1), channel_id=1, source_target_pairs={{0,1},{1,0},{2,3},{3,2},{4,5},{5,4},{6,7},{7,6},{8,9},{9,8},{10,11... | collective-permute-start | bytes 884744 | tf_op jit(solution)/shard_map/ppermute | solution.py:374
  146.8 24.4 %collective-permute-start.6 = (bf16[384,384]{1,0:T(8,128)(2,1)S(1)}, bf16[384,384]{1,0:T(8,128)(2,1)}, u32[]{:S(2)}, u32[]{:S(2)}) collective-permute-start(bf16[384,384]{1,0:T(8,128)(2,1)S(1)} %collective-permute-done.5), channel_id=1, source_target_pairs={{0,1},{1,0},{2,3},{3,2},{4,5},{5,4},{6,7},{7,6},{8,9},{9,8},{10,11... | collective-permute-start | bytes 884744 | tf_op jit(solution)/shard_map/ppermute | solution.py:374
  166.4 6.8 %collective-permute-start.4 = (bf16[384,384]{1,0:T(8,128)(2,1)S(1)}, bf16[384,384]{1,0:T(8,128)(2,1)S(1)}, u32[]{:S(2)}, u32[]{:S(2)}) collective-permute-start(bf16[384,384]{1,0:T(8,128)(2,1)S(1)} %bitcast.25), channel_id=1, source_target_pairs={{0,1},{1,0},{2,3},{3,2},{4,5},{5,4},{6,7},{7,6},{8,9},{9,8},{10,11... | collective-permute-start | bytes 884744 | tf_op jit(solution)/shard_map/ppermute | solution.py:374
  166.5 7.9 %slice-start.3 = ((s8[4718592]{0:T(1024)(128)(4,1)}), s8[4194304]{0:T(1024)(128)(4,1)S(1)}, s32[]{:S(2)}) async-start(s8[4718592]{0:T(1024)(128)(4,1)} %bitcast.23), calls=%async_computation.3 | async-start | bytes 8388608
  166.8 7.6 %slice-start.4 = ((s8[4718592]{0:T(1024)(128)(4,1)}), s8[524288]{0:T(1024)(128)(4,1)S(1)}, s32[]{:S(2)}) async-start(s8[4718592]{0:T(1024)(128)(4,1)} %bitcast.23), calls=%async_computation.4 | async-start | bytes 1048576

commit v4 on v3

--- a/solution.py
+++ b/solution.py
@@ -78,7 +78,7 @@
         ).astype(jnp.bfloat16)
 
 
-def attention(q, k, v, at, kv_tiles, tile_order, slot_of_row, place_of_slot, first, tiles):
+def attention(q, k, v, at, kv_tiles, tile_order, slot_of_row, place_of_slot, tiles):
     heads, _, rows, _ = q.shape
     key_tiles = k.shape[1]
     width = kv_tiles.shape[1]
@@ -93,7 +93,7 @@
             num_scalar_prefetch=3,
             grid=(tiles,),
             in_specs=[
-                pl.BlockSpec((heads, 1, rows, HEAD_DIM), lambda t, *_: (0, first + t, 0, 0)),
+                pl.BlockSpec((heads, 1, rows, HEAD_DIM), lambda t, *_: (0, t, 0, 0)),
                 key_spec,
                 key_spec,
             ],
@@ -138,7 +138,6 @@
         tile_order,
         lambda row, at: at[0],
         lambda slot, at: lax.rem(slot - at[0] + REACH + n, n),
-        0,
         1,
     )[0]
     partial = jnp.dot(attended, out_weight, preferred_element_type=jnp.float32).astype(jnp.bfloat16)
@@ -284,47 +283,114 @@
     )(queries, keys, values, out_weight)
 
 
-def project_body(first, at_ref, term_ref, weight_ref, *refs):
-    base_ref, out_ref, total = (None, *refs) if first else refs
-    step = pl.program_id(0)
-
-    @pl.when(step == 0)
-    def _():
-        total[...] = jnp.zeros(total.shape, jnp.float32) if first else base_ref[...]
-
-    total[...] += jnp.dot(term_ref[0], weight_ref[...], preferred_element_type=jnp.float32)
-
-    @pl.when(step == pl.num_programs(0) - 1)
-    def _():
-        out_ref[...] = total[...].astype(out_ref.dtype)
-
-
-def project(at, terms, weight, column_entry, base):
-    groups, rows, wide = terms.shape
-    first = base is None
-    columns = weight.shape[1] // (lax.axis_size("head") if first else 1)
-    whole = pl.BlockSpec((rows, columns), lambda s, at: (0, 0))
+def deliver_body(
+    groups, att_ref, w_ref, w_far_ref, out_ref, home, far, w_own_here, w_far_here, total,
+    w_sem, home_send, home_recv, far_send, far_recv,
+):
+    sub = lax.axis_size("seq") // groups
+    me = lax.axis_index("seq")
+    plane, inner = me // sub, me % sub
+    head = lax.axis_index("head")
+    other = {"head": 1 - head}
+    rows, wide = att_ref.shape[1:]
+    columns = out_ref.shape[1]
+
+    def across(o):
+        return {"seq": (plane + o) % groups * sub + inner}
+
+    own_columns = pl.ds(pl.multiple_of(head * columns, columns), columns)
+    fetch_own = pltpu.make_async_copy(w_ref.at[:, own_columns], w_own_here, w_sem.at[0])
+    fetch_far = pltpu.make_async_copy(w_far_ref, w_far_here, w_sem.at[1])
+    fetch_own.start()
+    fetch_far.start()
+
+    barrier = pltpu.get_barrier_semaphore()
+    for partner in [across(o) for o in range(1, groups)] + [other]:
+        pl.semaphore_signal(barrier, inc=1, device_id=partner, device_id_type=MESH)
+    pl.semaphore_wait(barrier, groups)
+
+    def on(src, o):
+        copy = pltpu.make_async_remote_copy(
+            src_ref=src.at[o],
+            dst_ref=far.at[o],
+            send_sem=far_send.at[o],
+            recv_sem=far_recv.at[o],
+            device_id=other,
+            device_id_type=MESH,
+        )
+        copy.start()
+        return copy
+
+    going = {}
+    for o in range(1, groups):
+        going[o] = pltpu.make_async_remote_copy(
+            src_ref=att_ref.at[o],
+            dst_ref=home.at[o],
+            send_sem=home_send.at[o],
+            recv_sem=home_recv.at[o],
+            device_id=across(groups - o),
+            device_id_type=MESH,
+        )
+        going[o].start()
+    crossing = {0: on(att_ref, 0)}
+
+    tile = math.gcd(columns, 3 * HEAD_DIM)
+
+    def multiply(src, o, weight, first):
+        block = pl.ds(pl.multiple_of((plane + o) % groups * wide, wide), wide)
+
+        def some_columns(i, carry):
+            here = pl.ds(pl.multiple_of(i * tile, tile), tile)
+            term = jnp.dot(src[o], weight[block, here], preferred_element_type=jnp.float32)
+            total[:, here] = term if first else total[:, here] + term
+            return carry
+
+        lax.fori_loop(0, columns // tile, some_columns, 0)
+
+    fetch_own.wait()
+    multiply(att_ref, 0, w_own_here, True)
+    for o in range(1, groups):
+        going[o].wait_recv()
+        crossing[o] = on(home, o)
+        multiply(home, o, w_own_here, False)
+    fetch_far.wait()
+    for o in range(groups):
+        crossing[o].wait_recv()
+        multiply(far, o, w_far_here, False)
+    out_ref[...] = total[...].astype(jnp.bfloat16)
+    for o in range(1, groups):
+        going[o].wait_send()
+    for o in range(groups):
+        crossing[o].wait_send()
+
+
+def deliver(attended, out_weight, w_far):
+    groups, rows, wide = attended.shape
+    depth, columns = w_far.shape
+    anywhere = pl.BlockSpec(memory_space=pl.ANY)
+    here = pl.BlockSpec(memory_space=pltpu.VMEM)
+    kind = jnp.bfloat16
     return pl.pallas_call(
-        functools.partial(project_body, first),
-        out_shape=jax.ShapeDtypeStruct((rows, columns), jnp.float32 if first else jnp.bfloat16),
-        grid_spec=pltpu.PrefetchScalarGridSpec(
-            num_scalar_prefetch=1,
-            grid=(groups,),
-            in_specs=[
-                pl.BlockSpec((1, rows, wide), lambda s, at: (s, 0, 0)),
-                pl.BlockSpec((wide, columns), lambda s, at: (at[2 + s], at[column_entry] if first else 0)),
-            ]
-            + ([] if first else [whole]),
-            out_specs=whole,
-            scratch_shapes=[pltpu.VMEM((rows, columns), jnp.float32)],
+        functools.partial(deliver_body, groups),
+        out_shape=jax.ShapeDtypeStruct((rows, columns), kind),
+        in_specs=[here, anywhere, anywhere],
+        out_specs=here,
+        scratch_shapes=[
+            pltpu.VMEM((groups, rows, wide), kind),
+            pltpu.VMEM((groups, rows, wide), kind),
+            pltpu.VMEM((depth, columns), kind),
+            pltpu.VMEM((depth, columns), kind),
+            pltpu.VMEM((rows, columns), jnp.float32),
+            pltpu.SemaphoreType.DMA((2,)),
+            pltpu.SemaphoreType.DMA((groups,)),
+            pltpu.SemaphoreType.DMA((groups,)),
+            pltpu.SemaphoreType.DMA((groups,)),
+            pltpu.SemaphoreType.DMA((groups,)),
+        ],
+        compiler_params=pltpu.CompilerParams(
+            collective_id=1, has_side_effects=True, vmem_limit_bytes=40 * 1024 * 1024
         ),
-        compiler_params=pltpu.CompilerParams(vmem_limit_bytes=40 * 1024 * 1024),
-        cost_estimate=pl.CostEstimate(
-            flops=2 * groups * rows * wide * columns,
-            bytes_accessed=2 * groups * wide * columns + 6 * rows * columns,
-            transcendentals=0,
-        ),
-    )(at, terms, weight, *([] if first else [base]))
+    )(attended, out_weight, w_far)
 
 
 def by_heads(groups, queries, keys, values, kv_tiles, tile_order, out_weight):
@@ -337,12 +403,10 @@
     while bit:
         bits.append(bit)
         bit //= 2
-    head = lax.axis_index("head")
-    at = jnp.stack([plane, inner] + [(plane + o) % groups for o in range(groups)] + [head])
-    at = at.astype(jnp.int32)
-
-    def slot_of_row(first, row, at):
-        return lax.rem(at[0] - first - row + groups, groups) * sub + at[1]
+    at = jnp.stack([plane, inner]).astype(jnp.int32)
+
+    def slot_of_row(row, at):
+        return lax.rem(at[0] - row + groups, groups) * sub + at[1]
 
     def place_of_slot(slot, at):
         from_plane = lax.div(slot, sub)
@@ -355,41 +419,8 @@
     columns = out_weight.shape[1] // lax.axis_size("head")
     q, k, v, w_far = exchange(groups, bits, queries, keys, values, out_weight, columns)
 
-    def plane_shift(x, by):
-        return lax.ppermute(
-            x, "seq", [(i, (i // sub + by) % groups * sub + i % sub) for i in range(n)]
-        )
-
-    pieces, far = [None] * groups, [None] * groups
-
-    def attend(first, tiles, q):
-        rows_of = functools.partial(slot_of_row, first)
-        found = attention(q, k, v, at, kv_tiles, tile_order, rows_of, place_of_slot, first, tiles)
-        for i in range(tiles):
-            o = first + i
-            pieces[o] = plane_shift(found[i], -o) if o else found[i]
-
-    def to_far(which):
-        for o in which:
-            far[o] = lax.ppermute(pieces[o], "head", [(0, 1), (1, 0)])
-
-    early = list(range(1, groups - 1))
-    if early:
-        attend(1, len(early), q)
-        attend(groups - 1, 1, q)
-        held, q = lax.optimization_barrier(([pieces[o] for o in early], q))
-        for o, piece in zip(early, held):
-            pieces[o] = piece
-        to_far(early)
-    else:
-        attend(groups - 1, 1, q)
-    attend(0, 1, q)
-    held, pieces[0] = lax.optimization_barrier(([far[o] for o in early], pieces[0]))
-    for o, piece in zip(early, held):
-        far[o] = piece
-    to_far([0, groups - 1])
-    half_way = project(at, jnp.stack(pieces), out_weight, 2 + groups, None)
-    return project(at, jnp.stack(far), w_far, None, half_way)
+    attended = attention(q, k, v, at, kv_tiles, tile_order, slot_of_row, place_of_slot, groups)
+    return deliver(attended, out_weight, w_far)
 
 
 def per_device(queries, keys, values, kv_tiles, tile_order, out_weight):

time: 178 us -> 181 us (1.017)
  the two profiles are of different devices: /device:TPU:4 before, /device:TPU:0 now
where the time goes in v4:
time: 181 us; the launch traced here: 179 us
  Pallas kernels  178 us (98%)
    pallas_call x1, Pallas kernels, exchange(): pl.pallas_call(functools.partial(exchange_body, groups, share, bits), out...  90.2 us
    pallas_call x1, Pallas kernels, deliver(): pl.pallas_call(functools.partial(deliver_body, groups), out_shape=jax.Sha...  51.9 us
    pallas_call x1, Pallas kernels, attention(): pl.pallas_call(functools.partial(attention_body, slot_of_row, place_of_sl...  35.8 us

profile of v4, /device:TPU:0, one launch (start us, length us, event | category | flops | bytes accessed | tf_op | source)
XLA Modules:
  0.0 178.9 jit_solution(301149720064419446)
XLA Ops:
  0.0 0.1 pad_add_fusion.at_ref
  0.1 0.0 copy-start.1
  0.1 0.0 copy-start.2
  0.1 90.2 %shard_map.64 = (bf16[3,4,384,128]{3,2,1,0:T(8,128)(2,1)}, bf16[3,16,384,128]{3,2,1,0:T(8,128)(2,1)}, bf16[3,16,384,128]{3,2,1,0:T(8,128)(2,1)}, bf16[1536,1536]{1,0:T(8,128)(2,1)}) custom-call(bf16[384,1536]{1,0:T(8,128)(2,1)} %q_ref.1, bf16[384,1536]{1,0:T(8,128)(2,1)} %k_ref.1, bf16[384,1536]{1,0:T(8,128)(2,1)} %v_ref.1, bf16[1536,3072]{1,0:T(8,128)(2,1)} %w_ref.3), custom_call_target="tpu_custom_call" | custom-call | tf_op jit(solution)/shard_map/pallas_call | solution.py:263
  90.2 0.0 copy-done.1
  90.2 0.0 copy-done.2
  90.3 0.0 copy-start
  90.3 35.8 %shard_map.65.att_ref = bf16[4,384,384]{2,1,0:T(8,128)(2,1)S(1)} custom-call(s32[2]{0:T(128)S(1)} %pad_add_fusion.at_ref, s32[16,13]{1,0:T(8,128)S(1)} %copy-done.1, s32[16]{0:T(128)S(1)} %copy-done.2, bf16[3,4,384,128]{3,2,1,0:T(8,128)(2,1)} %get-tuple-element.9.q_ref, bf16[3,16,384,128]{3,2,1,0:T(8,128)(2,1)} %get-tuple-element.10.k_ref, ...), custom_call_target="tpu_custom_call" | custom-call | flops 11777605632 | bytes 11796480 | tf_op jit(solution)/shard_map/pallas_call | solution.py:89
  126.0 0.0 copy-done
  126.0 51.9 %shard_map.66 = bf16[384,1536]{1,0:T(8,128)(2,1)S(1)} custom-call(bf16[4,384,384]{2,1,0:T(8,128)(2,1)S(1)} %shard_map.65.att_ref, bf16[1536,3072]{1,0:T(8,128)(2,1)} %w_ref.3, bf16[1536,1536]{1,0:T(8,128)(2,1)S(1)} %copy-done), custom_call_target="tpu_custom_call" | custom-call | tf_op jit(solution)/shard_map/pallas_call | solution.py:373
  177.9 1.0 copy.8
Async XLA Ops:
  0.1 90.2 %copy-start.1 = (s32[16,13]{1,0:T(8,128)S(1)}, s32[16,13]{1,0:T(8,128)}, u32[]{:S(2)}) copy-start(s32[16,13]{1,0:T(8,128)} %tiles_ref.1) | copy-start | bytes 2500
  0.1 90.2 %copy-start.2 = (s32[16]{0:T(128)S(1)}, s32[16]{0:T(128)}, u32[]{:S(2)}) copy-start(s32[16]{0:T(128)} %order_ref.1) | copy-start | bytes 196
  90.3 35.8 %copy-start = (bf16[1536,1536]{1,0:T(8,128)(2,1)S(1)}, bf16[1536,1536]{1,0:T(8,128)(2,1)}, u32[]{:S(2)}) copy-start(bf16[1536,1536]{1,0:T(8,128)(2,1)} %get-tuple-element.12.w_far_ref) | copy-start | bytes 14155780

commit v5 on v3

--- a/solution.py
+++ b/solution.py
@@ -93,7 +93,7 @@
             num_scalar_prefetch=3,
             grid=(tiles,),
             in_specs=[
-                pl.BlockSpec((heads, 1, rows, HEAD_DIM), lambda t, *_: (0, first + t, 0, 0)),
+                pl.BlockSpec((heads, 1, rows, HEAD_DIM), lambda t, *_: (0, first + 2 * t, 0, 0)),
                 key_spec,
                 key_spec,
             ],
@@ -342,7 +342,7 @@
     at = at.astype(jnp.int32)
 
     def slot_of_row(first, row, at):
-        return lax.rem(at[0] - first - row + groups, groups) * sub + at[1]
+        return lax.rem(at[0] - first - 2 * row + groups, groups) * sub + at[1]
 
     def place_of_slot(slot, at):
         from_plane = lax.div(slot, sub)
@@ -365,29 +365,32 @@
     def attend(first, tiles, q):
         rows_of = functools.partial(slot_of_row, first)
         found = attention(q, k, v, at, kv_tiles, tile_order, rows_of, place_of_slot, first, tiles)
-        for i in range(tiles):
-            o = first + i
-            pieces[o] = plane_shift(found[i], -o) if o else found[i]
+        return [found[i] for i in range(tiles)]
+
+    def send_home(which, found):
+        for o, piece in zip(which, found):
+            pieces[o] = plane_shift(piece, -o)
 
     def to_far(which):
         for o in which:
             far[o] = lax.ppermute(pieces[o], "head", [(0, 1), (1, 0)])
 
-    early = list(range(1, groups - 1))
-    if early:
-        attend(1, len(early), q)
-        attend(groups - 1, 1, q)
-        held, q = lax.optimization_barrier(([pieces[o] for o in early], q))
+    early, middle = list(range(1, groups, 2)), list(range(2, groups, 2))
+    send_home(early, attend(1, len(early), q))
+    if middle:
+        found = attend(2, len(middle), q)
+        held, found, q = lax.optimization_barrier(([pieces[o] for o in early], found, q))
         for o, piece in zip(early, held):
             pieces[o] = piece
-        to_far(early)
-    else:
-        attend(groups - 1, 1, q)
-    attend(0, 1, q)
+        send_home(middle, found)
+    to_far(early)
+    pieces[0] = attend(0, 1, q)[0]
     held, pieces[0] = lax.optimization_barrier(([far[o] for o in early], pieces[0]))
     for o, piece in zip(early, held):
         far[o] = piece
-    to_far([0, groups - 1])
+    for o in middle:
+        pieces[o], pieces[0] = lax.optimization_barrier((pieces[o], pieces[0]))
+    to_far([0, *middle])
     half_way = project(at, jnp.stack(pieces), out_weight, 2 + groups, None)
     return project(at, jnp.stack(far), w_far, None, half_way)
 

time: 178 us -> 172 us (0.966)
  the two profiles are of different devices: /device:TPU:4 before, /device:TPU:0 now
where the time goes in v5:
time: 172 us; the launch traced here: 170 us
  Pallas kernels  146 us (85%)
  starting transfers between devices  14.9 us (9%)
  waiting for transfers between devices  6.13 us (4%)
    pallas_call x1, Pallas kernels, exchange(): pl.pallas_call(functools.partial(exchange_body, groups, share, bits), out...  90.1 us
    pallas_call x3, Pallas kernels, attention(): pl.pallas_call(functools.partial(attention_body, slot_of_row, place_of_sl...  46.4 us
    ppermute x3, starting transfers between devices, plane_shift(): lax.ppermute(x, 'seq', [(i, (i // sub + by) % groups * sub + i % sub) for...  9.56 us
    pallas_call x2, Pallas kernels, project(): pl.pallas_call(functools.partial(project_body, first), out_shape=jax.Shap...  9.5 us
    ppermute x4, waiting for transfers between devices, to_far(): far[o] = lax.ppermute(pieces[o], 'head', [(0, 1), (1, 0)])  6.13 us
    ppermute x4, starting transfers between devices, to_far(): far[o] = lax.ppermute(pieces[o], 'head', [(0, 1), (1, 0)])  5.3 us
  transfers between devices with their start and end apart: 7, of which 2 were waited for; matrix products, arithmetic and copies ran while one was open for 1% of the time, Pallas kernels for 18%

profile of v5, /device:TPU:0, one launch (start us, length us, event | category | flops | bytes accessed | tf_op | source)
XLA Modules:
  0.0 170.1 jit_solution(7520165379375491379)
XLA Ops:
  0.0 0.0 copy-start.1
  0.0 0.0 copy-start.2
  0.0 90.1 %shard_map.64 = (bf16[3,4,384,128]{3,2,1,0:T(8,128)(2,1)}, bf16[3,16,384,128]{3,2,1,0:T(8,128)(2,1)}, bf16[3,16,384,128]{3,2,1,0:T(8,128)(2,1)}, bf16[1536,1536]{1,0:T(8,128)(2,1)}) custom-call(bf16[384,1536]{1,0:T(8,128)(2,1)} %q_ref.1, bf16[384,1536]{1,0:T(8,128)(2,1)} %k_ref.1, bf16[384,1536]{1,0:T(8,128)(2,1)} %v_ref.1, bf16[1536,3072]{1,0:T(8,128)(2,1)} %weight_ref.1), custom_call_target="tpu_custom_call" | custom-call | tf_op jit(solution)/shard_map/pallas_call | solution.py:264
  90.1 0.1 stack.61.at_ref
  90.2 0.0 copy-done.1
  90.2 0.0 copy-done.2
  90.2 0.0 copy-start
  90.2 1.3 copy-done
  91.5 19.9 %shard_map.65 = bf16[2,384,384]{2,1,0:T(8,128)(2,1)S(1)} custom-call(s32[7]{0:T(128)S(1)} %stack.61.at_ref, s32[16,13]{1,0:T(8,128)S(1)} %copy-done.1, s32[16]{0:T(128)S(1)} %copy-done.2, bf16[3,4,384,128]{3,2,1,0:T(8,128)(2,1)S(1)} %copy-done, bf16[3,16,384,128]{3,2,1,0:T(8,128)(2,1)} %get-tuple-element.19.k_ref, ...), custom_call_target="tpu_custom_call" | custom-call | flops 5888802816 | bytes 11796480 | tf_op jit(solution)/shard_map/pallas_call | solution.py:89
  111.4 0.1 slice_bitcast_fusion
  111.5 8.0 %collective-permute-start.1 = (bf16[384,384]{1,0:T(8,128)(2,1)S(1)}, bf16[384,384]{1,0:T(8,128)(2,1)S(1)}, u32[]{:S(2)}, u32[]{:S(2)}) collective-permute-start(bf16[384,384]{1,0:T(8,128)(2,1)S(1)} %get-tuple-element.31), channel_id=1, source_target_pairs={{0,8},{2,10},{4,12},{6,14},{8,16},{10,18},{12,20},{14,22},{16,24},... | collective-permute-start | bytes 884744 | tf_op jit(solution)/shard_map/ppermute | solution.py:359
  119.5 0.0 collective-permute-start
  119.5 0.0 slice-start
  119.5 0.0 slice-start.1
  119.5 13.4 %shard_map.66 = bf16[1,384,384]{2,1,0:T(8,128)(2,1)S(1)} custom-call(s32[7]{0:T(128)S(1)} %stack.61.at_ref, s32[16,13]{1,0:T(8,128)S(1)} %copy-done.1, s32[16]{0:T(128)S(1)} %copy-done.2, bf16[3,4,384,128]{3,2,1,0:T(8,128)(2,1)S(1)} %copy-done, bf16[3,16,384,128]{3,2,1,0:T(8,128)(2,1)} %get-tuple-element.19.k_ref, ...), custom_call_target="tpu_custom_call" | custom-call | flops 2944401408 | bytes 11796480 | tf_op jit(solution)/shard_map/pallas_call | solution.py:89
  132.9 0.0 collective-permute-done.1
  132.9 0.0 collective-permute-done
  133.0 0.0 slice-start.2
  133.0 3.1 %collective-permute-start.3 = (bf16[384,384]{1,0:T(8,128)(2,1)S(1)}, bf16[384,384]{1,0:T(8,128)(2,1)S(1)}, u32[]{:S(2)}, u32[]{:S(2)}) collective-permute-start(bf16[384,384]{1,0:T(8,128)(2,1)S(1)} %collective-permute-done), channel_id=1, source_target_pairs={{0,1},{1,0},{2,3},{3,2},{4,5},{5,4},{6,7},{7,6},{8,9},{9,8},{10,11... | collective-permute-start | bytes 884744 | tf_op jit(solution)/shard_map/ppermute | solution.py:376
  136.1 0.1 collective-permute-start.4
  136.2 1.5 collective-permute-start.2
  137.7 13.1 %shard_map.67 = bf16[1,384,384]{2,1,0:T(8,128)(2,1)S(1)} custom-call(s32[7]{0:T(128)S(1)} %stack.61.at_ref, s32[16,13]{1,0:T(8,128)S(1)} %copy-done.1, s32[16]{0:T(128)S(1)} %copy-done.2, bf16[3,4,384,128]{3,2,1,0:T(8,128)(2,1)S(1)} %copy-done, bf16[3,16,384,128]{3,2,1,0:T(8,128)(2,1)} %get-tuple-element.19.k_ref, ...), custom_call_target="tpu_custom_call" | custom-call | flops 2944401408 | bytes 11796480 | tf_op jit(solution)/shard_map/pallas_call | solution.py:89
  150.8 0.0 collective-permute-done.3
  150.8 0.0 collective-permute-done.4
  150.8 0.0 collective-permute-done.2
  150.8 2.0 %collective-permute-start.5 = (bf16[384,384]{1,0:T(8,128)(2,1)S(1)}, bf16[384,384]{1,0:T(8,128)(2,1)S(1)}, u32[]{:S(2)}, u32[]{:S(2)}) collective-permute-start(bf16[384,384]{1,0:T(8,128)(2,1)S(1)} %bitcast.25), channel_id=1, source_target_pairs={{0,1},{1,0},{2,3},{3,2},{4,5},{5,4},{6,7},{7,6},{8,9},{9,8},{10,11... | collective-permute-start | bytes 884744 | tf_op jit(solution)/shard_map/ppermute | solution.py:376
  152.8 0.1 collective-permute-start.6
  152.9 0.0 slice-start.3
  152.9 1.3 pad_maximum_fusion.1.term_ref
  154.2 0.0 slice-done
  154.2 0.0 slice-done.1
  154.2 0.0 slice-done.2
  154.2 0.0 slice-start.4
  154.2 4.4 %shard_map.68.refs_0_ = f32[384,1536]{1,0:T(8,128)S(1)} custom-call(s32[7]{0:T(128)S(1)} %stack.61.at_ref, bf16[4,384,384]{2,1,0:T(8,128)(2,1)S(1)} %pad_maximum_fusion.1.term_ref, bf16[1536,3072]{1,0:T(8,128)(2,1)S(1)} %bitcast.22), custom_call_target="tpu_custom_call" | custom-call | flops 1811939328 | bytes 8257536 | tf_op jit(solution)/shard_map/pallas_call | solution.py:307
  158.7 2.1 %collective-permute-done.5 = bf16[384,384]{1,0:T(8,128)(2,1)S(1)} collective-permute-done((bf16[384,384]{1,0:T(8,128)(2,1)S(1)}, bf16[384,384]{1,0:T(8,128)(2,1)S(1)}, u32[]{:S(2)}, u32[]{:S(2)}) %collective-permute-start.5) | collective-permute-done | bytes 294944 | tf_op jit(solution)/shard_map/ppermute | solution.py:376
  160.8 4.0 %collective-permute-done.6 = bf16[384,384]{1,0:T(8,128)(2,1)S(1)} collective-permute-done((bf16[384,384]{1,0:T(8,128)(2,1)}, bf16[384,384]{1,0:T(8,128)(2,1)S(1)}, u32[]{:S(2)}, u32[]{:S(2)}) %collective-permute-start.6) | collective-permute-done | bytes 294944 | tf_op jit(solution)/shard_map/ppermute | solution.py:376
  164.8 0.2 pad_maximum_fusion.term_ref
  165.0 0.0 slice-done.3
  165.0 0.0 slice-done.4
  165.0 5.1 %shard_map.69 = bf16[384,1536]{1,0:T(8,128)(2,1)} custom-call(s32[7]{0:T(128)S(1)} %stack.61.at_ref, bf16[4,384,384]{2,1,0:T(8,128)(2,1)S(1)} %pad_maximum_fusion.term_ref, bf16[1536,1536]{1,0:T(8,128)(2,1)S(1)} %bitcast.24, f32[384,1536]{1,0:T(8,128)S(1)} %shard_map.68.refs_0_), custom_call_target="tpu_custom_call" | custom-call | flops 1811939328 | bytes 8257536 | tf_op jit(solution)/shard_map/pallas_call | solution.py:307
  (2 shorter events, 0.0 us)
Async XLA Ops:
  0.0 90.2 %copy-start.1 = (s32[16,13]{1,0:T(8,128)S(1)}, s32[16,13]{1,0:T(8,128)}, u32[]{:S(2)}) copy-start(s32[16,13]{1,0:T(8,128)} %tiles_ref.5) | copy-start | bytes 2500
  0.0 90.2 %copy-start.2 = (s32[16]{0:T(128)S(1)}, s32[16]{0:T(128)}, u32[]{:S(2)}) copy-start(s32[16]{0:T(128)} %order_ref.5) | copy-start | bytes 196
  90.2 1.3 copy-start
  111.5 21.4 %collective-permute-start.1 = (bf16[384,384]{1,0:T(8,128)(2,1)S(1)}, bf16[384,384]{1,0:T(8,128)(2,1)S(1)}, u32[]{:S(2)}, u32[]{:S(2)}) collective-permute-start(bf16[384,384]{1,0:T(8,128)(2,1)S(1)} %get-tuple-element.31), channel_id=1, source_target_pairs={{0,8},{2,10},{4,12},{6,14},{8,16},{10,18},{12,20},{14,22},{16,24},... | collective-permute-start | bytes 884744 | tf_op jit(solution)/shard_map/ppermute | solution.py:359
  119.5 13.4 %collective-permute-start = (bf16[384,384]{1,0:T(8,128)(2,1)S(1)}, bf16[384,384]{1,0:T(8,128)(2,1)S(1)}, u32[]{:S(2)}, u32[]{:S(2)}) collective-permute-start(bf16[384,384]{1,0:T(8,128)(2,1)S(1)} %get-tuple-element.32), channel_id=1, source_target_pairs={{0,24},{2,26},{4,28},{6,30},{8,0},{10,2},{12,4},{14,6},{16,8},{18,... | collective-permute-start | bytes 884744 | tf_op jit(solution)/shard_map/ppermute | solution.py:359
  119.5 34.6 %slice-start = ((s8[9437184]{0:T(1024)(128)(4,1)}), s8[4194304]{0:T(1024)(128)(4,1)S(1)}, s32[]{:S(2)}) async-start(s8[9437184]{0:T(1024)(128)(4,1)} %bitcast.21), calls=%async_computation | async-start | bytes 8388608
  119.5 34.7 %slice-start.1 = ((s8[9437184]{0:T(1024)(128)(4,1)}), s8[4194304]{0:T(1024)(128)(4,1)S(1)}, s32[]{:S(2)}) async-start(s8[9437184]{0:T(1024)(128)(4,1)} %bitcast.21), calls=%async_computation.1 | async-start | bytes 8388608
  133.0 21.3 %slice-start.2 = ((s8[9437184]{0:T(1024)(128)(4,1)}), s8[1048576]{0:T(1024)(128)(4,1)S(1)}, s32[]{:S(2)}) async-start(s8[9437184]{0:T(1024)(128)(4,1)} %bitcast.21), calls=%async_computation.2 | async-start | bytes 2097152
  133.0 17.8 %collective-permute-start.3 = (bf16[384,384]{1,0:T(8,128)(2,1)S(1)}, bf16[384,384]{1,0:T(8,128)(2,1)S(1)}, u32[]{:S(2)}, u32[]{:S(2)}) collective-permute-start(bf16[384,384]{1,0:T(8,128)(2,1)S(1)} %collective-permute-done), channel_id=1, source_target_pairs={{0,1},{1,0},{2,3},{3,2},{4,5},{5,4},{6,7},{7,6},{8,9},{9,8},{10,11... | collective-permute-start | bytes 884744 | tf_op jit(solution)/shard_map/ppermute | solution.py:376
  136.1 14.7 %collective-permute-start.4 = (bf16[384,384]{1,0:T(8,128)(2,1)S(1)}, bf16[384,384]{1,0:T(8,128)(2,1)S(1)}, u32[]{:S(2)}, u32[]{:S(2)}) collective-permute-start(bf16[384,384]{1,0:T(8,128)(2,1)S(1)} %collective-permute-done.1), channel_id=1, source_target_pairs={{0,1},{1,0},{2,3},{3,2},{4,5},{5,4},{6,7},{7,6},{8,9},{9,8},{10,11... | collective-permute-start | bytes 884744 | tf_op jit(solution)/shard_map/ppermute | solution.py:376
  136.2 14.6 %collective-permute-start.2 = (bf16[384,384]{1,0:T(8,128)(2,1)S(1)}, bf16[384,384]{1,0:T(8,128)(2,1)}, u32[]{:S(2)}, u32[]{:S(2)}) collective-permute-start(bf16[384,384]{1,0:T(8,128)(2,1)S(1)} %bitcast.26), channel_id=1, source_target_pairs={{0,16},{2,18},{4,20},{6,22},{8,24},{10,26},{12,28},{14,30},{16,0},... | collective-permute-start | bytes 884744 | tf_op jit(solution)/shard_map/ppermute | solution.py:359
  150.8 10.0 %collective-permute-start.5 = (bf16[384,384]{1,0:T(8,128)(2,1)S(1)}, bf16[384,384]{1,0:T(8,128)(2,1)S(1)}, u32[]{:S(2)}, u32[]{:S(2)}) collective-permute-start(bf16[384,384]{1,0:T(8,128)(2,1)S(1)} %bitcast.25), channel_id=1, source_target_pairs={{0,1},{1,0},{2,3},{3,2},{4,5},{5,4},{6,7},{7,6},{8,9},{9,8},{10,11... | collective-permute-start | bytes 884744 | tf_op jit(solution)/shard_map/ppermute | solution.py:376
  152.8 12.0 %collective-permute-start.6 = (bf16[384,384]{1,0:T(8,128)(2,1)}, bf16[384,384]{1,0:T(8,128)(2,1)S(1)}, u32[]{:S(2)}, u32[]{:S(2)}) collective-permute-start(bf16[384,384]{1,0:T(8,128)(2,1)} %collective-permute-done.2), channel_id=1, source_target_pairs={{0,1},{1,0},{2,3},{3,2},{4,5},{5,4},{6,7},{7,6},{8,9},{9,8},{10,11... | collective-permute-start | bytes 884744 | tf_op jit(solution)/shard_map/ppermute | solution.py:376
  152.9 12.1 %slice-start.3 = ((s8[4718592]{0:T(1024)(128)(4,1)}), s8[4194304]{0:T(1024)(128)(4,1)S(1)}, s32[]{:S(2)}) async-start(s8[4718592]{0:T(1024)(128)(4,1)} %bitcast.23), calls=%async_computation.3 | async-start | bytes 8388608
  154.2 10.8 %slice-start.4 = ((s8[4718592]{0:T(1024)(128)(4,1)}), s8[524288]{0:T(1024)(128)(4,1)S(1)}, s32[]{:S(2)}) async-start(s8[4718592]{0:T(1024)(128)(4,1)} %bitcast.23), calls=%async_computation.4 | async-start | bytes 1048576

commit v6 on v5

--- a/solution.py
+++ b/solution.py
@@ -299,20 +299,20 @@
         out_ref[...] = total[...].astype(out_ref.dtype)
 
 
-def project(at, terms, weight, column_entry, base):
+def project(at, terms, weight, column_entry, base, start=0, step=1, kind=jnp.float32):
     groups, rows, wide = terms.shape
     first = base is None
     columns = weight.shape[1] // (lax.axis_size("head") if first else 1)
     whole = pl.BlockSpec((rows, columns), lambda s, at: (0, 0))
     return pl.pallas_call(
         functools.partial(project_body, first),
-        out_shape=jax.ShapeDtypeStruct((rows, columns), jnp.float32 if first else jnp.bfloat16),
+        out_shape=jax.ShapeDtypeStruct((rows, columns), kind),
         grid_spec=pltpu.PrefetchScalarGridSpec(
             num_scalar_prefetch=1,
             grid=(groups,),
             in_specs=[
                 pl.BlockSpec((1, rows, wide), lambda s, at: (s, 0, 0)),
-                pl.BlockSpec((wide, columns), lambda s, at: (at[2 + s], at[column_entry] if first else 0)),
+                pl.BlockSpec((wide, columns), lambda s, at: (at[2 + start + step * s], at[column_entry] if first else 0)),
             ]
             + ([] if first else [whole]),
             out_specs=whole,
@@ -392,7 +392,9 @@
         pieces[o], pieces[0] = lax.optimization_barrier((pieces[o], pieces[0]))
     to_far([0, *middle])
     half_way = project(at, jnp.stack(pieces), out_weight, 2 + groups, None)
-    return project(at, jnp.stack(far), w_far, None, half_way)
+    nearly = project(at, jnp.stack([far[o] for o in early]), w_far, None, half_way, 1, 2)
+    late = jnp.stack([far[o] for o in [0, *middle]])
+    return project(at, late, w_far, None, nearly, 0, 2, jnp.bfloat16)
 
 
 def per_device(queries, keys, values, kv_tiles, tile_order, out_weight):

time: 172 us -> 171 us (level)
  the two profiles are of different devices: /device:TPU:0 before, /device:TPU:7 now
where the time goes in v6:
time: 171 us
  Pallas kernels  143 us (84%)
  starting transfers between devices  19.2 us (11%)
  waiting for transfers between devices  5.99 us (4%)
    pallas_call x1, Pallas kernels, exchange(): pl.pallas_call(functools.partial(exchange_body, groups, share, bits), out...  89.8 us
    pallas_call x3, Pallas kernels, attention(): pl.pallas_call(functools.partial(attention_body, slot_of_row, place_of_sl...  42.7 us
    ppermute x3, starting transfers between devices, plane_shift(): lax.ppermute(x, 'seq', [(i, (i // sub + by) % groups * sub + i % sub) for...  16.2 us
    pallas_call x3, Pallas kernels, project(): pl.pallas_call(functools.partial(project_body, first), out_shape=jax.Shap...  10.4 us
    ppermute x4, waiting for transfers between devices, to_far(): far[o] = lax.ppermute(pieces[o], 'head', [(0, 1), (1, 0)])  4.12 us
  transfers between devices with their start and end apart: 7, of which 2 were waited for; matrix products, arithmetic and copies ran while one was open for 1% of the time, Pallas kernels for 19%

profile of v6, /device:TPU:7, one launch (start us, length us, event | category | flops | bytes accessed | tf_op | source)
XLA Modules:
  0.0 171.1 jit_solution(14582780129679151551)
XLA Ops:
  0.0 0.0 copy-start.1
  0.0 0.0 copy-start.2
  0.0 89.8 %shard_map.64 = (bf16[3,4,384,128]{3,2,1,0:T(8,128)(2,1)}, bf16[3,16,384,128]{3,2,1,0:T(8,128)(2,1)}, bf16[3,16,384,128]{3,2,1,0:T(8,128)(2,1)}, bf16[1536,1536]{1,0:T(8,128)(2,1)}) custom-call(bf16[384,1536]{1,0:T(8,128)(2,1)} %q_ref.1, bf16[384,1536]{1,0:T(8,128)(2,1)} %k_ref.1, bf16[384,1536]{1,0:T(8,128)(2,1)} %v_ref.1, bf16[1536,3072]{1,0:T(8,128)(2,1)} %weight_ref.1), custom_call_target="tpu_custom_call" | custom-call | tf_op jit(solution)/shard_map/pallas_call | solution.py:264
  89.8 0.1 stack.64.at_ref
  89.9 0.0 copy-done.1
  89.9 0.0 copy-done.2
  89.9 0.0 copy-start
  89.9 1.3 copy-done
  91.1 17.2 %shard_map.65 = bf16[2,384,384]{2,1,0:T(8,128)(2,1)S(1)} custom-call(s32[7]{0:T(128)S(1)} %stack.64.at_ref, s32[16,13]{1,0:T(8,128)S(1)} %copy-done.1, s32[16]{0:T(128)S(1)} %copy-done.2, bf16[3,4,384,128]{3,2,1,0:T(8,128)(2,1)S(1)} %copy-done, bf16[3,16,384,128]{3,2,1,0:T(8,128)(2,1)} %get-tuple-element.19.k_ref, ...), custom_call_target="tpu_custom_call" | custom-call | flops 5888802816 | bytes 11796480 | tf_op jit(solution)/shard_map/pallas_call | solution.py:89
  108.3 0.1 slice_bitcast_fusion
  108.4 10.3 %collective-permute-start.1 = (bf16[384,384]{1,0:T(8,128)(2,1)S(1)}, bf16[384,384]{1,0:T(8,128)(2,1)S(1)}, u32[]{:S(2)}, u32[]{:S(2)}) collective-permute-start(bf16[384,384]{1,0:T(8,128)(2,1)S(1)} %get-tuple-element.31), channel_id=1, source_target_pairs={{0,8},{2,10},{4,12},{6,14},{8,16},{10,18},{12,20},{14,22},{16,24},... | collective-permute-start | bytes 884744 | tf_op jit(solution)/shard_map/ppermute | solution.py:359
  118.7 0.0 collective-permute-start
  118.8 0.0 slice-start
  118.8 0.0 slice-start.1
  118.8 9.7 %shard_map.66 = bf16[1,384,384]{2,1,0:T(8,128)(2,1)S(1)} custom-call(s32[7]{0:T(128)S(1)} %stack.64.at_ref, s32[16,13]{1,0:T(8,128)S(1)} %copy-done.1, s32[16]{0:T(128)S(1)} %copy-done.2, bf16[3,4,384,128]{3,2,1,0:T(8,128)(2,1)S(1)} %copy-done, bf16[3,16,384,128]{3,2,1,0:T(8,128)(2,1)} %get-tuple-element.19.k_ref, ...), custom_call_target="tpu_custom_call" | custom-call | flops 2944401408 | bytes 11796480 | tf_op jit(solution)/shard_map/pallas_call | solution.py:89
  128.5 0.0 collective-permute-done.1
  128.5 1.9 %collective-permute-done = bf16[384,384]{1,0:T(8,128)(2,1)S(1)} collective-permute-done((bf16[384,384]{1,0:T(8,128)(2,1)S(1)}, bf16[384,384]{1,0:T(8,128)(2,1)S(1)}, u32[]{:S(2)}, u32[]{:S(2)}) %collective-permute-start) | collective-permute-done | bytes 294944 | tf_op jit(solution)/shard_map/ppermute | solution.py:359
  130.4 0.0 slice-start.2
  130.4 0.0 collective-permute-start.3
  130.4 1.5 collective-permute-start.4
  131.9 5.8 %collective-permute-start.2 = (bf16[384,384]{1,0:T(8,128)(2,1)S(1)}, bf16[384,384]{1,0:T(8,128)(2,1)S(1)}, u32[]{:S(2)}, u32[]{:S(2)}) collective-permute-start(bf16[384,384]{1,0:T(8,128)(2,1)S(1)} %bitcast.26), channel_id=1, source_target_pairs={{0,16},{2,18},{4,20},{6,22},{8,24},{10,26},{12,28},{14,30},{16,0},... | collective-permute-start | bytes 884744 | tf_op jit(solution)/shard_map/ppermute | solution.py:359
  137.7 15.8 %shard_map.67 = bf16[1,384,384]{2,1,0:T(8,128)(2,1)S(1)} custom-call(s32[7]{0:T(128)S(1)} %stack.64.at_ref, s32[16,13]{1,0:T(8,128)S(1)} %copy-done.1, s32[16]{0:T(128)S(1)} %copy-done.2, bf16[3,4,384,128]{3,2,1,0:T(8,128)(2,1)S(1)} %copy-done, bf16[3,16,384,128]{3,2,1,0:T(8,128)(2,1)} %get-tuple-element.19.k_ref, ...), custom_call_target="tpu_custom_call" | custom-call | flops 2944401408 | bytes 11796480 | tf_op jit(solution)/shard_map/pallas_call | solution.py:89
  153.5 0.0 collective-permute-done.3
  153.5 0.0 collective-permute-done.4
  153.5 0.0 collective-permute-done.2
  153.5 0.1 collective-permute-start.5
  153.7 1.4 collective-permute-start.6
  155.1 0.2 pad_maximum_fusion.term_ref
  155.2 0.0 slice-start.3
  155.2 1.2 pad_maximum_fusion.2.term_ref
  156.4 0.0 slice-done
  156.4 0.0 slice-done.1
  156.5 0.0 slice-done.2
  156.5 0.0 slice-start.4
  156.5 4.4 %shard_map.68.refs_0_ = f32[384,1536]{1,0:T(8,128)S(1)} custom-call(s32[7]{0:T(128)S(1)} %stack.64.at_ref, bf16[4,384,384]{2,1,0:T(8,128)(2,1)S(1)} %pad_maximum_fusion.term_ref, bf16[1536,3072]{1,0:T(8,128)(2,1)S(1)} %bitcast.22), custom_call_target="tpu_custom_call" | custom-call | flops 1811939328 | bytes 8257536 | tf_op jit(solution)/shard_map/pallas_call | solution.py:307
  160.9 0.0 slice-done.3
  160.9 0.0 slice-done.4
  161.0 2.5 %shard_map.69.refs_0_ = f32[384,1536]{1,0:T(8,128)S(1)} custom-call(s32[7]{0:T(128)S(1)} %stack.64.at_ref, bf16[2,384,384]{2,1,0:T(8,128)(2,1)S(1)} %pad_maximum_fusion.2.term_ref, bf16[1536,1536]{1,0:T(8,128)(2,1)S(1)} %bitcast.24, f32[384,1536]{1,0:T(8,128)S(1)} %shard_map.68.refs_0_), custom_call_target="tpu_custom_call" | custom-call | flops 905969664 | bytes 5898240 | tf_op jit(solution)/shard_map/pallas_call | solution.py:307
  163.4 0.0 collective-permute-done.5
  163.5 4.1 %collective-permute-done.6 = bf16[384,384]{1,0:T(8,128)(2,1)S(1)} collective-permute-done((bf16[384,384]{1,0:T(8,128)(2,1)S(1)}, bf16[384,384]{1,0:T(8,128)(2,1)S(1)}, u32[]{:S(2)}, u32[]{:S(2)}) %collective-permute-start.6) | collective-permute-done | bytes 294944 | tf_op jit(solution)/shard_map/ppermute | solution.py:376
  167.6 0.1 pad_maximum_fusion.1.term_ref
  167.6 3.4 %shard_map.70 = bf16[384,1536]{1,0:T(8,128)(2,1)} custom-call(s32[7]{0:T(128)S(1)} %stack.64.at_ref, bf16[2,384,384]{2,1,0:T(8,128)(2,1)S(1)} %pad_maximum_fusion.1.term_ref, bf16[1536,1536]{1,0:T(8,128)(2,1)S(1)} %bitcast.24, f32[384,1536]{1,0:T(8,128)S(1)} %shard_map.69.refs_0_), custom_call_target="tpu_custom_call" | custom-call | flops 905969664 | bytes 5898240 | tf_op jit(solution)/shard_map/pallas_call | solution.py:307
  (2 shorter events, 0.0 us)
Async XLA Ops:
  0.0 89.9 %copy-start.1 = (s32[16,13]{1,0:T(8,128)S(1)}, s32[16,13]{1,0:T(8,128)}, u32[]{:S(2)}) copy-start(s32[16,13]{1,0:T(8,128)} %tiles_ref.5) | copy-start | bytes 2500
  0.0 89.9 %copy-start.2 = (s32[16]{0:T(128)S(1)}, s32[16]{0:T(128)}, u32[]{:S(2)}) copy-start(s32[16]{0:T(128)} %order_ref.5) | copy-start | bytes 196
  89.9 1.3 copy-start
  108.4 20.1 %collective-permute-start.1 = (bf16[384,384]{1,0:T(8,128)(2,1)S(1)}, bf16[384,384]{1,0:T(8,128)(2,1)S(1)}, u32[]{:S(2)}, u32[]{:S(2)}) collective-permute-start(bf16[384,384]{1,0:T(8,128)(2,1)S(1)} %get-tuple-element.31), channel_id=1, source_target_pairs={{0,8},{2,10},{4,12},{6,14},{8,16},{10,18},{12,20},{14,22},{16,24},... | collective-permute-start | bytes 884744 | tf_op jit(solution)/shard_map/ppermute | solution.py:359
  118.7 11.6 %collective-permute-start = (bf16[384,384]{1,0:T(8,128)(2,1)S(1)}, bf16[384,384]{1,0:T(8,128)(2,1)S(1)}, u32[]{:S(2)}, u32[]{:S(2)}) collective-permute-start(bf16[384,384]{1,0:T(8,128)(2,1)S(1)} %get-tuple-element.32), channel_id=1, source_target_pairs={{0,24},{2,26},{4,28},{6,30},{8,0},{10,2},{12,4},{14,6},{16,8},{18,... | collective-permute-start | bytes 884744 | tf_op jit(solution)/shard_map/ppermute | solution.py:359
  118.8 37.7 %slice-start = ((s8[9437184]{0:T(1024)(128)(4,1)}), s8[4194304]{0:T(1024)(128)(4,1)S(1)}, s32[]{:S(2)}) async-start(s8[9437184]{0:T(1024)(128)(4,1)} %bitcast.21), calls=%async_computation | async-start | bytes 8388608
  118.8 37.7 %slice-start.1 = ((s8[9437184]{0:T(1024)(128)(4,1)}), s8[4194304]{0:T(1024)(128)(4,1)S(1)}, s32[]{:S(2)}) async-start(s8[9437184]{0:T(1024)(128)(4,1)} %bitcast.21), calls=%async_computation.1 | async-start | bytes 8388608
  130.4 26.1 %slice-start.2 = ((s8[9437184]{0:T(1024)(128)(4,1)}), s8[1048576]{0:T(1024)(128)(4,1)S(1)}, s32[]{:S(2)}) async-start(s8[9437184]{0:T(1024)(128)(4,1)} %bitcast.21), calls=%async_computation.2 | async-start | bytes 2097152
  130.4 23.1 %collective-permute-start.3 = (bf16[384,384]{1,0:T(8,128)(2,1)S(1)}, bf16[384,384]{1,0:T(8,128)(2,1)S(1)}, u32[]{:S(2)}, u32[]{:S(2)}) collective-permute-start(bf16[384,384]{1,0:T(8,128)(2,1)S(1)} %collective-permute-done), channel_id=1, source_target_pairs={{0,1},{1,0},{2,3},{3,2},{4,5},{5,4},{6,7},{7,6},{8,9},{9,8},{10,11... | collective-permute-start | bytes 884744 | tf_op jit(solution)/shard_map/ppermute | solution.py:376
  130.4 23.1 %collective-permute-start.4 = (bf16[384,384]{1,0:T(8,128)(2,1)S(1)}, bf16[384,384]{1,0:T(8,128)(2,1)}, u32[]{:S(2)}, u32[]{:S(2)}) collective-permute-start(bf16[384,384]{1,0:T(8,128)(2,1)S(1)} %collective-permute-done.1), channel_id=1, source_target_pairs={{0,1},{1,0},{2,3},{3,2},{4,5},{5,4},{6,7},{7,6},{8,9},{9,8},{10,11... | collective-permute-start | bytes 884744 | tf_op jit(solution)/shard_map/ppermute | solution.py:376
  131.9 21.7 %collective-permute-start.2 = (bf16[384,384]{1,0:T(8,128)(2,1)S(1)}, bf16[384,384]{1,0:T(8,128)(2,1)S(1)}, u32[]{:S(2)}, u32[]{:S(2)}) collective-permute-start(bf16[384,384]{1,0:T(8,128)(2,1)S(1)} %bitcast.26), channel_id=1, source_target_pairs={{0,16},{2,18},{4,20},{6,22},{8,24},{10,26},{12,28},{14,30},{16,0},... | collective-permute-start | bytes 884744 | tf_op jit(solution)/shard_map/ppermute | solution.py:359
  153.5 9.9 %collective-permute-start.5 = (bf16[384,384]{1,0:T(8,128)(2,1)S(1)}, bf16[384,384]{1,0:T(8,128)(2,1)S(1)}, u32[]{:S(2)}, u32[]{:S(2)}) collective-permute-start(bf16[384,384]{1,0:T(8,128)(2,1)S(1)} %bitcast.25), channel_id=1, source_target_pairs={{0,1},{1,0},{2,3},{3,2},{4,5},{5,4},{6,7},{7,6},{8,9},{9,8},{10,11... | collective-permute-start | bytes 884744 | tf_op jit(solution)/shard_map/ppermute | solution.py:376
  153.7 13.9 %collective-permute-start.6 = (bf16[384,384]{1,0:T(8,128)(2,1)S(1)}, bf16[384,384]{1,0:T(8,128)(2,1)S(1)}, u32[]{:S(2)}, u32[]{:S(2)}) collective-permute-start(bf16[384,384]{1,0:T(8,128)(2,1)S(1)} %collective-permute-done.2), channel_id=1, source_target_pairs={{0,1},{1,0},{2,3},{3,2},{4,5},{5,4},{6,7},{7,6},{8,9},{9,8},{10,11... | collective-permute-start | bytes 884744 | tf_op jit(solution)/shard_map/ppermute | solution.py:376
  155.2 5.7 %slice-start.3 = ((s8[4718592]{0:T(1024)(128)(4,1)}), s8[4194304]{0:T(1024)(128)(4,1)S(1)}, s32[]{:S(2)}) async-start(s8[4718592]{0:T(1024)(128)(4,1)} %bitcast.23), calls=%async_computation.3 | async-start | bytes 8388608
  156.5 4.5 %slice-start.4 = ((s8[4718592]{0:T(1024)(128)(4,1)}), s8[524288]{0:T(1024)(128)(4,1)S(1)}, s32[]{:S(2)}) async-start(s8[4718592]{0:T(1024)(128)(4,1)} %bitcast.23), calls=%async_computation.4 | async-start | bytes 1048576
